TPU v7x, 32 devices: a whole 2x2x4 slice. The times are simulated.
32 devices in a mesh: ctx: 8 (over z, y), ch: 4 (over x, core).
Axes of the slice: x: 2, y: 2, z: 4, core: 2. Of those that a mesh axis runs over, the one named last changes fastest.
Arguments:
- outer_gate: bfloat16 [2048, 4096], P('ctx', 'ch'), may hold values from -6 to 6
- inner_gate: bfloat16 [2048, 4096], P('ctx', 'ch'), may hold values from -6 to 6
- values_in: bfloat16 [2048, 4096], P('ctx', 'ch'), may hold values from -6 to 6
- filters: float32 [2048, 4096], P('ctx', 'ch'), as said below
- skip_gain: float32 [4096], P('ch'), may hold values from 0.5 to 1.5
- w_out: bfloat16 [4096, 4096], P('ch', 'ctx'), may hold values from -0.125 to 0.125
Outputs:
- mixed: bfloat16 [2048, 4096], P('ctx', 'ch')
Inputs may be any that keep to these rules, and one draw needn't show every extreme that they name: `filters`: finite values.
All inputs are finite; a program needn't handle non-finite values.
Results may differ from a plain program's by a relative error of at most 0.022.
Values may be sent and summed in bfloat16 or wider, within the bound.
No kernel may reach another device: no remote copies, remote signals or barrier semaphores. Data moves between devices by JAX's collectives and lax.ppermute only.
A program may use at most 128 MiB of HBM per device.

v0:
```python
import math

import jax
import jax.numpy as jnp
import numpy as np
from jax import lax
from jax.experimental import pallas as pl
from jax.experimental.pallas import tpu as pltpu
from jax.sharding import PartitionSpec as P

BF16, F32 = jnp.bfloat16, jnp.float32
MIB = 2**20


def tables(block):
    freqs = np.arange(block, dtype=np.float64)[:, None] + 0.5
    window = np.arange(-block, block, dtype=np.float64)[None, :]
    angles = math.pi / block * freqs * window
    forward = np.concatenate([np.cos(angles), -np.sin(angles)], axis=0)
    places = angles[:, block:].T
    inverse = np.concatenate([np.cos(places), -np.sin(places)], axis=1) / block
    return forward.astype(BF16), inverse.astype(BF16)


def pack_kernel(outer_ref, inner_ref, values_ref, filters_ref, out_ref):
    n, _, _, chans = out_ref.shape
    gated = (inner_ref[...].astype(F32) * values_ref[...].astype(F32)).astype(BF16)
    lags = filters_ref[...].astype(BF16)
    outer = outer_ref[...]
    for d in range(n):
        part = slice(d * chans, (d + 1) * chans)
        out_ref[d, 0] = gated[:, part]
        out_ref[d, 1] = lags[:, part]
        out_ref[d, 2] = outer[:, part]


def pack(outer_gate, inner_gate, values_in, filters, n):
    block, wide = outer_gate.shape
    tile = block // 2
    return pl.pallas_call(
        pack_kernel,
        grid=(block // tile,),
        in_specs=[pl.BlockSpec((tile, wide), lambda t: (t, 0))] * 4,
        out_specs=pl.BlockSpec((n, 3, tile, wide // n), lambda t: (0, 0, t, 0)),
        out_shape=jax.ShapeDtypeStruct((n, 3, block, wide // n), BF16),
        compiler_params=pltpu.CompilerParams(vmem_limit_bytes=60 * MIB),
        cost_estimate=pl.CostEstimate(flops=2**18, bytes_accessed=4 * MIB, transcendentals=0),
        name="pack",
    )(outer_gate, inner_gate, values_in, filters)


def conv_kernel(places, in_ref, skip_ref, fwd_ref, inv_ref, mix_ref, xs, gs, ys):
    n, _, block, chans = in_ref.shape
    for k in range(n):
        xs[k] = jnp.dot(fwd_ref[:, block:], in_ref[k, 0], preferred_element_type=F32)
        lag = jnp.dot(fwd_ref[:, block:], in_ref[k, 1], preferred_element_type=F32)
        if k:
            lag += jnp.dot(fwd_ref[:, :block], in_ref[k - 1, 1], preferred_element_type=F32)
        gs[k] = lag

    step = 8

    @pl.loop(0, block // step)
    def _(c):
        re = pl.ds(pl.multiple_of(c * step, step), step)
        im = pl.ds(pl.multiple_of(block + c * step, step), step)
        xr = [xs[k, re, :] for k in range(n)]
        xi = [xs[k, im, :] for k in range(n)]
        gr = [gs[k, re, :] for k in range(n)]
        gi = [gs[k, im, :] for k in range(n)]
        xt = [a + b for a, b in zip(xr, xi)]
        gt = [a + b for a, b in zip(gr, gi)]
        for i in range(n):
            one = xr[0] * gr[i]
            two = xi[0] * gi[i]
            three = xt[0] * gt[i]
            for k in range(1, i + 1):
                one += xr[k] * gr[i - k]
                two += xi[k] * gi[i - k]
                three += xt[k] * gt[i - k]
            ys[i, re, :] = one - two
            ys[i, im, :] = three - (one + two)

    for i in range(n):
        conv = jnp.dot(inv_ref[...], ys[i].astype(BF16), preferred_element_type=F32)
        mix = in_ref[i, 2].astype(F32) * (conv + skip_ref[...] * in_ref[i, 0].astype(F32))
        chunk, place = places[i]
        mix_ref[place, chunk] = mix.astype(BF16)


def convolve(packed, skip, places):
    n, _, block, chans = packed.shape
    forward, inverse = tables(block)
    return pl.pallas_call(
        lambda *refs: conv_kernel(places, *refs),
        out_shape=jax.ShapeDtypeStruct((n // 2, 2, block, chans), BF16),
        scratch_shapes=[pltpu.VMEM((n, 2 * block, chans), F32)] * 3,
        compiler_params=pltpu.CompilerParams(vmem_limit_bytes=16 * MIB),
        cost_estimate=pl.CostEstimate(flops=2**31, bytes_accessed=4 * MIB, transcendentals=0),
        name="convolve",
    )(packed, skip, jnp.asarray(forward), jnp.asarray(inverse))


def project_kernel(shape, m, last, here_ref, table_ref, *refs):
    refs = list(refs)
    total = refs.pop(0)[...] if len(refs) > sum(shape) + m * len(shape) + 1 + last else None
    for parts in shape:
        piece, slabs = refs[:parts], refs[parts : parts + m]
        del refs[: parts + m]
        left, right = [], []
        for b in range(m):
            source = lax.bitwise_xor(here_ref[1], b)
            share = m // parts
            inner = lax.bitwise_and(source, share - 1)
            rows = piece[0][inner]
            if parts == 2:
                rows = jnp.where(source < share, rows, piece[1][inner])
            left.append(rows.reshape(-1, rows.shape[-1]))
            right.append(slabs[b][0])
        term = jnp.dot(
            jnp.concatenate(left, axis=1),
            jnp.concatenate(right, axis=0),
            preferred_element_type=F32,
        )
        total = term if total is None else total + term
    if last:
        total = total.astype(BF16)
        block = total.shape[0] // 2
        chunks = [total[:block], total[block:]]

        @pl.when(lax.rem(here_ref[0], 2) == 0)
        def _():
            refs[0][...], refs[1][...] = chunks

        @pl.when(lax.rem(here_ref[0], 2) == 1)
        def _():
            refs[1][...], refs[0][...] = chunks
    else:
        refs[0][...] = total


def project(pieces, owners, total, here, weights, last=False):
    m = len(weights)
    _, chans, columns = weights[0].shape
    block = pieces[0][0].shape[-2]
    operands, specs = [], []

    def whole(shape):
        return pl.BlockSpec(shape, lambda t, *_: (0,) * len(shape))

    if total is not None:
        operands.append(total)
        specs.append(whole(total.shape))
    for s, piece in enumerate(pieces):
        operands += piece + weights
        specs += [whole(part.shape) for part in piece]

        def rows(t, here, table, s=s):
            return (table[here[0] * len(pieces) + s], 0, 0)

        specs += [pl.BlockSpec((1, chans, columns), rows)] * m
    outs = [((block, columns), BF16)] * 2 if last else [((2 * block, columns), F32)]
    shape = [len(piece) for piece in pieces]
    return pl.pallas_call(
        lambda *refs: project_kernel(shape, m, last, *refs),
        grid_spec=pltpu.PrefetchScalarGridSpec(
            num_scalar_prefetch=2,
            grid=(1,),
            in_specs=specs,
            out_specs=[whole(size) for size, _ in outs],
        ),
        out_shape=[jax.ShapeDtypeStruct(*out) for out in outs],
        compiler_params=pltpu.CompilerParams(vmem_limit_bytes=60 * MIB),
        cost_estimate=pl.CostEstimate(flops=0, bytes_accessed=0, transcendentals=0),
        name="project",
    )(here, jnp.asarray(owners.reshape(-1)), *operands)


def ring_of(deep, across):
    walk = []
    for a in range(across):
        column = list(range(1, deep))
        walk += [d * across + a for d in (column if a % 2 == 0 else column[::-1])]
    return walk + [a for a in reversed(range(across))]


def per_device(outer_gate, inner_gate, values_in, filters, skip_gain, w_out):
    n, m = lax.axis_size("ctx"), lax.axis_size("ch")
    j, k = lax.axis_index("ctx"), lax.axis_index("ch")
    block, wide = outer_gate.shape
    chans = wide // n
    across = n // 4
    half = m // 2
    assert n == 2 * m
    here = jnp.stack([j, k]).astype(jnp.int32)

    def row_block(h, d):
        return (h + 2 * (d % 2)) * across + d // 2

    places = {row_block(h, d): (h, d) for h in range(2) for d in range(m)}

    weights = [w_out.reshape(n, chans, -1)]
    while len(weights) < m:
        pairs = [(d, d ^ len(weights)) for d in range(m)]
        if len(weights) == 1:
            weights.append(lax.ppermute(weights[0], "ch", pairs))
        else:
            for even in list(weights[::2]):
                far = lax.ppermute(even, "ch", pairs)
                weights += [far, lax.ppermute(far, "ch", [(d, d ^ 1) for d in range(m)])]

    packed = pack(outer_gate, inner_gate, values_in, filters, n)
    packed = lax.all_to_all(packed, "ctx", 0, 0)
    skip = lax.dynamic_slice_in_dim(skip_gain, j * chans, chans, 0)[None, :]
    packed, weights = lax.optimization_barrier((packed, weights))
    mix = lax.all_to_all(convolve(packed, skip, places), "ch", 0, 0)

    ring = ring_of(4, across)
    spot = np.argsort(np.array(ring))
    routes = [[(ring[p], ring[(p + way) % n]) for p in range(n)] for way in (1, -1)]

    def owners(offsets):
        return np.array([[ring[(spot[a] + o) % n] for o in offsets] for a in range(n)], np.int32)

    tips = [mix, mix]
    pieces, offsets = [[mix]], [0]
    for s in range(1, n // 2):
        if s == n // 2 - 1:
            total = project(pieces, owners(offsets), None, here, weights)
        tips = [lax.ppermute(tip, "ctx", route) for tip, route in zip(tips, routes)]
        pieces += [[tip] for tip in tips]
        offsets += [-s, s]
    tips, total = lax.optimization_barrier((tips, total))
    halves = [lax.ppermute(tip[way * half : (way + 1) * half], "ctx", routes[way]) for way, tip in enumerate(tips)]
    total = project([[tip] for tip in tips], owners(offsets[-2:]), total[0], here, weights)
    sent = project([halves], owners([n // 2]), total[0], here, weights, last=True)

    found = []
    for e in range(2):
        route = []
        for a in range(n):
            for b in range(m):
                route.append((a * m + b, row_block((a + e) % 2, b) * m + a // 2))
        found.append(lax.ppermute(sent[e], ("ctx", "ch"), route))
    even = (j // across) % 2 == 0
    return jnp.where(even, jnp.concatenate(found, axis=1), jnp.concatenate(found[::-1], axis=1))


def solution(mesh):
    placed = (
        P("ctx", "ch"),
        P("ctx", "ch"),
        P("ctx", "ch"),
        P("ctx", "ch"),
        P("ch"),
        P("ch", "ctx"),
    )
    return jax.shard_map(
        per_device, mesh=mesh, in_specs=placed, out_specs=P("ctx", "ch"), check_vma=False
    )
```

profile of v0, /device:TPU:2, one launch (start us, length us, event | category | flops | bytes accessed | tf_op | source)
XLA Modules:
  0.0 129.8 jit_solution(12926095179279602794)
XLA Ops:
  0.0 2.7 %pack.1 = bf16[8,3,256,128]{3,2,1,0:T(8,128)(2,1)} custom-call(bf16[256,1024]{1,0:T(8,128)(2,1)} %outer_ref.1, bf16[256,1024]{1,0:T(8,128)(2,1)} %inner_ref.1, bf16[256,1024]{1,0:T(8,128)(2,1)} %values_ref.1, f32[256,1024]{1,0:T(8,128)} %filters_ref.1), custom_call_target="tpu_custom_call" | custom-call | flops 262144 | bytes 4194304 | tf_op jit(solution)/shard_map/pack/pallas_call | solution.py:40
  2.8 6.0 %all-to-all-start = ((bf16[8,3,256,128]{3,2,1,0:T(8,128)(2,1)}), bf16[8,3,256,128]{3,2,1,0:T(8,128)(2,1)S(1)}, u32[]{:S(2)}, u32[]{:S(2)}) async-start(bf16[8,3,256,128]{3,2,1,0:T(8,128)(2,1)} %pack.1), calls=%async_computation | async-start | bytes 3145728 | tf_op jit(solution)/shard_map/all_to_all | solution.py:213
  9.4 24.2 %collective-permute-done.1.refs_5_.refs_10_.refs_15_.refs_20_.refs_25_.refs_6_.refs_11_.refs_7_ = bf16[8,128,512]{2,1,0:T(8,128)(2,1)} collective-permute-done((bf16[8,128,512]{2,1,0:T(8,128)(2,1)S(1)}, bf16[8,128,512]{2,1,0:T(8,128)(2,1)}, u32[]{:S(2)}, u32[]{:S(2)}) %collective-permute-start.1) | collective-permute-done | bytes 1048608 | tf_op jit(solution)/shard_map/ppermute | solution.py:209
  33.6 2.9 %collective-permute-done.2.refs_6_.refs_11_.refs_16_.refs_21_.refs_26_.refs_7_.refs_12_.refs_8_ = bf16[8,128,512]{2,1,0:T(8,128)(2,1)} collective-permute-done((bf16[8,128,512]{2,1,0:T(8,128)(2,1)}, bf16[8,128,512]{2,1,0:T(8,128)(2,1)}, u32[]{:S(2)}, u32[]{:S(2)}) %collective-permute-start.2) | collective-permute-done | bytes 1048608 | tf_op jit(solution)/shard_map/ppermute | solution.py:210
  36.5 9.2 %all-to-all-done.refs_0_ = bf16[8,3,256,128]{3,2,1,0:T(8,128)(2,1)S(1)} async-done(((bf16[8,3,256,128]{3,2,1,0:T(8,128)(2,1)}), bf16[8,3,256,128]{3,2,1,0:T(8,128)(2,1)S(1)}, u32[]{:S(2)}, u32[]{:S(2)}) %all-to-all-start) | async-done | bytes 1572896 | tf_op jit(solution)/shard_map/all_to_all | solution.py:213
  45.8 3.9 %convolve.1 = bf16[4,2,256,128]{3,2,1,0:T(8,128)(2,1)S(1)} custom-call(bf16[8,3,256,128]{3,2,1,0:T(8,128)(2,1)S(1)} %all-to-all-done.refs_0_, f32[1,128]{1,0:T(1,128)S(1)} %dynamic-slice_bitcast_fusion.refs_1_, bf16[512,512]{1,0:T(8,128)(2,1)S(1)} %copy-done.1, bf16[256,512]{1,0:T(8,128)(2,1)S(1)} %copy-done.2), custom_call_target="tpu_custom_call" | custom-call | flops 2147483648 | bytes 4194304 | tf_op jit(solution)/shard_map/convolve/pallas_call | solution.py:94
  49.7 10.3 %all_to_all.10.refs_2_ = bf16[4,2,256,128]{3,2,1,0:T(8,128)(2,1)S(1)} all-to-all(bf16[4,2,256,128]{3,2,1,0:T(8,128)(2,1)S(1)} %convolve.1), channel_id=1, replica_groups=mesh['ctx'=8,'ch'=4] {'ch'}, dimensions={0} | all-to-all | bytes 1048576 | tf_op jit(solution)/shard_map/all_to_all | solution.py:216
  59.9 2.0 %collective-permute-start.6 = (bf16[4,2,256,128]{3,2,1,0:T(8,128)(2,1)S(1)}, bf16[4,2,256,128]{3,2,1,0:T(8,128)(2,1)S(1)}, u32[]{:S(2)}, u32[]{:S(2)}) collective-permute-start(bf16[4,2,256,128]{3,2,1,0:T(8,128)(2,1)S(1)} %all_to_all.10.refs_2_), channel_id=1, source_target_pairs={{8,0},{16,8},{24,16},{28,24},{20,28},{12,20},{4,12},{0,4},{9,1},{1... | collective-permute-start | bytes 1572872 | tf_op jit(solution)/shard_map/ppermute | solution.py:230
  62.0 11.7 %collective-permute-done.3.refs_7_ = bf16[4,2,256,128]{3,2,1,0:T(8,128)(2,1)S(1)} collective-permute-done((bf16[4,2,256,128]{3,2,1,0:T(8,128)(2,1)S(1)}, bf16[4,2,256,128]{3,2,1,0:T(8,128)(2,1)S(1)}, u32[]{:S(2)}, u32[]{:S(2)}) %collective-permute-start.3) | collective-permute-done | bytes 524320 | tf_op jit(solution)/shard_map/ppermute | solution.py:230
  74.0 1.7 %collective-permute-start.7 = (bf16[4,2,256,128]{3,2,1,0:T(8,128)(2,1)S(1)}, bf16[4,2,256,128]{3,2,1,0:T(8,128)(2,1)}, u32[]{:S(2)}, u32[]{:S(2)}) collective-permute-start(bf16[4,2,256,128]{3,2,1,0:T(8,128)(2,1)S(1)} %collective-permute-done.6.refs_12_), channel_id=1, source_target_pairs={{8,0},{16,8},{24,16},{28,24},{20,28},{12,20},{4,12},{0,4},{9,1},{1... | collective-permute-start | bytes 1572872 | tf_op jit(solution)/shard_map/ppermute | solution.py:230
  75.7 10.9 %collective-permute-done.4.refs_17_ = bf16[4,2,256,128]{3,2,1,0:T(8,128)(2,1)S(1)} collective-permute-done((bf16[4,2,256,128]{3,2,1,0:T(8,128)(2,1)S(1)}, bf16[4,2,256,128]{3,2,1,0:T(8,128)(2,1)S(1)}, u32[]{:S(2)}, u32[]{:S(2)}) %collective-permute-start.4) | collective-permute-done | bytes 524320 | tf_op jit(solution)/shard_map/ppermute | solution.py:230
  87.2 1.4 %collective-permute-start.8 = (bf16[4,2,256,128]{3,2,1,0:T(8,128)(2,1)}, bf16[4,2,256,128]{3,2,1,0:T(8,128)(2,1)S(1)}, u32[]{:S(2)}, u32[]{:S(2)}) collective-permute-start(bf16[4,2,256,128]{3,2,1,0:T(8,128)(2,1)} %collective-permute-done.7.refs_22_), channel_id=1, source_target_pairs={{8,0},{16,8},{24,16},{28,24},{20,28},{12,20},{4,12},{0,4},{9,1},{1... | collective-permute-start | bytes 1572872 | tf_op jit(solution)/shard_map/ppermute | solution.py:230
  89.3 5.7 %project.3.refs_2_ = f32[512,512]{1,0:T(8,128)} custom-call(s32[2]{0:T(128)} %pad_add_fusion.refs_0_, s32[40]{0:T(128)} %constant.50.clone.refs_1_, bf16[4,2,256,128]{3,2,1,0:T(8,128)(2,1)} %copy-done.4, bf16[8,128,512]{2,1,0:T(8,128)(2,1)} %bitcast.5, ...), custom_call_target="tpu_custom_call" | custom-call | tf_op jit(solution)/shard_map/project/pallas_call | solution.py:164
  95.0 3.7 %collective-permute-done.5.refs_3_ = bf16[4,2,256,128]{3,2,1,0:T(8,128)(2,1)S(1)} collective-permute-done((bf16[4,2,256,128]{3,2,1,0:T(8,128)(2,1)S(1)}, bf16[4,2,256,128]{3,2,1,0:T(8,128)(2,1)S(1)}, u32[]{:S(2)}, u32[]{:S(2)}) %collective-permute-start.5) | collective-permute-done | bytes 524320 | tf_op jit(solution)/shard_map/ppermute | solution.py:230
  98.7 0.9 collective-permute-done.8.refs_8_
  99.6 1.4 %collective-permute-start.10 = (bf16[2,2,256,128]{3,2,1,0:T(8,128)(2,1)S(1)}, bf16[2,2,256,128]{3,2,1,0:T(8,128)(2,1)S(1)}, u32[]{:S(2)}, u32[]{:S(2)}) collective-permute-start(bf16[2,2,256,128]{3,2,1,0:T(8,128)(2,1)S(1)} %slice.7), channel_id=1, source_target_pairs={{8,0},{16,8},{24,16},{28,24},{20,28},{12,20},{4,12},{0,4},{9,1},{1... | collective-permute-start | bytes 786440 | tf_op jit(solution)/shard_map/ppermute | solution.py:234
  100.9 0.8 collective-permute-start.9
  101.7 4.2 %project.4.refs_2_ = f32[512,512]{1,0:T(8,128)} custom-call(s32[2]{0:T(128)} %pad_add_fusion.refs_0_, s32[16]{0:T(128)} %constant.51.clone.refs_1_, f32[512,512]{1,0:T(8,128)} %project.3.refs_2_, bf16[4,2,256,128]{3,2,1,0:T(8,128)(2,1)} %copy-done.5, bf16[8,128,512]{2,1,0:T(8,128)(2,1)} %bitcast.10, ...), custom_call_target="tpu_custom_call" | custom-call | tf_op jit(solution)/shard_map/project/pallas_call | solution.py:164
  106.0 1.4 %collective-permute-done.9.refs_3_ = bf16[2,2,256,128]{3,2,1,0:T(8,128)(2,1)S(1)} collective-permute-done((bf16[2,2,256,128]{3,2,1,0:T(8,128)(2,1)S(1)}, bf16[2,2,256,128]{3,2,1,0:T(8,128)(2,1)S(1)}, u32[]{:S(2)}, u32[]{:S(2)}) %collective-permute-start.9) | collective-permute-done | bytes 262176 | tf_op jit(solution)/shard_map/ppermute | solution.py:234
  108.1 3.5 %project.5 = (bf16[256,512]{1,0:T(8,128)(2,1)}, bf16[256,512]{1,0:T(8,128)(2,1)}) custom-call(s32[2]{0:T(128)} %pad_add_fusion.refs_0_, s32[8]{0:T(128)} %constant.52.clone.refs_1_, f32[512,512]{1,0:T(8,128)} %project.4.refs_2_, bf16[2,2,256,128]{3,2,1,0:T(8,128)(2,1)} %copy-done.11, bf16[2,2,256,128]{3,2,1,0:T(8,128)(2,1)} %copy-done.10, ...), custom_call_target="tpu_custom_call" | custom-call | tf_op jit(solution)/shard_map/project/pallas_call | solution.py:164
  111.5 3.4 %collective-permute-start.11 = (bf16[256,512]{1,0:T(8,128)(2,1)}, bf16[256,512]{1,0:T(8,128)(2,1)S(1)}, u32[]{:S(2)}, u32[]{:S(2)}) collective-permute-start(bf16[256,512]{1,0:T(8,128)(2,1)} %get-tuple-element.23), channel_id=1, source_target_pairs={{0,0},{1,16},{2,4},{3,20},{4,8},{5,24},{6,12},{7,28},{8,1},{9,17},... | collective-permute-start | bytes 786440 | tf_op jit(solution)/shard_map/ppermute | solution.py:244
  115.1 10.7 %collective-permute-done.11 = bf16[256,512]{1,0:T(8,128)(2,1)S(1)} collective-permute-done((bf16[256,512]{1,0:T(8,128)(2,1)}, bf16[256,512]{1,0:T(8,128)(2,1)S(1)}, u32[]{:S(2)}, u32[]{:S(2)}) %collective-permute-start.11) | collective-permute-done | bytes 262176 | tf_op jit(solution)/shard_map/ppermute | solution.py:244
  125.8 3.1 %collective-permute-done.12 = bf16[256,512]{1,0:T(8,128)(2,1)S(1)} collective-permute-done((bf16[256,512]{1,0:T(8,128)(2,1)}, bf16[256,512]{1,0:T(8,128)(2,1)S(1)}, u32[]{:S(2)}, u32[]{:S(2)}) %collective-permute-start.12) | collective-permute-done | bytes 262176 | tf_op jit(solution)/shard_map/ppermute | solution.py:244
  128.9 0.9 maximum_select_fusion
  (39 shorter events, 3.2 us)
Async XLA Ops:
  0.0 33.5 %copy-start = (f32[1024]{0:T(1024)S(1)}, f32[1024]{0:T(1024)}, u32[]{:S(2)}) copy-start(f32[1024]{0:T(1024)} %param.15) | copy-start | bytes 12292
  2.8 6.0 %copy-start.3 = (bf16[1024,512]{1,0:T(8,128)(2,1)S(1)}, bf16[1024,512]{1,0:T(8,128)(2,1)}, u32[]{:S(2)}) copy-start(bf16[1024,512]{1,0:T(8,128)(2,1)} %param.16) | copy-start | bytes 3145732
  2.8 43.0 %copy-start.1 = (bf16[512,512]{1,0:T(8,128)(2,1)S(1)}, bf16[512,512]{1,0:T(8,128)(2,1)}, u32[]{:S(2)}) copy-start(bf16[512,512]{1,0:T(8,128)(2,1)} %constant.48.clone.refs_2_) | copy-start | bytes 1572868
  2.8 43.0 %copy-start.2 = (bf16[256,512]{1,0:T(8,128)(2,1)S(1)}, bf16[256,512]{1,0:T(8,128)(2,1)}, u32[]{:S(2)}) copy-start(bf16[256,512]{1,0:T(8,128)(2,1)} %constant.49.clone.refs_3_) | copy-start | bytes 786436
  2.8 43.0 %all-to-all-start = ((bf16[8,3,256,128]{3,2,1,0:T(8,128)(2,1)}), bf16[8,3,256,128]{3,2,1,0:T(8,128)(2,1)S(1)}, u32[]{:S(2)}, u32[]{:S(2)}) async-start(bf16[8,3,256,128]{3,2,1,0:T(8,128)(2,1)} %pack.1), calls=%async_computation | async-start | bytes 3145728 | tf_op jit(solution)/shard_map/all_to_all | solution.py:213
  8.7 24.8 %collective-permute-start.1 = (bf16[8,128,512]{2,1,0:T(8,128)(2,1)S(1)}, bf16[8,128,512]{2,1,0:T(8,128)(2,1)}, u32[]{:S(2)}, u32[]{:S(2)}) collective-permute-start(bf16[8,128,512]{2,1,0:T(8,128)(2,1)S(1)} %bitcast.13), channel_id=1, source_target_pairs={{0,2},{1,3},{2,0},{3,1},{4,6},{5,7},{6,4},{7,5},{8,10},{9,11},{10,... | collective-permute-start | bytes 3145736 | tf_op jit(solution)/shard_map/ppermute | solution.py:209
  9.3 24.3 %collective-permute-start = (bf16[8,128,512]{2,1,0:T(8,128)(2,1)S(1)}, bf16[8,128,512]{2,1,0:T(8,128)(2,1)}, u32[]{:S(2)}, u32[]{:S(2)}) collective-permute-start(bf16[8,128,512]{2,1,0:T(8,128)(2,1)S(1)} %bitcast.14), channel_id=1, source_target_pairs={{0,1},{1,0},{2,3},{3,2},{4,5},{5,4},{6,7},{7,6},{8,9},{9,8},{10,11... | collective-permute-start | bytes 3145736 | tf_op jit(solution)/shard_map/ppermute | solution.py:206
  33.5 3.0 %collective-permute-start.2 = (bf16[8,128,512]{2,1,0:T(8,128)(2,1)}, bf16[8,128,512]{2,1,0:T(8,128)(2,1)}, u32[]{:S(2)}, u32[]{:S(2)}) collective-permute-start(bf16[8,128,512]{2,1,0:T(8,128)(2,1)} %collective-permute-done.1.refs_5_.refs_10_.refs_15_.refs_20_.refs_25_.refs_6_.refs_11_.refs_7_), channel_id=1, source_target_pairs={{0,1},{1,0},{2,3},{3,2},{4,5},{5,4},{6,7},{7,6},{8,9},{9,8},{10,11... | collective-permute-start | bytes 3145736 | tf_op jit(solution)/shard_map/ppermute | solution.py:210
  59.9 29.3 %copy-start.4 = (bf16[4,2,256,128]{3,2,1,0:T(8,128)(2,1)}, bf16[4,2,256,128]{3,2,1,0:T(8,128)(2,1)S(1)}, u32[]{:S(2)}) copy-start(bf16[4,2,256,128]{3,2,1,0:T(8,128)(2,1)S(1)} %all_to_all.10.refs_2_) | copy-start | bytes 1572868
  59.9 13.8 %collective-permute-start.3 = (bf16[4,2,256,128]{3,2,1,0:T(8,128)(2,1)S(1)}, bf16[4,2,256,128]{3,2,1,0:T(8,128)(2,1)S(1)}, u32[]{:S(2)}, u32[]{:S(2)}) collective-permute-start(bf16[4,2,256,128]{3,2,1,0:T(8,128)(2,1)S(1)} %all_to_all.10.refs_2_), channel_id=1, source_target_pairs={{8,16},{16,24},{24,28},{28,20},{20,12},{12,4},{4,0},{0,8},{9,17},{... | collective-permute-start | bytes 1572872 | tf_op jit(solution)/shard_map/ppermute | solution.py:230
  59.9 14.0 %collective-permute-start.6 = (bf16[4,2,256,128]{3,2,1,0:T(8,128)(2,1)S(1)}, bf16[4,2,256,128]{3,2,1,0:T(8,128)(2,1)S(1)}, u32[]{:S(2)}, u32[]{:S(2)}) collective-permute-start(bf16[4,2,256,128]{3,2,1,0:T(8,128)(2,1)S(1)} %all_to_all.10.refs_2_), channel_id=1, source_target_pairs={{8,0},{16,8},{24,16},{28,24},{20,28},{12,20},{4,12},{0,4},{9,1},{1... | collective-permute-start | bytes 1572872 | tf_op jit(solution)/shard_map/ppermute | solution.py:230
  73.7 15.6 %copy-start.7 = (bf16[4,2,256,128]{3,2,1,0:T(8,128)(2,1)}, bf16[4,2,256,128]{3,2,1,0:T(8,128)(2,1)S(1)}, u32[]{:S(2)}) copy-start(bf16[4,2,256,128]{3,2,1,0:T(8,128)(2,1)S(1)} %collective-permute-done.3.refs_7_) | copy-start | bytes 1572868
  73.7 12.9 %collective-permute-start.4 = (bf16[4,2,256,128]{3,2,1,0:T(8,128)(2,1)S(1)}, bf16[4,2,256,128]{3,2,1,0:T(8,128)(2,1)S(1)}, u32[]{:S(2)}, u32[]{:S(2)}) collective-permute-start(bf16[4,2,256,128]{3,2,1,0:T(8,128)(2,1)S(1)} %collective-permute-done.3.refs_7_), channel_id=1, source_target_pairs={{8,16},{16,24},{24,28},{28,20},{20,12},{12,4},{4,0},{0,8},{9,17},{... | collective-permute-start | bytes 1572872 | tf_op jit(solution)/shard_map/ppermute | solution.py:230
  74.0 15.3 %copy-start.8 = (bf16[4,2,256,128]{3,2,1,0:T(8,128)(2,1)}, bf16[4,2,256,128]{3,2,1,0:T(8,128)(2,1)S(1)}, u32[]{:S(2)}) copy-start(bf16[4,2,256,128]{3,2,1,0:T(8,128)(2,1)S(1)} %collective-permute-done.6.refs_12_) | copy-start | bytes 1572868
  74.0 13.2 %collective-permute-start.7 = (bf16[4,2,256,128]{3,2,1,0:T(8,128)(2,1)S(1)}, bf16[4,2,256,128]{3,2,1,0:T(8,128)(2,1)}, u32[]{:S(2)}, u32[]{:S(2)}) collective-permute-start(bf16[4,2,256,128]{3,2,1,0:T(8,128)(2,1)S(1)} %collective-permute-done.6.refs_12_), channel_id=1, source_target_pairs={{8,0},{16,8},{24,16},{28,24},{20,28},{12,20},{4,12},{0,4},{9,1},{1... | collective-permute-start | bytes 1572872 | tf_op jit(solution)/shard_map/ppermute | solution.py:230
  86.6 2.7 %copy-start.9 = (bf16[4,2,256,128]{3,2,1,0:T(8,128)(2,1)}, bf16[4,2,256,128]{3,2,1,0:T(8,128)(2,1)S(1)}, u32[]{:S(2)}) copy-start(bf16[4,2,256,128]{3,2,1,0:T(8,128)(2,1)S(1)} %collective-permute-done.4.refs_17_) | copy-start | bytes 1572868
  86.6 12.1 %collective-permute-start.5 = (bf16[4,2,256,128]{3,2,1,0:T(8,128)(2,1)S(1)}, bf16[4,2,256,128]{3,2,1,0:T(8,128)(2,1)S(1)}, u32[]{:S(2)}, u32[]{:S(2)}) collective-permute-start(bf16[4,2,256,128]{3,2,1,0:T(8,128)(2,1)S(1)} %collective-permute-done.4.refs_17_), channel_id=1, source_target_pairs={{8,16},{16,24},{24,28},{28,20},{20,12},{12,4},{4,0},{0,8},{9,17},{... | collective-permute-start | bytes 1572872 | tf_op jit(solution)/shard_map/ppermute | solution.py:230
  87.2 12.3 %collective-permute-start.8 = (bf16[4,2,256,128]{3,2,1,0:T(8,128)(2,1)}, bf16[4,2,256,128]{3,2,1,0:T(8,128)(2,1)S(1)}, u32[]{:S(2)}, u32[]{:S(2)}) collective-permute-start(bf16[4,2,256,128]{3,2,1,0:T(8,128)(2,1)} %collective-permute-done.7.refs_22_), channel_id=1, source_target_pairs={{8,0},{16,8},{24,16},{28,24},{20,28},{12,20},{4,12},{0,4},{9,1},{1... | collective-permute-start | bytes 1572872 | tf_op jit(solution)/shard_map/ppermute | solution.py:230
  98.7 3.0 %copy-start.5 = (bf16[4,2,256,128]{3,2,1,0:T(8,128)(2,1)}, bf16[4,2,256,128]{3,2,1,0:T(8,128)(2,1)S(1)}, u32[]{:S(2)}) copy-start(bf16[4,2,256,128]{3,2,1,0:T(8,128)(2,1)S(1)} %collective-permute-done.5.refs_3_) | copy-start | bytes 1572868
  99.5 2.2 %copy-start.6 = (bf16[4,2,256,128]{3,2,1,0:T(8,128)(2,1)}, bf16[4,2,256,128]{3,2,1,0:T(8,128)(2,1)S(1)}, u32[]{:S(2)}) copy-start(bf16[4,2,256,128]{3,2,1,0:T(8,128)(2,1)S(1)} %collective-permute-done.8.refs_8_) | copy-start | bytes 1572868
  99.6 6.4 %collective-permute-start.10 = (bf16[2,2,256,128]{3,2,1,0:T(8,128)(2,1)S(1)}, bf16[2,2,256,128]{3,2,1,0:T(8,128)(2,1)S(1)}, u32[]{:S(2)}, u32[]{:S(2)}) collective-permute-start(bf16[2,2,256,128]{3,2,1,0:T(8,128)(2,1)S(1)} %slice.7), channel_id=1, source_target_pairs={{8,0},{16,8},{24,16},{28,24},{20,28},{12,20},{4,12},{0,4},{9,1},{1... | collective-permute-start | bytes 786440 | tf_op jit(solution)/shard_map/ppermute | solution.py:234
  100.9 6.4 %collective-permute-start.9 = (bf16[2,2,256,128]{3,2,1,0:T(8,128)(2,1)S(1)}, bf16[2,2,256,128]{3,2,1,0:T(8,128)(2,1)S(1)}, u32[]{:S(2)}, u32[]{:S(2)}) collective-permute-start(bf16[2,2,256,128]{3,2,1,0:T(8,128)(2,1)S(1)} %slice.6), channel_id=1, source_target_pairs={{8,16},{16,24},{24,28},{28,20},{20,12},{12,4},{4,0},{0,8},{9,17},{... | collective-permute-start | bytes 786440 | tf_op jit(solution)/shard_map/ppermute | solution.py:234
  111.5 14.3 %collective-permute-start.11 = (bf16[256,512]{1,0:T(8,128)(2,1)}, bf16[256,512]{1,0:T(8,128)(2,1)S(1)}, u32[]{:S(2)}, u32[]{:S(2)}) collective-permute-start(bf16[256,512]{1,0:T(8,128)(2,1)} %get-tuple-element.23), channel_id=1, source_target_pairs={{0,0},{1,16},{2,4},{3,20},{4,8},{5,24},{6,12},{7,28},{8,1},{9,17},... | collective-permute-start | bytes 786440 | tf_op jit(solution)/shard_map/ppermute | solution.py:244
  115.0 13.9 %collective-permute-start.12 = (bf16[256,512]{1,0:T(8,128)(2,1)}, bf16[256,512]{1,0:T(8,128)(2,1)S(1)}, u32[]{:S(2)}, u32[]{:S(2)}) collective-permute-start(bf16[256,512]{1,0:T(8,128)(2,1)} %get-tuple-element.24), channel_id=1, source_target_pairs={{0,8},{1,24},{2,12},{3,28},{4,0},{5,16},{6,4},{7,20},{8,9},{9,25},... | collective-permute-start | bytes 786440 | tf_op jit(solution)/shard_map/ppermute | solution.py:244
  (2 other events, 2.1 us)
where the time goes:
time: 130 us
  waiting for transfers between devices  78.7 us (61%)
  Pallas kernels  20 us (15%)
  starting transfers between devices  18.3 us (14%)
  blocking collectives  10.3 us (8%)
  other arithmetic  1.58 us (1%)
    ppermute x6, waiting for transfers between devices, per_device(): tips = [lax.ppermute(tip, 'ctx', route) for tip, route in zip(tips, routes)]  27.2 us
    ppermute x1, waiting for transfers between devices, per_device(): far = lax.ppermute(even, 'ch', pairs)  24.2 us
    ppermute x2, waiting for transfers between devices, per_device(): found.append(lax.ppermute(sent[e], ('ctx', 'ch'), route))  13.8 us
    pallas_call x3, Pallas kernels, project(): pl.pallas_call(lambda *refs: project_kernel(shape, m, last, *refs), grid_...  13.3 us
    all_to_all x1, blocking collectives, per_device(): mix = lax.all_to_all(convolve(packed, skip, places), 'ch', 0, 0)  10.3 us
    all_to_all x1, waiting for transfers between devices, per_device(): packed = lax.all_to_all(packed, 'ctx', 0, 0)  9.2 us
    ppermute x6, starting transfers between devices, per_device(): tips = [lax.ppermute(tip, 'ctx', route) for tip, route in zip(tips, routes)]  6.08 us
    all_to_all x1, starting transfers between devices, per_device(): packed = lax.all_to_all(packed, 'ctx', 0, 0)  5.98 us
  transfers between devices with their start and end apart: 14, of which 11 were waited for; matrix products, arithmetic and copies ran while one was open for 1% of the time, Pallas kernels for 8%

commit v1 on v0

--- a/solution.py
+++ b/solution.py
@@ -49,7 +49,8 @@
     )(outer_gate, inner_gate, values_in, filters)
 
 
-def conv_kernel(places, in_ref, skip_ref, fwd_ref, inv_ref, mix_ref, xs, gs, ys):
+def conv_kernel(places, here_ref, in_ref, skip_ref, fwd_ref, inv_ref, *rest):
+    mixes, (xs, gs, ys, mix_ref) = rest[:-4], rest[-4:]
     n, _, block, chans = in_ref.shape
     for k in range(n):
         xs[k] = jnp.dot(fwd_ref[:, block:], in_ref[k, 0], preferred_element_type=F32)
@@ -86,40 +87,46 @@
         mix = in_ref[i, 2].astype(F32) * (conv + skip_ref[...] * in_ref[i, 0].astype(F32))
         chunk, place = places[i]
         mix_ref[place, chunk] = mix.astype(BF16)
-
-
-def convolve(packed, skip, places):
+    for b, ref in enumerate(mixes):
+        ref[...] = mix_ref[lax.bitwise_xor(here_ref[1], b)]
+
+
+def convolve(here, packed, skip, places):
     n, _, block, chans = packed.shape
+    m = n // 2
     forward, inverse = tables(block)
+
+    def whole(*shape):
+        return pl.BlockSpec(shape, lambda t, here: (0,) * len(shape))
+
     return pl.pallas_call(
         lambda *refs: conv_kernel(places, *refs),
-        out_shape=jax.ShapeDtypeStruct((n // 2, 2, block, chans), BF16),
-        scratch_shapes=[pltpu.VMEM((n, 2 * block, chans), F32)] * 3,
-        compiler_params=pltpu.CompilerParams(vmem_limit_bytes=16 * MIB),
+        grid_spec=pltpu.PrefetchScalarGridSpec(
+            num_scalar_prefetch=1,
+            grid=(1,),
+            in_specs=[whole(*a.shape) for a in (packed, skip, forward, inverse)],
+            out_specs=[whole(2, block, chans)] * m,
+            scratch_shapes=[pltpu.VMEM((n, 2 * block, chans), F32)] * 3
+            + [pltpu.VMEM((m, 2, block, chans), BF16)],
+        ),
+        out_shape=[jax.ShapeDtypeStruct((2, block, chans), BF16)] * m,
+        compiler_params=pltpu.CompilerParams(vmem_limit_bytes=20 * MIB),
         cost_estimate=pl.CostEstimate(flops=2**31, bytes_accessed=4 * MIB, transcendentals=0),
         name="convolve",
-    )(packed, skip, jnp.asarray(forward), jnp.asarray(inverse))
-
-
-def project_kernel(shape, m, last, here_ref, table_ref, *refs):
+    )(here, packed, skip, jnp.asarray(forward), jnp.asarray(inverse))
+
+
+def project_kernel(count, m, last, here_ref, table_ref, *refs):
     refs = list(refs)
-    total = refs.pop(0)[...] if len(refs) > sum(shape) + m * len(shape) + 1 + last else None
-    for parts in shape:
-        piece, slabs = refs[:parts], refs[parts : parts + m]
-        del refs[: parts + m]
-        left, right = [], []
-        for b in range(m):
-            source = lax.bitwise_xor(here_ref[1], b)
-            share = m // parts
-            inner = lax.bitwise_and(source, share - 1)
-            rows = piece[0][inner]
-            if parts == 2:
-                rows = jnp.where(source < share, rows, piece[1][inner])
-            left.append(rows.reshape(-1, rows.shape[-1]))
-            right.append(slabs[b][0])
+    total = refs.pop(0)[...] if len(refs) > (2 + m) * count + 1 + last else None
+    for _ in range(count):
+        piece, slabs = refs[:2], refs[2 : 2 + m]
+        del refs[: 2 + m]
+        share = m // 2
+        left = [piece[b // share][b % share] for b in range(m)]
         term = jnp.dot(
-            jnp.concatenate(left, axis=1),
-            jnp.concatenate(right, axis=0),
+            jnp.concatenate([a.reshape(-1, a.shape[-1]) for a in left], axis=1),
+            jnp.concatenate([slab[0] for slab in slabs], axis=0),
             preferred_element_type=F32,
         )
         total = term if total is None else total + term
@@ -140,7 +147,7 @@
 
 
 def project(pieces, owners, total, here, weights, last=False):
-    m = len(weights)
+    m, count = len(weights), len(pieces)
     _, chans, columns = weights[0].shape
     block = pieces[0][0].shape[-2]
     operands, specs = [], []
@@ -152,17 +159,16 @@
         operands.append(total)
         specs.append(whole(total.shape))
     for s, piece in enumerate(pieces):
-        operands += piece + weights
+        operands += list(piece) + weights
         specs += [whole(part.shape) for part in piece]
 
         def rows(t, here, table, s=s):
-            return (table[here[0] * len(pieces) + s], 0, 0)
+            return (table[here[0] * count + s], 0, 0)
 
         specs += [pl.BlockSpec((1, chans, columns), rows)] * m
     outs = [((block, columns), BF16)] * 2 if last else [((2 * block, columns), F32)]
-    shape = [len(piece) for piece in pieces]
-    return pl.pallas_call(
-        lambda *refs: project_kernel(shape, m, last, *refs),
+    found = pl.pallas_call(
+        lambda *refs: project_kernel(count, m, last, *refs),
         grid_spec=pltpu.PrefetchScalarGridSpec(
             num_scalar_prefetch=2,
             grid=(1,),
@@ -174,6 +180,7 @@
         cost_estimate=pl.CostEstimate(flops=0, bytes_accessed=0, transcendentals=0),
         name="project",
     )(here, jnp.asarray(owners.reshape(-1)), *operands)
+    return found if last else found[0]
 
 
 def ring_of(deep, across):
@@ -213,27 +220,35 @@
     packed = lax.all_to_all(packed, "ctx", 0, 0)
     skip = lax.dynamic_slice_in_dim(skip_gain, j * chans, chans, 0)[None, :]
     packed, weights = lax.optimization_barrier((packed, weights))
-    mix = lax.all_to_all(convolve(packed, skip, places), "ch", 0, 0)
+    parts = list(convolve(here, packed, skip, places))
+    parts = parts[:1] + [
+        lax.ppermute(part, "ch", [(d, d ^ b) for d in range(m)]) for b, part in enumerate(parts) if b
+    ]
 
     ring = ring_of(4, across)
     spot = np.argsort(np.array(ring))
     routes = [[(ring[p], ring[(p + way) % n]) for p in range(n)] for way in (1, -1)]
 
-    def owners(offsets):
+    def owners(*offsets):
         return np.array([[ring[(spot[a] + o) % n] for o in offsets] for a in range(n)], np.int32)
 
-    tips = [mix, mix]
-    pieces, offsets = [[mix]], [0]
-    for s in range(1, n // 2):
-        if s == n // 2 - 1:
-            total = project(pieces, owners(offsets), None, here, weights)
-        tips = [lax.ppermute(tip, "ctx", route) for tip, route in zip(tips, routes)]
-        pieces += [[tip] for tip in tips]
-        offsets += [-s, s]
-    tips, total = lax.optimization_barrier((tips, total))
-    halves = [lax.ppermute(tip[way * half : (way + 1) * half], "ctx", routes[way]) for way, tip in enumerate(tips)]
-    total = project([[tip] for tip in tips], owners(offsets[-2:]), total[0], here, weights)
-    sent = project([halves], owners([n // 2]), total[0], here, weights, last=True)
+    own = [jnp.stack(parts[:half]), jnp.stack(parts[half:])]
+    tips = [[piece, piece] for piece in own]
+    arrived, sums = [([own], [0])], None
+    for s in range(1, n // 2 + 1):
+        if s >= 3:
+            ready = arrived[: s - 1] if s == 3 else arrived[s - 2 : s - 1]
+            pieces, offsets = (sum(lists, []) for lists in zip(*ready))
+            sums = project(pieces, owners(*offsets), sums, here, weights)
+            tips[0], sums = lax.optimization_barrier((tips[0], sums))
+        for h in range(2):
+            for way in range(2) if s < n // 2 else [h]:
+                tips[h][way] = lax.ppermute(tips[h][way], "ctx", routes[way])
+        if s < n // 2:
+            arrived.append(([list(piece) for piece in zip(*tips)], [-s, s]))
+    pieces, offsets = arrived[-1]
+    sums = project(pieces, owners(*offsets), sums, here, weights)
+    sent = project([[tips[0][0], tips[1][1]]], owners(n // 2), sums, here, weights, last=True)
 
     found = []
     for e in range(2):

time: 130 us -> 122 us (0.938)
  blocking collectives: 10.3 us -> 0 us
  waiting for transfers between devices: 78.7 us -> 68.4 us
  starting transfers between devices: 18.3 us -> 26.2 us
  Pallas kernels: 20 us -> 23.6 us
    ppermute x8 -> x17, waiting for transfers between devices: 28.6 us -> 17.3 us  [the longest x14 13 us: per_device(): tips[h][way] = lax.ppermute(tips[h][way], 'ctx', routes[way])]
    all_to_all x1 -> x0, blocking collectives: 10.3 us -> none  [per_device(): mix = lax.all_to_all(convolve(packed, skip, places), 'ch', 0, 0)]
    ppermute x8 -> x17, starting transfers between devices: 8.21 us -> 16.3 us  [the longest x14 14.4 us: per_device(): tips[h][way] = lax.ppermute(tips[h][way], 'ctx', routes[way])]
    pallas_call x4 -> x5, Pallas kernels: 17.2 us -> 20.8 us  [the longest x4 16.3 us: project(): pl.pallas_call(lambda *refs: project_kernel(count, m, last, *refs), grid_...]
  transfers between devices with their start and end apart: 14 -> 23, of which waited for: 11 -> 16; matrix products, arithmetic and copies ran while one was open for 1% -> 0% of each run, Pallas kernels for 8% -> 11%
where the time goes in v1:
time: 122 us; the launch traced here: 121 us
  waiting for transfers between devices  68.4 us (56%)
  starting transfers between devices  26.2 us (21%)
  Pallas kernels  23.6 us (19%)
  local copies, waits for them, and re-layouts  1.77 us (1%)
    ppermute x1, waiting for transfers between devices, per_device(): far = lax.ppermute(even, 'ch', pairs)  24.2 us
    pallas_call x4, Pallas kernels, project(): pl.pallas_call(lambda *refs: project_kernel(count, m, last, *refs), grid_...  16.3 us
    ppermute x2, waiting for transfers between devices, per_device(): found.append(lax.ppermute(sent[e], ('ctx', 'ch'), route))  14.9 us
    ppermute x14, starting transfers between devices, per_device(): tips[h][way] = lax.ppermute(tips[h][way], 'ctx', routes[way])  14.4 us
    ppermute x14, waiting for transfers between devices, per_device(): tips[h][way] = lax.ppermute(tips[h][way], 'ctx', routes[way])  13 us
    all_to_all x1, waiting for transfers between devices, per_device(): packed = lax.all_to_all(packed, 'ctx', 0, 0)  9.2 us
    all_to_all x1, starting transfers between devices, per_device(): packed = lax.all_to_all(packed, 'ctx', 0, 0)  5.98 us
    pallas_call x1, Pallas kernels, convolve(): pl.pallas_call(lambda *refs: conv_kernel(places, *refs), grid_spec=pltpu....  4.49 us
  transfers between devices with their start and end apart: 23, of which 16 were waited for; matrix products, arithmetic and copies ran while one was open for 0% of the time, Pallas kernels for 11%

profile of v1, /device:TPU:2, one launch (start us, length us, event | category | flops | bytes accessed | tf_op | source)
XLA Modules:
  0.0 121.3 jit_solution(1530193453285607279)
XLA Ops:
  0.0 2.8 %pack.1 = bf16[8,3,256,128]{3,2,1,0:T(8,128)(2,1)} custom-call(bf16[256,1024]{1,0:T(8,128)(2,1)} %outer_ref.1, bf16[256,1024]{1,0:T(8,128)(2,1)} %inner_ref.1, bf16[256,1024]{1,0:T(8,128)(2,1)} %values_ref.1, f32[256,1024]{1,0:T(8,128)} %filters_ref.1), custom_call_target="tpu_custom_call" | custom-call | flops 262144 | bytes 4194304 | tf_op jit(solution)/shard_map/pack/pallas_call | solution.py:40
  2.8 6.0 %all-to-all-start = ((bf16[8,3,256,128]{3,2,1,0:T(8,128)(2,1)}), bf16[8,3,256,128]{3,2,1,0:T(8,128)(2,1)S(1)}, u32[]{:S(2)}, u32[]{:S(2)}) async-start(bf16[8,3,256,128]{3,2,1,0:T(8,128)(2,1)} %pack.1), calls=%async_computation | async-start | bytes 3145728 | tf_op jit(solution)/shard_map/all_to_all | solution.py:220
  9.4 24.2 %collective-permute-done.1.refs_6_.refs_12_.refs_18_.refs_7_.refs_13_ = bf16[8,128,512]{2,1,0:T(8,128)(2,1)} collective-permute-done((bf16[8,128,512]{2,1,0:T(8,128)(2,1)S(1)}, bf16[8,128,512]{2,1,0:T(8,128)(2,1)}, u32[]{:S(2)}, u32[]{:S(2)}) %collective-permute-start.1) | collective-permute-done | bytes 1048608 | tf_op jit(solution)/shard_map/ppermute | solution.py:216
  33.7 2.8 %collective-permute-done.2.refs_7_.refs_13_.refs_19_.refs_8_.refs_14_ = bf16[8,128,512]{2,1,0:T(8,128)(2,1)} collective-permute-done((bf16[8,128,512]{2,1,0:T(8,128)(2,1)}, bf16[8,128,512]{2,1,0:T(8,128)(2,1)}, u32[]{:S(2)}, u32[]{:S(2)}) %collective-permute-start.2) | collective-permute-done | bytes 1048608 | tf_op jit(solution)/shard_map/ppermute | solution.py:217
  36.6 9.2 %all-to-all-done.refs_1_ = bf16[8,3,256,128]{3,2,1,0:T(8,128)(2,1)S(1)} async-done(((bf16[8,3,256,128]{3,2,1,0:T(8,128)(2,1)}), bf16[8,3,256,128]{3,2,1,0:T(8,128)(2,1)S(1)}, u32[]{:S(2)}, u32[]{:S(2)}) %all-to-all-start) | async-done | bytes 1572896 | tf_op jit(solution)/shard_map/all_to_all | solution.py:220
  45.8 4.5 %convolve.1 = (bf16[2,256,128]{2,1,0:T(8,128)(2,1)S(1)}, bf16[2,256,128]{2,1,0:T(8,128)(2,1)S(1)}, bf16[2,256,128]{2,1,0:T(8,128)(2,1)S(1)}, bf16[2,256,128]{2,1,0:T(8,128)(2,1)S(1)}) custom-call(s32[2]{0:T(128)S(1)} %pad_add_fusion.refs_0_, bf16[8,3,256,128]{3,2,1,0:T(8,128)(2,1)S(1)} %all-to-all-done.refs_1_, ...), custom_call_target="tpu_custom_call" | custom-call | flops 2147483648 | bytes 4194304 | tf_op jit(solution)/shard_map/convolve/pallas_call | solution.py:102
  52.3 2.0 %collective-permute-start.6 = (bf16[2,2,256,128]{3,2,1,0:T(8,128)(2,1)S(1)}, bf16[2,2,256,128]{3,2,1,0:T(8,128)(2,1)S(1)}, u32[]{:S(2)}, u32[]{:S(2)}) collective-permute-start(bf16[2,2,256,128]{3,2,1,0:T(8,128)(2,1)S(1)} %pad_maximum_fusion.refs_2_), channel_id=1, source_target_pairs={{8,0},{16,8},{24,16},{28,24},{20,28},{12,20},{4,12},{0,4},{9,1},{1... | collective-permute-start | bytes 786440 | tf_op jit(solution)/shard_map/ppermute | solution.py:246
  54.3 2.4 %collective-permute-done.8 = bf16[2,256,128]{2,1,0:T(8,128)(2,1)S(1)} collective-permute-done((bf16[2,256,128]{2,1,0:T(8,128)(2,1)S(1)}, bf16[2,256,128]{2,1,0:T(8,128)(2,1)S(1)}, u32[]{:S(2)}, u32[]{:S(2)}) %collective-permute-start.8) | collective-permute-done | bytes 131104 | tf_op jit(solution)/shard_map/ppermute | solution.py:225
  56.7 1.9 %collective-permute-done.9 = bf16[2,256,128]{2,1,0:T(8,128)(2,1)S(1)} collective-permute-done((bf16[2,256,128]{2,1,0:T(8,128)(2,1)S(1)}, bf16[2,256,128]{2,1,0:T(8,128)(2,1)S(1)}, u32[]{:S(2)}, u32[]{:S(2)}) %collective-permute-start.9) | collective-permute-done | bytes 131104 | tf_op jit(solution)/shard_map/ppermute | solution.py:225
  58.7 1.5 %collective-permute-start.11 = (bf16[2,2,256,128]{3,2,1,0:T(8,128)(2,1)S(1)}, bf16[2,2,256,128]{3,2,1,0:T(8,128)(2,1)S(1)}, u32[]{:S(2)}, u32[]{:S(2)}) collective-permute-start(bf16[2,2,256,128]{3,2,1,0:T(8,128)(2,1)S(1)} %pad_maximum_fusion.1.refs_3_), channel_id=1, source_target_pairs={{8,0},{16,8},{24,16},{28,24},{20,28},{12,20},{4,12},{0,4},{9,1},{1... | collective-permute-start | bytes 786440 | tf_op jit(solution)/shard_map/ppermute | solution.py:246
  61.2 1.7 %collective-permute-start.7 = (bf16[2,2,256,128]{3,2,1,0:T(8,128)(2,1)S(1)}, bf16[2,2,256,128]{3,2,1,0:T(8,128)(2,1)S(1)}, u32[]{:S(2)}, u32[]{:S(2)}) collective-permute-start(bf16[2,2,256,128]{3,2,1,0:T(8,128)(2,1)S(1)} %collective-permute-done.6.refs_14_), channel_id=1, source_target_pairs={{8,0},{16,8},{24,16},{28,24},{20,28},{12,20},{4,12},{0,4},{9,1},{1... | collective-permute-start | bytes 786440 | tf_op jit(solution)/shard_map/ppermute | solution.py:246
  62.9 4.9 %collective-permute-done.11.refs_15_ = bf16[2,2,256,128]{3,2,1,0:T(8,128)(2,1)S(1)} collective-permute-done((bf16[2,2,256,128]{3,2,1,0:T(8,128)(2,1)S(1)}, bf16[2,2,256,128]{3,2,1,0:T(8,128)(2,1)S(1)}, u32[]{:S(2)}, u32[]{:S(2)}) %collective-permute-start.11) | collective-permute-done | bytes 262176 | tf_op jit(solution)/shard_map/ppermute | solution.py:246
  67.8 1.4 %collective-permute-start.15 = (bf16[2,2,256,128]{3,2,1,0:T(8,128)(2,1)S(1)}, bf16[2,2,256,128]{3,2,1,0:T(8,128)(2,1)S(1)}, u32[]{:S(2)}, u32[]{:S(2)}) collective-permute-start(bf16[2,2,256,128]{3,2,1,0:T(8,128)(2,1)S(1)} %collective-permute-done.11.refs_15_), channel_id=1, source_target_pairs={{8,0},{16,8},{24,16},{28,24},{20,28},{12,20},{4,12},{0,4},{9,1},{1... | collective-permute-start | bytes 786440 | tf_op jit(solution)/shard_map/ppermute | solution.py:246
  70.0 4.5 %project.4.refs_2_ = f32[512,512]{1,0:T(8,128)} custom-call(s32[2]{0:T(128)} %copy-done.1, s32[24]{0:T(128)} %constant.52.clone.refs_1_, bf16[2,2,256,128]{3,2,1,0:T(8,128)(2,1)} %copy-done.5, bf16[2,2,256,128]{3,2,1,0:T(8,128)(2,1)} %copy-done.6, bf16[8,128,512]{2,1,0:T(8,128)(2,1)} %bitcast.10, ...), custom_call_target="tpu_custom_call" | custom-call | tf_op jit(solution)/shard_map/project/pallas_call | solution.py:170
  75.5 1.4 %collective-permute-start.13 = (bf16[2,2,256,128]{3,2,1,0:T(8,128)(2,1)S(1)}, bf16[2,2,256,128]{3,2,1,0:T(8,128)(2,1)S(1)}, u32[]{:S(2)}, u32[]{:S(2)}) collective-permute-start(bf16[2,2,256,128]{3,2,1,0:T(8,128)(2,1)S(1)} %collective-permute-done.7.refs_9_), channel_id=1, source_target_pairs={{8,0},{16,8},{24,16},{28,24},{20,28},{12,20},{4,12},{0,4},{9,1},{1... | collective-permute-start | bytes 786440 | tf_op jit(solution)/shard_map/ppermute | solution.py:246
  77.0 2.1 %collective-permute-done.15.refs_10_ = bf16[2,2,256,128]{3,2,1,0:T(8,128)(2,1)S(1)} collective-permute-done((bf16[2,2,256,128]{3,2,1,0:T(8,128)(2,1)S(1)}, bf16[2,2,256,128]{3,2,1,0:T(8,128)(2,1)S(1)}, u32[]{:S(2)}, u32[]{:S(2)}) %collective-permute-start.15) | collective-permute-done | bytes 262176 | tf_op jit(solution)/shard_map/ppermute | solution.py:246
  79.0 1.4 %collective-permute-start.17 = (bf16[2,2,256,128]{3,2,1,0:T(8,128)(2,1)S(1)}, bf16[2,2,256,128]{3,2,1,0:T(8,128)(2,1)S(1)}, u32[]{:S(2)}, u32[]{:S(2)}) collective-permute-start(bf16[2,2,256,128]{3,2,1,0:T(8,128)(2,1)S(1)} %collective-permute-done.15.refs_10_), channel_id=1, source_target_pairs={{8,0},{16,8},{24,16},{28,24},{20,28},{12,20},{4,12},{0,4},{9,1},{1... | collective-permute-start | bytes 786440 | tf_op jit(solution)/shard_map/ppermute | solution.py:246
  81.2 4.2 %project.5.refs_2_ = f32[512,512]{1,0:T(8,128)} custom-call(s32[2]{0:T(128)} %copy-done.1, s32[16]{0:T(128)} %constant.53.clone.refs_1_, f32[512,512]{1,0:T(8,128)} %project.4.refs_2_, bf16[2,2,256,128]{3,2,1,0:T(8,128)(2,1)} %copy-done.11, bf16[2,2,256,128]{3,2,1,0:T(8,128)(2,1)} %copy-done.12, bf16[8,128,512]{2,1,0:T(8,128)(2,1)} %bitcast.13, ...), custom_call_target="tpu_custom_call" | custom-call | tf_op jit(solution)/shard_map/project/pallas_call | solution.py:170
  86.8 3.2 %collective-permute-done.17.refs_10_ = bf16[2,2,256,128]{3,2,1,0:T(8,128)(2,1)S(1)} collective-permute-done((bf16[2,2,256,128]{3,2,1,0:T(8,128)(2,1)S(1)}, bf16[2,2,256,128]{3,2,1,0:T(8,128)(2,1)S(1)}, u32[]{:S(2)}, u32[]{:S(2)}) %collective-permute-start.17) | collective-permute-done | bytes 262176 | tf_op jit(solution)/shard_map/ppermute | solution.py:246
  92.5 4.2 %project.6.refs_2_ = f32[512,512]{1,0:T(8,128)} custom-call(s32[2]{0:T(128)} %copy-done.1, s32[16]{0:T(128)} %constant.54.clone.refs_1_, f32[512,512]{1,0:T(8,128)} %project.5.refs_2_, bf16[2,2,256,128]{3,2,1,0:T(8,128)(2,1)} %copy-done.15, bf16[2,2,256,128]{3,2,1,0:T(8,128)(2,1)} %copy-done.19, bf16[8,128,512]{2,1,0:T(8,128)(2,1)} %bitcast.15, ...), custom_call_target="tpu_custom_call" | custom-call | tf_op jit(solution)/shard_map/project/pallas_call | solution.py:170
  98.6 3.5 %project.7 = (bf16[256,512]{1,0:T(8,128)(2,1)}, bf16[256,512]{1,0:T(8,128)(2,1)}) custom-call(s32[2]{0:T(128)} %copy-done.1, s32[8]{0:T(128)} %constant.55.clone.refs_1_, f32[512,512]{1,0:T(8,128)} %project.6.refs_2_, bf16[2,2,256,128]{3,2,1,0:T(8,128)(2,1)} %copy-done.18, bf16[2,2,256,128]{3,2,1,0:T(8,128)(2,1)} %copy-done.20, ...), custom_call_target="tpu_custom_call" | custom-call | tf_op jit(solution)/shard_map/project/pallas_call | solution.py:170
  102.0 3.3 %collective-permute-start.20 = (bf16[256,512]{1,0:T(8,128)(2,1)}, bf16[256,512]{1,0:T(8,128)(2,1)S(1)}, u32[]{:S(2)}, u32[]{:S(2)}) collective-permute-start(bf16[256,512]{1,0:T(8,128)(2,1)} %get-tuple-element.35), channel_id=1, source_target_pairs={{0,0},{1,16},{2,4},{3,20},{4,8},{5,24},{6,12},{7,28},{8,1},{9,17},... | collective-permute-start | bytes 786440 | tf_op jit(solution)/shard_map/ppermute | solution.py:259
  105.4 12.3 %collective-permute-done.20 = bf16[256,512]{1,0:T(8,128)(2,1)S(1)} collective-permute-done((bf16[256,512]{1,0:T(8,128)(2,1)}, bf16[256,512]{1,0:T(8,128)(2,1)S(1)}, u32[]{:S(2)}, u32[]{:S(2)}) %collective-permute-start.20) | collective-permute-done | bytes 262176 | tf_op jit(solution)/shard_map/ppermute | solution.py:259
  117.7 2.6 %collective-permute-done.21 = bf16[256,512]{1,0:T(8,128)(2,1)S(1)} collective-permute-done((bf16[256,512]{1,0:T(8,128)(2,1)}, bf16[256,512]{1,0:T(8,128)(2,1)S(1)}, u32[]{:S(2)}, u32[]{:S(2)}) %collective-permute-start.21) | collective-permute-done | bytes 262176 | tf_op jit(solution)/shard_map/ppermute | solution.py:259
  (75 shorter events, 13.2 us)
Async XLA Ops:
  2.8 43.0 %copy-start.3 = (bf16[256,512]{1,0:T(8,128)(2,1)S(1)}, bf16[256,512]{1,0:T(8,128)(2,1)}, u32[]{:S(2)}) copy-start(bf16[256,512]{1,0:T(8,128)(2,1)} %constant.51.clone.refs_4_) | copy-start | bytes 786436
  2.8 43.0 %all-to-all-start = ((bf16[8,3,256,128]{3,2,1,0:T(8,128)(2,1)}), bf16[8,3,256,128]{3,2,1,0:T(8,128)(2,1)S(1)}, u32[]{:S(2)}, u32[]{:S(2)}) async-start(bf16[8,3,256,128]{3,2,1,0:T(8,128)(2,1)} %pack.1), calls=%async_computation | async-start | bytes 3145728 | tf_op jit(solution)/shard_map/all_to_all | solution.py:220
  8.8 24.8 %collective-permute-start.1 = (bf16[8,128,512]{2,1,0:T(8,128)(2,1)S(1)}, bf16[8,128,512]{2,1,0:T(8,128)(2,1)}, u32[]{:S(2)}, u32[]{:S(2)}) collective-permute-start(bf16[8,128,512]{2,1,0:T(8,128)(2,1)S(1)} %bitcast.18), channel_id=1, source_target_pairs={{0,2},{1,3},{2,0},{3,1},{4,6},{5,7},{6,4},{7,5},{8,10},{9,11},{10,... | collective-permute-start | bytes 3145736 | tf_op jit(solution)/shard_map/ppermute | solution.py:216
  9.4 24.3 %collective-permute-start = (bf16[8,128,512]{2,1,0:T(8,128)(2,1)S(1)}, bf16[8,128,512]{2,1,0:T(8,128)(2,1)}, u32[]{:S(2)}, u32[]{:S(2)}) collective-permute-start(bf16[8,128,512]{2,1,0:T(8,128)(2,1)S(1)} %bitcast.19), channel_id=1, source_target_pairs={{0,1},{1,0},{2,3},{3,2},{4,5},{5,4},{6,7},{7,6},{8,9},{9,8},{10,11... | collective-permute-start | bytes 3145736 | tf_op jit(solution)/shard_map/ppermute | solution.py:213
  33.6 3.0 %collective-permute-start.2 = (bf16[8,128,512]{2,1,0:T(8,128)(2,1)}, bf16[8,128,512]{2,1,0:T(8,128)(2,1)}, u32[]{:S(2)}, u32[]{:S(2)}) collective-permute-start(bf16[8,128,512]{2,1,0:T(8,128)(2,1)} %collective-permute-done.1.refs_6_.refs_12_.refs_18_.refs_7_.refs_13_), channel_id=1, source_target_pairs={{0,1},{1,0},{2,3},{3,2},{4,5},{5,4},{6,7},{7,6},{8,9},{9,8},{10,11... | collective-permute-start | bytes 3145736 | tf_op jit(solution)/shard_map/ppermute | solution.py:217
  50.3 1.9 %collective-permute-start.3 = (bf16[2,256,128]{2,1,0:T(8,128)(2,1)S(1)}, bf16[2,256,128]{2,1,0:T(8,128)(2,1)S(1)}, u32[]{:S(2)}, u32[]{:S(2)}) collective-permute-start(bf16[2,256,128]{2,1,0:T(8,128)(2,1)S(1)} %get-tuple-element.23), channel_id=1, source_target_pairs={{0,1},{1,0},{2,3},{3,2},{4,5},{5,4},{6,7},{7,6},{8,9},{9,8},{10,11... | collective-permute-start | bytes 393224 | tf_op jit(solution)/shard_map/ppermute | solution.py:225
  50.4 6.4 %collective-permute-start.8 = (bf16[2,256,128]{2,1,0:T(8,128)(2,1)S(1)}, bf16[2,256,128]{2,1,0:T(8,128)(2,1)S(1)}, u32[]{:S(2)}, u32[]{:S(2)}) collective-permute-start(bf16[2,256,128]{2,1,0:T(8,128)(2,1)S(1)} %get-tuple-element.24), channel_id=1, source_target_pairs={{0,2},{1,3},{2,0},{3,1},{4,6},{5,7},{6,4},{7,5},{8,10},{9,11},{10,... | collective-permute-start | bytes 393224 | tf_op jit(solution)/shard_map/ppermute | solution.py:225
  51.0 7.7 %collective-permute-start.9 = (bf16[2,256,128]{2,1,0:T(8,128)(2,1)S(1)}, bf16[2,256,128]{2,1,0:T(8,128)(2,1)S(1)}, u32[]{:S(2)}, u32[]{:S(2)}) collective-permute-start(bf16[2,256,128]{2,1,0:T(8,128)(2,1)S(1)} %get-tuple-element.25), channel_id=1, source_target_pairs={{0,3},{1,2},{2,1},{3,0},{4,7},{5,6},{6,5},{7,4},{8,11},{9,10},{10,... | collective-permute-start | bytes 393224 | tf_op jit(solution)/shard_map/ppermute | solution.py:225
  52.3 8.6 %collective-permute-start.4 = (bf16[2,2,256,128]{3,2,1,0:T(8,128)(2,1)S(1)}, bf16[2,2,256,128]{3,2,1,0:T(8,128)(2,1)S(1)}, u32[]{:S(2)}, u32[]{:S(2)}) collective-permute-start(bf16[2,2,256,128]{3,2,1,0:T(8,128)(2,1)S(1)} %pad_maximum_fusion.refs_2_), channel_id=1, source_target_pairs={{8,16},{16,24},{24,28},{28,20},{20,12},{12,4},{4,0},{0,8},{9,17},{... | collective-permute-start | bytes 786440 | tf_op jit(solution)/shard_map/ppermute | solution.py:246
  52.3 8.8 %collective-permute-start.6 = (bf16[2,2,256,128]{3,2,1,0:T(8,128)(2,1)S(1)}, bf16[2,2,256,128]{3,2,1,0:T(8,128)(2,1)S(1)}, u32[]{:S(2)}, u32[]{:S(2)}) collective-permute-start(bf16[2,2,256,128]{3,2,1,0:T(8,128)(2,1)S(1)} %pad_maximum_fusion.refs_2_), channel_id=1, source_target_pairs={{8,0},{16,8},{24,16},{28,24},{20,28},{12,20},{4,12},{0,4},{9,1},{1... | collective-permute-start | bytes 786440 | tf_op jit(solution)/shard_map/ppermute | solution.py:246
  58.7 9.1 %collective-permute-start.11 = (bf16[2,2,256,128]{3,2,1,0:T(8,128)(2,1)S(1)}, bf16[2,2,256,128]{3,2,1,0:T(8,128)(2,1)S(1)}, u32[]{:S(2)}, u32[]{:S(2)}) collective-permute-start(bf16[2,2,256,128]{3,2,1,0:T(8,128)(2,1)S(1)} %pad_maximum_fusion.1.refs_3_), channel_id=1, source_target_pairs={{8,0},{16,8},{24,16},{28,24},{20,28},{12,20},{4,12},{0,4},{9,1},{1... | collective-permute-start | bytes 786440 | tf_op jit(solution)/shard_map/ppermute | solution.py:246
  60.1 9.1 %collective-permute-start.10 = (bf16[2,2,256,128]{3,2,1,0:T(8,128)(2,1)S(1)}, bf16[2,2,256,128]{3,2,1,0:T(8,128)(2,1)S(1)}, u32[]{:S(2)}, u32[]{:S(2)}) collective-permute-start(bf16[2,2,256,128]{3,2,1,0:T(8,128)(2,1)S(1)} %pad_maximum_fusion.1.refs_3_), channel_id=1, source_target_pairs={{8,16},{16,24},{24,28},{28,20},{20,12},{12,4},{4,0},{0,8},{9,17},{... | collective-permute-start | bytes 786440 | tf_op jit(solution)/shard_map/ppermute | solution.py:246
  60.9 14.0 %collective-permute-start.5 = (bf16[2,2,256,128]{3,2,1,0:T(8,128)(2,1)S(1)}, bf16[2,2,256,128]{3,2,1,0:T(8,128)(2,1)S(1)}, u32[]{:S(2)}, u32[]{:S(2)}) collective-permute-start(bf16[2,2,256,128]{3,2,1,0:T(8,128)(2,1)S(1)} %collective-permute-done.4.refs_8_), channel_id=1, source_target_pairs={{8,16},{16,24},{24,28},{28,20},{20,12},{12,4},{4,0},{0,8},{9,17},{... | collective-permute-start | bytes 786440 | tf_op jit(solution)/shard_map/ppermute | solution.py:246
  61.2 13.7 %collective-permute-start.7 = (bf16[2,2,256,128]{3,2,1,0:T(8,128)(2,1)S(1)}, bf16[2,2,256,128]{3,2,1,0:T(8,128)(2,1)S(1)}, u32[]{:S(2)}, u32[]{:S(2)}) collective-permute-start(bf16[2,2,256,128]{3,2,1,0:T(8,128)(2,1)S(1)} %collective-permute-done.6.refs_14_), channel_id=1, source_target_pairs={{8,0},{16,8},{24,16},{28,24},{20,28},{12,20},{4,12},{0,4},{9,1},{1... | collective-permute-start | bytes 786440 | tf_op jit(solution)/shard_map/ppermute | solution.py:246
  67.8 11.2 %collective-permute-start.15 = (bf16[2,2,256,128]{3,2,1,0:T(8,128)(2,1)S(1)}, bf16[2,2,256,128]{3,2,1,0:T(8,128)(2,1)S(1)}, u32[]{:S(2)}, u32[]{:S(2)}) collective-permute-start(bf16[2,2,256,128]{3,2,1,0:T(8,128)(2,1)S(1)} %collective-permute-done.11.refs_15_), channel_id=1, source_target_pairs={{8,0},{16,8},{24,16},{28,24},{20,28},{12,20},{4,12},{0,4},{9,1},{1... | collective-permute-start | bytes 786440 | tf_op jit(solution)/shard_map/ppermute | solution.py:246
  69.3 11.2 %collective-permute-start.14 = (bf16[2,2,256,128]{3,2,1,0:T(8,128)(2,1)S(1)}, bf16[2,2,256,128]{3,2,1,0:T(8,128)(2,1)S(1)}, u32[]{:S(2)}, u32[]{:S(2)}) collective-permute-start(bf16[2,2,256,128]{3,2,1,0:T(8,128)(2,1)S(1)} %collective-permute-done.10.refs_9_), channel_id=1, source_target_pairs={{8,16},{16,24},{24,28},{28,20},{20,12},{12,4},{4,0},{0,8},{9,17},{... | collective-permute-start | bytes 786440 | tf_op jit(solution)/shard_map/ppermute | solution.py:246
  74.9 11.2 %collective-permute-start.12 = (bf16[2,2,256,128]{3,2,1,0:T(8,128)(2,1)S(1)}, bf16[2,2,256,128]{3,2,1,0:T(8,128)(2,1)S(1)}, u32[]{:S(2)}, u32[]{:S(2)}) collective-permute-start(bf16[2,2,256,128]{3,2,1,0:T(8,128)(2,1)S(1)} %collective-permute-done.5.refs_3_), channel_id=1, source_target_pairs={{8,16},{16,24},{24,28},{28,20},{20,12},{12,4},{4,0},{0,8},{9,17},{... | collective-permute-start | bytes 786440 | tf_op jit(solution)/shard_map/ppermute | solution.py:246
  75.5 10.6 %collective-permute-start.13 = (bf16[2,2,256,128]{3,2,1,0:T(8,128)(2,1)S(1)}, bf16[2,2,256,128]{3,2,1,0:T(8,128)(2,1)S(1)}, u32[]{:S(2)}, u32[]{:S(2)}) collective-permute-start(bf16[2,2,256,128]{3,2,1,0:T(8,128)(2,1)S(1)} %collective-permute-done.7.refs_9_), channel_id=1, source_target_pairs={{8,0},{16,8},{24,16},{28,24},{20,28},{12,20},{4,12},{0,4},{9,1},{1... | collective-permute-start | bytes 786440 | tf_op jit(solution)/shard_map/ppermute | solution.py:246
  79.0 10.9 %collective-permute-start.17 = (bf16[2,2,256,128]{3,2,1,0:T(8,128)(2,1)S(1)}, bf16[2,2,256,128]{3,2,1,0:T(8,128)(2,1)S(1)}, u32[]{:S(2)}, u32[]{:S(2)}) collective-permute-start(bf16[2,2,256,128]{3,2,1,0:T(8,128)(2,1)S(1)} %collective-permute-done.15.refs_10_), channel_id=1, source_target_pairs={{8,0},{16,8},{24,16},{28,24},{20,28},{12,20},{4,12},{0,4},{9,1},{1... | collective-permute-start | bytes 786440 | tf_op jit(solution)/shard_map/ppermute | solution.py:246
  80.5 11.2 %collective-permute-start.16 = (bf16[2,2,256,128]{3,2,1,0:T(8,128)(2,1)S(1)}, bf16[2,2,256,128]{3,2,1,0:T(8,128)(2,1)S(1)}, u32[]{:S(2)}, u32[]{:S(2)}) collective-permute-start(bf16[2,2,256,128]{3,2,1,0:T(8,128)(2,1)S(1)} %collective-permute-done.14.refs_4_), channel_id=1, source_target_pairs={{8,16},{16,24},{24,28},{28,20},{20,12},{12,4},{4,0},{0,8},{9,17},{... | collective-permute-start | bytes 786440 | tf_op jit(solution)/shard_map/ppermute | solution.py:246
  86.1 10.6 %collective-permute-start.18 = (bf16[2,2,256,128]{3,2,1,0:T(8,128)(2,1)S(1)}, bf16[2,2,256,128]{3,2,1,0:T(8,128)(2,1)S(1)}, u32[]{:S(2)}, u32[]{:S(2)}) collective-permute-start(bf16[2,2,256,128]{3,2,1,0:T(8,128)(2,1)S(1)} %collective-permute-done.12.refs_3_), channel_id=1, source_target_pairs={{8,16},{16,24},{24,28},{28,20},{20,12},{12,4},{4,0},{0,8},{9,17},{... | collective-permute-start | bytes 786440 | tf_op jit(solution)/shard_map/ppermute | solution.py:246
  90.0 7.9 %collective-permute-start.19 = (bf16[2,2,256,128]{3,2,1,0:T(8,128)(2,1)S(1)}, bf16[2,2,256,128]{3,2,1,0:T(8,128)(2,1)S(1)}, u32[]{:S(2)}, u32[]{:S(2)}) collective-permute-start(bf16[2,2,256,128]{3,2,1,0:T(8,128)(2,1)S(1)} %collective-permute-done.17.refs_10_), channel_id=1, source_target_pairs={{8,0},{16,8},{24,16},{28,24},{20,28},{12,20},{4,12},{0,4},{9,1},{1... | collective-permute-start | bytes 786440 | tf_op jit(solution)/shard_map/ppermute | solution.py:246
  102.0 15.7 %collective-permute-start.20 = (bf16[256,512]{1,0:T(8,128)(2,1)}, bf16[256,512]{1,0:T(8,128)(2,1)S(1)}, u32[]{:S(2)}, u32[]{:S(2)}) collective-permute-start(bf16[256,512]{1,0:T(8,128)(2,1)} %get-tuple-element.35), channel_id=1, source_target_pairs={{0,0},{1,16},{2,4},{3,20},{4,8},{5,24},{6,12},{7,28},{8,1},{9,17},... | collective-permute-start | bytes 786440 | tf_op jit(solution)/shard_map/ppermute | solution.py:259
  105.3 15.0 %collective-permute-start.21 = (bf16[256,512]{1,0:T(8,128)(2,1)}, bf16[256,512]{1,0:T(8,128)(2,1)S(1)}, u32[]{:S(2)}, u32[]{:S(2)}) collective-permute-start(bf16[256,512]{1,0:T(8,128)(2,1)} %get-tuple-element.36), channel_id=1, source_target_pairs={{0,8},{1,24},{2,12},{3,28},{4,0},{5,16},{6,4},{7,20},{8,9},{9,25},... | collective-permute-start | bytes 786440 | tf_op jit(solution)/shard_map/ppermute | solution.py:259
  (20 other events, 179.3 us)

commit v2 on v1

--- a/solution.py
+++ b/solution.py
@@ -22,36 +22,46 @@
     return forward.astype(BF16), inverse.astype(BF16)
 
 
-def pack_kernel(outer_ref, inner_ref, values_ref, filters_ref, out_ref):
-    n, _, _, chans = out_ref.shape
+def pack_kernel(here_ref, outer_ref, inner_ref, values_ref, filters_ref, *rest):
+    outs, ordered = rest[:-1], rest[-1]
+    n, _, _, chans = ordered.shape
     gated = (inner_ref[...].astype(F32) * values_ref[...].astype(F32)).astype(BF16)
     lags = filters_ref[...].astype(BF16)
     outer = outer_ref[...]
     for d in range(n):
         part = slice(d * chans, (d + 1) * chans)
-        out_ref[d, 0] = gated[:, part]
-        out_ref[d, 1] = lags[:, part]
-        out_ref[d, 2] = outer[:, part]
-
-
-def pack(outer_gate, inner_gate, values_in, filters, n):
+        ordered[d, 0] = gated[:, part]
+        ordered[d, 1] = lags[:, part]
+        ordered[d, 2] = outer[:, part]
+    for d, out in enumerate(outs):
+        out[...] = ordered[lax.bitwise_xor(here_ref[0], d)]
+
+
+def pack(here, outer_gate, inner_gate, values_in, filters, n):
     block, wide = outer_gate.shape
-    tile = block // 2
+    tile, chans = block // 2, wide // n
     return pl.pallas_call(
         pack_kernel,
-        grid=(block // tile,),
-        in_specs=[pl.BlockSpec((tile, wide), lambda t: (t, 0))] * 4,
-        out_specs=pl.BlockSpec((n, 3, tile, wide // n), lambda t: (0, 0, t, 0)),
-        out_shape=jax.ShapeDtypeStruct((n, 3, block, wide // n), BF16),
+        grid_spec=pltpu.PrefetchScalarGridSpec(
+            num_scalar_prefetch=1,
+            grid=(block // tile,),
+            in_specs=[pl.BlockSpec((tile, wide), lambda t, here: (t, 0))] * 4,
+            out_specs=[pl.BlockSpec((3, tile, chans), lambda t, here: (0, t, 0))] * n,
+            scratch_shapes=[pltpu.VMEM((n, 3, tile, chans), BF16)],
+        ),
+        out_shape=[jax.ShapeDtypeStruct((3, block, chans), BF16)] * n,
         compiler_params=pltpu.CompilerParams(vmem_limit_bytes=60 * MIB),
-        cost_estimate=pl.CostEstimate(flops=2**18, bytes_accessed=4 * MIB, transcendentals=0),
+        cost_estimate=pl.CostEstimate(flops=0, bytes_accessed=0, transcendentals=0),
         name="pack",
-    )(outer_gate, inner_gate, values_in, filters)
-
-
-def conv_kernel(places, here_ref, in_ref, skip_ref, fwd_ref, inv_ref, *rest):
-    mixes, (xs, gs, ys, mix_ref) = rest[:-4], rest[-4:]
+    )(here, outer_gate, inner_gate, values_in, filters)
+
+
+def conv_kernel(places, here_ref, skip_ref, fwd_ref, inv_ref, *rest):
+    rest, (xs, gs, ys, mix_ref, in_ref) = rest[:-5], rest[-5:]
     n, _, block, chans = in_ref.shape
+    mixes = rest[n:]
+    for d, ref in enumerate(rest[:n]):
+        in_ref[lax.bitwise_xor(here_ref[0], d)] = ref[...]
     for k in range(n):
         xs[k] = jnp.dot(fwd_ref[:, block:], in_ref[k, 0], preferred_element_type=F32)
         lag = jnp.dot(fwd_ref[:, block:], in_ref[k, 1], preferred_element_type=F32)
@@ -92,7 +102,8 @@
 
 
 def convolve(here, packed, skip, places):
-    n, _, block, chans = packed.shape
+    n = len(packed)
+    _, block, chans = packed[0].shape
     m = n // 2
     forward, inverse = tables(block)
 
@@ -104,16 +115,16 @@
         grid_spec=pltpu.PrefetchScalarGridSpec(
             num_scalar_prefetch=1,
             grid=(1,),
-            in_specs=[whole(*a.shape) for a in (packed, skip, forward, inverse)],
+            in_specs=[whole(*a.shape) for a in (skip, forward, inverse, *packed)],
             out_specs=[whole(2, block, chans)] * m,
             scratch_shapes=[pltpu.VMEM((n, 2 * block, chans), F32)] * 3
-            + [pltpu.VMEM((m, 2, block, chans), BF16)],
+            + [pltpu.VMEM((m, 2, block, chans), BF16), pltpu.VMEM((n, 3, block, chans), BF16)],
         ),
         out_shape=[jax.ShapeDtypeStruct((2, block, chans), BF16)] * m,
         compiler_params=pltpu.CompilerParams(vmem_limit_bytes=20 * MIB),
         cost_estimate=pl.CostEstimate(flops=2**31, bytes_accessed=4 * MIB, transcendentals=0),
         name="convolve",
-    )(here, packed, skip, jnp.asarray(forward), jnp.asarray(inverse))
+    )(here, skip, jnp.asarray(forward), jnp.asarray(inverse), *packed)
 
 
 def project_kernel(count, m, last, here_ref, table_ref, *refs):
@@ -176,7 +187,7 @@
             out_specs=[whole(size) for size, _ in outs],
         ),
         out_shape=[jax.ShapeDtypeStruct(*out) for out in outs],
-        compiler_params=pltpu.CompilerParams(vmem_limit_bytes=60 * MIB),
+        compiler_params=pltpu.CompilerParams(vmem_limit_bytes=(10 if last else 60) * MIB),
         cost_estimate=pl.CostEstimate(flops=0, bytes_accessed=0, transcendentals=0),
         name="project",
     )(here, jnp.asarray(owners.reshape(-1)), *operands)
@@ -206,20 +217,17 @@
 
     places = {row_block(h, d): (h, d) for h in range(2) for d in range(m)}
 
+    packed = list(pack(here, outer_gate, inner_gate, values_in, filters, n))
+    far, near = list(range(n - 1, n // 2 - 1, -1)), list(range(1, n // 2))
+    order = far[:1] + [d for pair in zip(far[1:], near) for d in pair]
+    for d in order:
+        packed[d] = lax.ppermute(packed[d], "ctx", [(i, i ^ d) for i in range(n)])
+    skip = lax.dynamic_slice_in_dim(skip_gain, j * chans, chans, 0)[None, :]
+
     weights = [w_out.reshape(n, chans, -1)]
-    while len(weights) < m:
-        pairs = [(d, d ^ len(weights)) for d in range(m)]
-        if len(weights) == 1:
-            weights.append(lax.ppermute(weights[0], "ch", pairs))
-        else:
-            for even in list(weights[::2]):
-                far = lax.ppermute(even, "ch", pairs)
-                weights += [far, lax.ppermute(far, "ch", [(d, d ^ 1) for d in range(m)])]
-
-    packed = pack(outer_gate, inner_gate, values_in, filters, n)
-    packed = lax.all_to_all(packed, "ctx", 0, 0)
-    skip = lax.dynamic_slice_in_dim(skip_gain, j * chans, chans, 0)[None, :]
-    packed, weights = lax.optimization_barrier((packed, weights))
+    for b in range(1, m):
+        weights.append(lax.ppermute(weights[0], "ch", [(d, d ^ b) for d in range(m)]))
+    packed, weights[:-1] = lax.optimization_barrier((packed, weights[:-1]))
     parts = list(convolve(here, packed, skip, places))
     parts = parts[:1] + [
         lax.ppermute(part, "ch", [(d, d ^ b) for d in range(m)]) for b, part in enumerate(parts) if b
@@ -232,6 +240,7 @@
     def owners(*offsets):
         return np.array([[ring[(spot[a] + o) % n] for o in offsets] for a in range(n)], np.int32)
 
+    parts[half:], weights[-1] = lax.optimization_barrier((parts[half:], weights[-1]))
     own = [jnp.stack(parts[:half]), jnp.stack(parts[half:])]
     tips = [[piece, piece] for piece in own]
     arrived, sums = [([own], [0])], None

time: 122 us -> 136 us (1.11)
  starting transfers between devices: 26.2 us -> 44.7 us
  waiting for transfers between devices: 68.4 us -> 55 us
  local copies, waits for them, and re-layouts: 1.77 us -> 9.32 us
    ppermute x3 -> x10, starting transfers between devices: 0.61 us -> 18.2 us  [the longest x7 17.2 us: per_device(): packed[d] = lax.ppermute(packed[d], 'ctx', [(i, i ^ d) for i in range(n)])]
    all_to_all x1 -> x0, waiting for transfers between devices: 9.2 us -> none  [per_device(): packed = lax.all_to_all(packed, 'ctx', 0, 0)]
    unnamed x42 -> x58, local copies, waits for them, and re-layouts: 1.69 us -> 9.25 us
    ppermute x14, starting transfers between devices: 14.4 us -> 20.8 us  [per_device(): tips[h][way] = lax.ppermute(tips[h][way], 'ctx', routes[way])]
    all_to_all x1 -> x0, starting transfers between devices: 5.98 us -> none  [per_device(): packed = lax.all_to_all(packed, 'ctx', 0, 0)]
    ppermute x3 -> x10, waiting for transfers between devices: 27 us -> 23.3 us  [the longest x7 23.2 us: per_device(): packed[d] = lax.ppermute(packed[d], 'ctx', [(i, i ^ d) for i in range(n)])]
    ppermute x3, waiting for transfers between devices: 4.28 us -> 1.07 us  [per_device(): lax.ppermute(part, 'ch', [(d, d ^ b) for d in range(m)])]
    ppermute x14, waiting for transfers between devices: 13 us -> 15.4 us  [per_device(): tips[h][way] = lax.ppermute(tips[h][way], 'ctx', routes[way])]
  transfers between devices with their start and end apart: 23 -> 29, of which waited for: 16 -> 16; matrix products, arithmetic and copies ran while one was open for 0% -> 1% of each run, Pallas kernels for 11% -> 16%
where the time goes in v2:
time: 136 us; the launch traced here: 135 us
  waiting for transfers between devices  55 us (40%)
  starting transfers between devices  44.7 us (33%)
  Pallas kernels  24.6 us (18%)
  local copies, waits for them, and re-layouts  9.32 us (7%)
  other arithmetic  1.6 us (1%)
    ppermute x7, waiting for transfers between devices, per_device(): packed[d] = lax.ppermute(packed[d], 'ctx', [(i, i ^ d) for i in range(n)])  23.2 us
    ppermute x14, starting transfers between devices, per_device(): tips[h][way] = lax.ppermute(tips[h][way], 'ctx', routes[way])  20.8 us
    ppermute x7, starting transfers between devices, per_device(): packed[d] = lax.ppermute(packed[d], 'ctx', [(i, i ^ d) for i in range(n)])  17.2 us
    pallas_call x4, Pallas kernels, project(): pl.pallas_call(lambda *refs: project_kernel(count, m, last, *refs), grid_...  15.5 us
    ppermute x14, waiting for transfers between devices, per_device(): tips[h][way] = lax.ppermute(tips[h][way], 'ctx', routes[way])  15.4 us
    ppermute x2, waiting for transfers between devices, per_device(): found.append(lax.ppermute(sent[e], ('ctx', 'ch'), route))  15.2 us
    unnamed x58, local copies, waits for them, and re-layouts  9.25 us
    pallas_call x1, Pallas kernels, convolve(): pl.pallas_call(lambda *refs: conv_kernel(places, *refs), grid_spec=pltpu....  5.54 us
  transfers between devices with their start and end apart: 29, of which 16 were waited for; matrix products, arithmetic and copies ran while one was open for 1% of the time, Pallas kernels for 16%

profile of v2, /device:TPU:2, one launch (start us, length us, event | category | flops | bytes accessed | tf_op | source)
XLA Modules:
  0.0 135.5 jit_solution(16918205405840120683)
XLA Ops:
  0.7 3.6 %pack.1 = (bf16[3,256,128]{2,1,0:T(8,128)(2,1)}, bf16[3,256,128]{2,1,0:T(8,128)(2,1)}, bf16[3,256,128]{2,1,0:T(8,128)(2,1)}, bf16[3,256,128]{2,1,0:T(8,128)(2,1)...) custom-call(s32[2]{0:T(128)} %pad_add_fusion.here_ref.refs_0_, ...), custom_call_target="tpu_custom_call" | custom-call | tf_op jit(solution)/shard_map/pack/pallas_call | solution.py:43
  9.0 2.9 %collective-permute-done.refs_5_ = bf16[3,256,128]{2,1,0:T(8,128)(2,1)S(1)} collective-permute-done((bf16[3,256,128]{2,1,0:T(8,128)(2,1)}, bf16[3,256,128]{2,1,0:T(8,128)(2,1)S(1)}, u32[]{:S(2)}, u32[]{:S(2)}) %collective-permute-start) | collective-permute-done | bytes 196640 | tf_op jit(solution)/shard_map/ppermute | solution.py:224
  11.8 2.8 %collective-permute-start.2 = (bf16[3,256,128]{2,1,0:T(8,128)(2,1)}, bf16[3,256,128]{2,1,0:T(8,128)(2,1)S(1)}, u32[]{:S(2)}, u32[]{:S(2)}) collective-permute-start(bf16[3,256,128]{2,1,0:T(8,128)(2,1)} %get-tuple-element.41), channel_id=1, source_target_pairs={{0,12},{4,8},{8,4},{12,0},{16,28},{20,24},{24,20},{28,16},{1,13},{... | collective-permute-start | bytes 589832 | tf_op jit(solution)/shard_map/ppermute | solution.py:224
  15.0 2.6 %collective-permute-start.3 = (bf16[3,256,128]{2,1,0:T(8,128)(2,1)}, bf16[3,256,128]{2,1,0:T(8,128)(2,1)S(1)}, u32[]{:S(2)}, u32[]{:S(2)}) collective-permute-start(bf16[3,256,128]{2,1,0:T(8,128)(2,1)} %get-tuple-element.42), channel_id=1, source_target_pairs={{0,16},{4,20},{8,24},{12,28},{16,0},{20,4},{24,8},{28,12},{1,17},{... | collective-permute-start | bytes 589832 | tf_op jit(solution)/shard_map/ppermute | solution.py:224
  17.6 3.8 %collective-permute-done.2.refs_7_ = bf16[3,256,128]{2,1,0:T(8,128)(2,1)S(1)} collective-permute-done((bf16[3,256,128]{2,1,0:T(8,128)(2,1)}, bf16[3,256,128]{2,1,0:T(8,128)(2,1)S(1)}, u32[]{:S(2)}, u32[]{:S(2)}) %collective-permute-start.2) | collective-permute-done | bytes 196640 | tf_op jit(solution)/shard_map/ppermute | solution.py:224
  22.1 3.1 %collective-permute-start.4 = (bf16[3,256,128]{2,1,0:T(8,128)(2,1)}, bf16[3,256,128]{2,1,0:T(8,128)(2,1)S(1)}, u32[]{:S(2)}, u32[]{:S(2)}) collective-permute-start(bf16[3,256,128]{2,1,0:T(8,128)(2,1)} %get-tuple-element.43), channel_id=1, source_target_pairs={{0,20},{4,16},{8,28},{12,24},{16,4},{20,0},{24,12},{28,8},{1,21},{... | collective-permute-start | bytes 589832 | tf_op jit(solution)/shard_map/ppermute | solution.py:224
  25.2 7.1 %collective-permute-done.3.refs_8_ = bf16[3,256,128]{2,1,0:T(8,128)(2,1)S(1)} collective-permute-done((bf16[3,256,128]{2,1,0:T(8,128)(2,1)}, bf16[3,256,128]{2,1,0:T(8,128)(2,1)S(1)}, u32[]{:S(2)}, u32[]{:S(2)}) %collective-permute-start.3) | collective-permute-done | bytes 196640 | tf_op jit(solution)/shard_map/ppermute | solution.py:224
  33.0 3.0 %collective-permute-start.5 = (bf16[3,256,128]{2,1,0:T(8,128)(2,1)}, bf16[3,256,128]{2,1,0:T(8,128)(2,1)}, u32[]{:S(2)}, u32[]{:S(2)}) collective-permute-start(bf16[3,256,128]{2,1,0:T(8,128)(2,1)} %get-tuple-element.44), channel_id=1, source_target_pairs={{0,24},{4,28},{8,16},{12,20},{16,8},{20,12},{24,0},{28,4},{1,25},{... | collective-permute-start | bytes 589832 | tf_op jit(solution)/shard_map/ppermute | solution.py:224
  36.0 2.4 %collective-permute-done.4.refs_9_ = bf16[3,256,128]{2,1,0:T(8,128)(2,1)S(1)} collective-permute-done((bf16[3,256,128]{2,1,0:T(8,128)(2,1)}, bf16[3,256,128]{2,1,0:T(8,128)(2,1)S(1)}, u32[]{:S(2)}, u32[]{:S(2)}) %collective-permute-start.4) | collective-permute-done | bytes 196640 | tf_op jit(solution)/shard_map/ppermute | solution.py:224
  41.2 6.6 %collective-permute-done.6.refs_11_ = bf16[3,256,128]{2,1,0:T(8,128)(2,1)} collective-permute-done((bf16[3,256,128]{2,1,0:T(8,128)(2,1)}, bf16[3,256,128]{2,1,0:T(8,128)(2,1)}, u32[]{:S(2)}, u32[]{:S(2)}) %collective-permute-start.6) | collective-permute-done | bytes 196640 | tf_op jit(solution)/shard_map/ppermute | solution.py:224
  53.8 5.5 %convolve.1 = (bf16[2,256,128]{2,1,0:T(8,128)(2,1)S(1)}, bf16[2,256,128]{2,1,0:T(8,128)(2,1)S(1)}, bf16[2,256,128]{2,1,0:T(8,128)(2,1)S(1)}, bf16[2,256,128]{2,1,0:T(8,128)(2,1)S(1)}) custom-call(s32[2]{0:T(128)S(1)} %copy-done.8, f32[1,128]{1,0:T(1,128)S(1)} %dynamic-slice_bitcast_fusion.refs_1_, bf16[512,512]{1,0:T(8,128)(2,1)S(1)} %copy-done.18, ...), custom_call_target="tpu_custom_call" | custom-call | flops 2147483648 | bytes 4194304 | tf_op jit(solution)/shard_map/convolve/pallas_call | solution.py:113
  61.4 5.3 %collective-permute-start.10 = (bf16[2,2,256,128]{3,2,1,0:T(8,128)(2,1)S(1)}, bf16[2,2,256,128]{3,2,1,0:T(8,128)(2,1)S(1)}, u32[]{:S(2)}, u32[]{:S(2)}) collective-permute-start(bf16[2,2,256,128]{3,2,1,0:T(8,128)(2,1)S(1)} %pad_maximum_fusion.refs_2_), channel_id=1, source_target_pairs={{8,16},{16,24},{24,28},{28,20},{20,12},{12,4},{4,0},{0,8},{9,17},{... | collective-permute-start | bytes 786440 | tf_op jit(solution)/shard_map/ppermute | solution.py:255
  69.3 3.8 %collective-permute-start.17 = (bf16[2,2,256,128]{3,2,1,0:T(8,128)(2,1)S(1)}, bf16[2,2,256,128]{3,2,1,0:T(8,128)(2,1)S(1)}, u32[]{:S(2)}, u32[]{:S(2)}) collective-permute-start(bf16[2,2,256,128]{3,2,1,0:T(8,128)(2,1)S(1)} %pad_maximum_fusion.1.refs_3_), channel_id=1, source_target_pairs={{8,16},{16,24},{24,28},{28,20},{20,12},{12,4},{4,0},{0,8},{9,17},{... | collective-permute-start | bytes 786440 | tf_op jit(solution)/shard_map/ppermute | solution.py:255
  73.1 2.4 %collective-permute-start.11 = (bf16[2,2,256,128]{3,2,1,0:T(8,128)(2,1)S(1)}, bf16[2,2,256,128]{3,2,1,0:T(8,128)(2,1)S(1)}, u32[]{:S(2)}, u32[]{:S(2)}) collective-permute-start(bf16[2,2,256,128]{3,2,1,0:T(8,128)(2,1)S(1)} %collective-permute-done.10.refs_8_), channel_id=1, source_target_pairs={{8,16},{16,24},{24,28},{28,20},{20,12},{12,4},{4,0},{0,8},{9,17},{... | collective-permute-start | bytes 786440 | tf_op jit(solution)/shard_map/ppermute | solution.py:255
  76.2 5.6 %collective-permute-done.18.refs_15_ = bf16[2,2,256,128]{3,2,1,0:T(8,128)(2,1)S(1)} collective-permute-done((bf16[2,2,256,128]{3,2,1,0:T(8,128)(2,1)S(1)}, bf16[2,2,256,128]{3,2,1,0:T(8,128)(2,1)S(1)}, u32[]{:S(2)}, u32[]{:S(2)}) %collective-permute-start.18) | collective-permute-done | bytes 262176 | tf_op jit(solution)/shard_map/ppermute | solution.py:255
  83.8 4.5 %project.4.refs_2_ = f32[512,512]{1,0:T(8,128)} custom-call(s32[2]{0:T(128)} %pad_add_fusion.here_ref.refs_0_, s32[24]{0:T(128)} %constant.52.clone.refs_1_, bf16[2,2,256,128]{3,2,1,0:T(8,128)(2,1)} %copy-done.20, bf16[2,2,256,128]{3,2,1,0:T(8,128)(2,1)} %copy-done.21, bf16[8,128,512]{2,1,0:T(8,128)(2,1)} %bitcast.11, bf16[8,128,512]{2,1,0:T(8,128)(2,1)} %copy-done.3, ...), custom_call_target="tpu_custom_call" | custom-call | tf_op jit(solution)/shard_map/project/pallas_call | solution.py:181
  90.4 2.7 %collective-permute-done.22.refs_10_ = bf16[2,2,256,128]{3,2,1,0:T(8,128)(2,1)} collective-permute-done((bf16[2,2,256,128]{3,2,1,0:T(8,128)(2,1)S(1)}, bf16[2,2,256,128]{3,2,1,0:T(8,128)(2,1)}, u32[]{:S(2)}, u32[]{:S(2)}) %collective-permute-start.22) | collective-permute-done | bytes 262176 | tf_op jit(solution)/shard_map/ppermute | solution.py:255
  95.2 4.2 %project.5.refs_2_ = f32[512,512]{1,0:T(8,128)} custom-call(s32[2]{0:T(128)} %pad_add_fusion.here_ref.refs_0_, s32[16]{0:T(128)} %constant.53.clone.refs_1_, f32[512,512]{1,0:T(8,128)} %project.4.refs_2_, bf16[2,2,256,128]{3,2,1,0:T(8,128)(2,1)} %copy-done.26, bf16[2,2,256,128]{3,2,1,0:T(8,128)(2,1)} %collective-permute-done.21.refs_4_, ...), custom_call_target="tpu_custom_call" | custom-call | tf_op jit(solution)/shard_map/project/pallas_call | solution.py:181
  101.0 2.8 %collective-permute-done.24.refs_10_ = bf16[2,2,256,128]{3,2,1,0:T(8,128)(2,1)} collective-permute-done((bf16[2,2,256,128]{3,2,1,0:T(8,128)(2,1)}, bf16[2,2,256,128]{3,2,1,0:T(8,128)(2,1)}, u32[]{:S(2)}, u32[]{:S(2)}) %collective-permute-start.24) | collective-permute-done | bytes 262176 | tf_op jit(solution)/shard_map/ppermute | solution.py:255
  104.0 4.2 %project.6.refs_2_ = f32[512,512]{1,0:T(8,128)} custom-call(s32[2]{0:T(128)} %pad_add_fusion.here_ref.refs_0_, s32[16]{0:T(128)} %constant.54.clone.refs_1_, f32[512,512]{1,0:T(8,128)} %project.5.refs_2_, bf16[2,2,256,128]{3,2,1,0:T(8,128)(2,1)} %collective-permute-done.19.refs_3_, bf16[2,2,256,128]{3,2,1,0:T(8,128)(2,1)} %collective-permute-done.23.refs_4_, ...), custom_call_target="tpu_custom_call" | custom-call | tf_op jit(solution)/shard_map/project/pallas_call | solution.py:181
  109.2 2.5 %collective-permute-done.26.refs_4_ = bf16[2,2,256,128]{3,2,1,0:T(8,128)(2,1)S(1)} collective-permute-done((bf16[2,2,256,128]{3,2,1,0:T(8,128)(2,1)}, bf16[2,2,256,128]{3,2,1,0:T(8,128)(2,1)S(1)}, u32[]{:S(2)}, u32[]{:S(2)}) %collective-permute-start.26) | collective-permute-done | bytes 262176 | tf_op jit(solution)/shard_map/ppermute | solution.py:255
  113.0 2.6 %project.7 = (bf16[256,512]{1,0:T(8,128)(2,1)}, bf16[256,512]{1,0:T(8,128)(2,1)S(1)}) custom-call(s32[2]{0:T(128)S(1)} %copy-done.9, s32[8]{0:T(128)S(1)} %copy-done.10, f32[512,512]{1,0:T(8,128)S(1)} %copy-done.7, bf16[2,2,256,128]{3,2,1,0:T(8,128)(2,1)S(1)} %collective-permute-done.25.refs_3_, ...), custom_call_target="tpu_custom_call" | custom-call | tf_op jit(solution)/shard_map/project/pallas_call | solution.py:181
  119.3 11.7 %collective-permute-done.27 = bf16[256,512]{1,0:T(8,128)(2,1)S(1)} collective-permute-done((bf16[256,512]{1,0:T(8,128)(2,1)}, bf16[256,512]{1,0:T(8,128)(2,1)S(1)}, u32[]{:S(2)}, u32[]{:S(2)}) %collective-permute-start.27) | collective-permute-done | bytes 262176 | tf_op jit(solution)/shard_map/ppermute | solution.py:268
  131.1 3.5 %collective-permute-done.28 = bf16[256,512]{1,0:T(8,128)(2,1)S(1)} collective-permute-done((bf16[256,512]{1,0:T(8,128)(2,1)S(1)}, bf16[256,512]{1,0:T(8,128)(2,1)S(1)}, u32[]{:S(2)}, u32[]{:S(2)}) %collective-permute-start.28) | collective-permute-done | bytes 262176 | tf_op jit(solution)/shard_map/ppermute | solution.py:268
  (103 shorter events, 36.0 us)
Async XLA Ops:
  0.0 47.8 %collective-permute-start.7 = (bf16[8,128,512]{2,1,0:T(8,128)(2,1)}, bf16[8,128,512]{2,1,0:T(8,128)(2,1)S(1)}, u32[]{:S(2)}, u32[]{:S(2)}) collective-permute-start(bf16[8,128,512]{2,1,0:T(8,128)(2,1)} %bitcast.9), channel_id=1, source_target_pairs={{0,1},{1,0},{2,3},{3,2},{4,5},{5,4},{6,7},{7,6},{8,9},{9,8},{10,11... | collective-permute-start | bytes 3145736 | tf_op jit(solution)/shard_map/ppermute | solution.py:229
  0.0 47.8 %collective-permute-start.8 = (bf16[8,128,512]{2,1,0:T(8,128)(2,1)}, bf16[8,128,512]{2,1,0:T(8,128)(2,1)S(1)}, u32[]{:S(2)}, u32[]{:S(2)}) collective-permute-start(bf16[8,128,512]{2,1,0:T(8,128)(2,1)} %bitcast.10), channel_id=1, source_target_pairs={{0,2},{1,3},{2,0},{3,1},{4,6},{5,7},{6,4},{7,5},{8,10},{9,11},{10,... | collective-permute-start | bytes 3145736 | tf_op jit(solution)/shard_map/ppermute | solution.py:229
  6.4 60.3 %collective-permute-start.16 = (bf16[8,128,512]{2,1,0:T(8,128)(2,1)S(1)}, bf16[8,128,512]{2,1,0:T(8,128)(2,1)}, u32[]{:S(2)}, u32[]{:S(2)}) collective-permute-start(bf16[8,128,512]{2,1,0:T(8,128)(2,1)S(1)} %bitcast.18), channel_id=1, source_target_pairs={{0,3},{1,2},{2,1},{3,0},{4,7},{5,6},{6,5},{7,4},{8,11},{9,10},{10,... | collective-permute-start | bytes 3145736 | tf_op jit(solution)/shard_map/ppermute | solution.py:229
  11.8 9.6 %collective-permute-start.2 = (bf16[3,256,128]{2,1,0:T(8,128)(2,1)}, bf16[3,256,128]{2,1,0:T(8,128)(2,1)S(1)}, u32[]{:S(2)}, u32[]{:S(2)}) collective-permute-start(bf16[3,256,128]{2,1,0:T(8,128)(2,1)} %get-tuple-element.41), channel_id=1, source_target_pairs={{0,12},{4,8},{8,4},{12,0},{16,28},{20,24},{24,20},{28,16},{1,13},{... | collective-permute-start | bytes 589832 | tf_op jit(solution)/shard_map/ppermute | solution.py:224
  15.0 17.3 %collective-permute-start.3 = (bf16[3,256,128]{2,1,0:T(8,128)(2,1)}, bf16[3,256,128]{2,1,0:T(8,128)(2,1)S(1)}, u32[]{:S(2)}, u32[]{:S(2)}) collective-permute-start(bf16[3,256,128]{2,1,0:T(8,128)(2,1)} %get-tuple-element.42), channel_id=1, source_target_pairs={{0,16},{4,20},{8,24},{12,28},{16,0},{20,4},{24,8},{28,12},{1,17},{... | collective-permute-start | bytes 589832 | tf_op jit(solution)/shard_map/ppermute | solution.py:224
  22.1 16.3 %collective-permute-start.4 = (bf16[3,256,128]{2,1,0:T(8,128)(2,1)}, bf16[3,256,128]{2,1,0:T(8,128)(2,1)S(1)}, u32[]{:S(2)}, u32[]{:S(2)}) collective-permute-start(bf16[3,256,128]{2,1,0:T(8,128)(2,1)} %get-tuple-element.43), channel_id=1, source_target_pairs={{0,20},{4,16},{8,28},{12,24},{16,4},{20,0},{24,12},{28,8},{1,21},{... | collective-permute-start | bytes 589832 | tf_op jit(solution)/shard_map/ppermute | solution.py:224
  33.0 8.2 %collective-permute-start.5 = (bf16[3,256,128]{2,1,0:T(8,128)(2,1)}, bf16[3,256,128]{2,1,0:T(8,128)(2,1)}, u32[]{:S(2)}, u32[]{:S(2)}) collective-permute-start(bf16[3,256,128]{2,1,0:T(8,128)(2,1)} %get-tuple-element.44), channel_id=1, source_target_pairs={{0,24},{4,28},{8,16},{12,20},{16,8},{20,12},{24,0},{28,4},{1,25},{... | collective-permute-start | bytes 589832 | tf_op jit(solution)/shard_map/ppermute | solution.py:224
  39.1 8.8 %collective-permute-start.6 = (bf16[3,256,128]{2,1,0:T(8,128)(2,1)}, bf16[3,256,128]{2,1,0:T(8,128)(2,1)}, u32[]{:S(2)}, u32[]{:S(2)}) collective-permute-start(bf16[3,256,128]{2,1,0:T(8,128)(2,1)} %get-tuple-element.45), channel_id=1, source_target_pairs={{0,28},{4,24},{8,20},{12,16},{16,12},{20,8},{24,4},{28,0},{1,29},{... | collective-permute-start | bytes 589832 | tf_op jit(solution)/shard_map/ppermute | solution.py:224
  59.5 8.2 %collective-permute-start.15 = (bf16[2,256,128]{2,1,0:T(8,128)(2,1)S(1)}, bf16[2,256,128]{2,1,0:T(8,128)(2,1)S(1)}, u32[]{:S(2)}, u32[]{:S(2)}) collective-permute-start(bf16[2,256,128]{2,1,0:T(8,128)(2,1)S(1)} %get-tuple-element.57), channel_id=1, source_target_pairs={{0,3},{1,2},{2,1},{3,0},{4,7},{5,6},{6,5},{7,4},{8,11},{9,10},{10,... | collective-permute-start | bytes 393224 | tf_op jit(solution)/shard_map/ppermute | solution.py:233
  61.4 11.8 %collective-permute-start.10 = (bf16[2,2,256,128]{3,2,1,0:T(8,128)(2,1)S(1)}, bf16[2,2,256,128]{3,2,1,0:T(8,128)(2,1)S(1)}, u32[]{:S(2)}, u32[]{:S(2)}) collective-permute-start(bf16[2,2,256,128]{3,2,1,0:T(8,128)(2,1)S(1)} %pad_maximum_fusion.refs_2_), channel_id=1, source_target_pairs={{8,16},{16,24},{24,28},{28,20},{20,12},{12,4},{4,0},{0,8},{9,17},{... | collective-permute-start | bytes 786440 | tf_op jit(solution)/shard_map/ppermute | solution.py:255
  66.6 9.5 %collective-permute-start.12 = (bf16[2,2,256,128]{3,2,1,0:T(8,128)(2,1)S(1)}, bf16[2,2,256,128]{3,2,1,0:T(8,128)(2,1)S(1)}, u32[]{:S(2)}, u32[]{:S(2)}) collective-permute-start(bf16[2,2,256,128]{3,2,1,0:T(8,128)(2,1)S(1)} %pad_maximum_fusion.refs_2_), channel_id=1, source_target_pairs={{8,0},{16,8},{24,16},{28,24},{20,28},{12,20},{4,12},{0,4},{9,1},{1... | collective-permute-start | bytes 786440 | tf_op jit(solution)/shard_map/ppermute | solution.py:255
  67.8 14.0 %collective-permute-start.18 = (bf16[2,2,256,128]{3,2,1,0:T(8,128)(2,1)S(1)}, bf16[2,2,256,128]{3,2,1,0:T(8,128)(2,1)S(1)}, u32[]{:S(2)}, u32[]{:S(2)}) collective-permute-start(bf16[2,2,256,128]{3,2,1,0:T(8,128)(2,1)S(1)} %pad_maximum_fusion.1.refs_3_), channel_id=1, source_target_pairs={{8,0},{16,8},{24,16},{28,24},{20,28},{12,20},{4,12},{0,4},{9,1},{1... | collective-permute-start | bytes 786440 | tf_op jit(solution)/shard_map/ppermute | solution.py:255
  69.3 12.5 %collective-permute-start.17 = (bf16[2,2,256,128]{3,2,1,0:T(8,128)(2,1)S(1)}, bf16[2,2,256,128]{3,2,1,0:T(8,128)(2,1)S(1)}, u32[]{:S(2)}, u32[]{:S(2)}) collective-permute-start(bf16[2,2,256,128]{3,2,1,0:T(8,128)(2,1)S(1)} %pad_maximum_fusion.1.refs_3_), channel_id=1, source_target_pairs={{8,16},{16,24},{24,28},{28,20},{20,12},{12,4},{4,0},{0,8},{9,17},{... | collective-permute-start | bytes 786440 | tf_op jit(solution)/shard_map/ppermute | solution.py:255
  73.1 15.2 %collective-permute-start.11 = (bf16[2,2,256,128]{3,2,1,0:T(8,128)(2,1)S(1)}, bf16[2,2,256,128]{3,2,1,0:T(8,128)(2,1)S(1)}, u32[]{:S(2)}, u32[]{:S(2)}) collective-permute-start(bf16[2,2,256,128]{3,2,1,0:T(8,128)(2,1)S(1)} %collective-permute-done.10.refs_8_), channel_id=1, source_target_pairs={{8,16},{16,24},{24,28},{28,20},{20,12},{12,4},{4,0},{0,8},{9,17},{... | collective-permute-start | bytes 786440 | tf_op jit(solution)/shard_map/ppermute | solution.py:255
  76.2 12.2 %collective-permute-start.13 = (bf16[2,2,256,128]{3,2,1,0:T(8,128)(2,1)S(1)}, bf16[2,2,256,128]{3,2,1,0:T(8,128)(2,1)S(1)}, u32[]{:S(2)}, u32[]{:S(2)}) collective-permute-start(bf16[2,2,256,128]{3,2,1,0:T(8,128)(2,1)S(1)} %collective-permute-done.12.refs_14_), channel_id=1, source_target_pairs={{8,0},{16,8},{24,16},{28,24},{20,28},{12,20},{4,12},{0,4},{9,1},{1... | collective-permute-start | bytes 786440 | tf_op jit(solution)/shard_map/ppermute | solution.py:255
  81.8 11.3 %collective-permute-start.22 = (bf16[2,2,256,128]{3,2,1,0:T(8,128)(2,1)S(1)}, bf16[2,2,256,128]{3,2,1,0:T(8,128)(2,1)}, u32[]{:S(2)}, u32[]{:S(2)}) collective-permute-start(bf16[2,2,256,128]{3,2,1,0:T(8,128)(2,1)S(1)} %collective-permute-done.18.refs_15_), channel_id=1, source_target_pairs={{8,0},{16,8},{24,16},{28,24},{20,28},{12,20},{4,12},{0,4},{9,1},{1... | collective-permute-start | bytes 786440 | tf_op jit(solution)/shard_map/ppermute | solution.py:255
  81.8 11.3 %collective-permute-start.21 = (bf16[2,2,256,128]{3,2,1,0:T(8,128)(2,1)S(1)}, bf16[2,2,256,128]{3,2,1,0:T(8,128)(2,1)}, u32[]{:S(2)}, u32[]{:S(2)}) collective-permute-start(bf16[2,2,256,128]{3,2,1,0:T(8,128)(2,1)S(1)} %collective-permute-done.17.refs_9_), channel_id=1, source_target_pairs={{8,16},{16,24},{24,28},{28,20},{20,12},{12,4},{4,0},{0,8},{9,17},{... | collective-permute-start | bytes 786440 | tf_op jit(solution)/shard_map/ppermute | solution.py:255
  88.3 11.1 %collective-permute-start.19 = (bf16[2,2,256,128]{3,2,1,0:T(8,128)(2,1)S(1)}, bf16[2,2,256,128]{3,2,1,0:T(8,128)(2,1)}, u32[]{:S(2)}, u32[]{:S(2)}) collective-permute-start(bf16[2,2,256,128]{3,2,1,0:T(8,128)(2,1)S(1)} %collective-permute-done.11.refs_3_), channel_id=1, source_target_pairs={{8,16},{16,24},{24,28},{28,20},{20,12},{12,4},{4,0},{0,8},{9,17},{... | collective-permute-start | bytes 786440 | tf_op jit(solution)/shard_map/ppermute | solution.py:255
  90.0 9.5 %collective-permute-start.20 = (bf16[2,2,256,128]{3,2,1,0:T(8,128)(2,1)S(1)}, bf16[2,2,256,128]{3,2,1,0:T(8,128)(2,1)S(1)}, u32[]{:S(2)}, u32[]{:S(2)}) collective-permute-start(bf16[2,2,256,128]{3,2,1,0:T(8,128)(2,1)S(1)} %collective-permute-done.13.refs_9_), channel_id=1, source_target_pairs={{8,0},{16,8},{24,16},{28,24},{20,28},{12,20},{4,12},{0,4},{9,1},{1... | collective-permute-start | bytes 786440 | tf_op jit(solution)/shard_map/ppermute | solution.py:255
  93.1 10.7 %collective-permute-start.24 = (bf16[2,2,256,128]{3,2,1,0:T(8,128)(2,1)}, bf16[2,2,256,128]{3,2,1,0:T(8,128)(2,1)}, u32[]{:S(2)}, u32[]{:S(2)}) collective-permute-start(bf16[2,2,256,128]{3,2,1,0:T(8,128)(2,1)} %collective-permute-done.22.refs_10_), channel_id=1, source_target_pairs={{8,0},{16,8},{24,16},{28,24},{20,28},{12,20},{4,12},{0,4},{9,1},{1... | collective-permute-start | bytes 786440 | tf_op jit(solution)/shard_map/ppermute | solution.py:255
  93.1 10.9 %collective-permute-start.23 = (bf16[2,2,256,128]{3,2,1,0:T(8,128)(2,1)}, bf16[2,2,256,128]{3,2,1,0:T(8,128)(2,1)}, u32[]{:S(2)}, u32[]{:S(2)}) collective-permute-start(bf16[2,2,256,128]{3,2,1,0:T(8,128)(2,1)} %collective-permute-done.21.refs_4_), channel_id=1, source_target_pairs={{8,16},{16,24},{24,28},{28,20},{20,12},{12,4},{4,0},{0,8},{9,17},{... | collective-permute-start | bytes 786440 | tf_op jit(solution)/shard_map/ppermute | solution.py:255
  99.4 9.8 %collective-permute-start.25 = (bf16[2,2,256,128]{3,2,1,0:T(8,128)(2,1)}, bf16[2,2,256,128]{3,2,1,0:T(8,128)(2,1)S(1)}, u32[]{:S(2)}, u32[]{:S(2)}) collective-permute-start(bf16[2,2,256,128]{3,2,1,0:T(8,128)(2,1)} %collective-permute-done.19.refs_3_), channel_id=1, source_target_pairs={{8,16},{16,24},{24,28},{28,20},{20,12},{12,4},{4,0},{0,8},{9,17},{... | collective-permute-start | bytes 786440 | tf_op jit(solution)/shard_map/ppermute | solution.py:255
  115.6 15.5 %collective-permute-start.27 = (bf16[256,512]{1,0:T(8,128)(2,1)}, bf16[256,512]{1,0:T(8,128)(2,1)S(1)}, u32[]{:S(2)}, u32[]{:S(2)}) collective-permute-start(bf16[256,512]{1,0:T(8,128)(2,1)} %get-tuple-element.69), channel_id=1, source_target_pairs={{0,0},{1,16},{2,4},{3,20},{4,8},{5,24},{6,12},{7,28},{8,1},{9,17},... | collective-permute-start | bytes 786440 | tf_op jit(solution)/shard_map/ppermute | solution.py:268
  117.6 16.9 %collective-permute-start.28 = (bf16[256,512]{1,0:T(8,128)(2,1)S(1)}, bf16[256,512]{1,0:T(8,128)(2,1)S(1)}, u32[]{:S(2)}, u32[]{:S(2)}) collective-permute-start(bf16[256,512]{1,0:T(8,128)(2,1)S(1)} %get-tuple-element.70), channel_id=1, source_target_pairs={{0,8},{1,24},{2,12},{3,28},{4,0},{5,16},{6,4},{7,20},{8,9},{9,25},... | collective-permute-start | bytes 786440 | tf_op jit(solution)/shard_map/ppermute | solution.py:268
  (34 other events, 239.7 us)

commit v3 on v1

--- a/solution.py
+++ b/solution.py
@@ -52,12 +52,16 @@
 def conv_kernel(places, here_ref, in_ref, skip_ref, fwd_ref, inv_ref, *rest):
     mixes, (xs, gs, ys, mix_ref) = rest[:-4], rest[-4:]
     n, _, block, chans = in_ref.shape
-    for k in range(n):
-        xs[k] = jnp.dot(fwd_ref[:, block:], in_ref[k, 0], preferred_element_type=F32)
-        lag = jnp.dot(fwd_ref[:, block:], in_ref[k, 1], preferred_element_type=F32)
-        if k:
-            lag += jnp.dot(fwd_ref[:, :block], in_ref[k - 1, 1], preferred_element_type=F32)
-        gs[k] = lag
+    empty = jnp.zeros((block, chans), BF16)
+    for k in range(0, n, 2):
+        pair = jnp.concatenate([in_ref[k, 0], in_ref[k + 1, 0]], axis=1)
+        both = jnp.dot(fwd_ref[:, block:], pair, preferred_element_type=F32)
+        xs[k], xs[k + 1] = both[:, :chans], both[:, chans:]
+        pair = jnp.concatenate([in_ref[k, 1], in_ref[k + 1, 1]], axis=1)
+        both = jnp.dot(fwd_ref[:, block:], pair, preferred_element_type=F32)
+        pair = jnp.concatenate([in_ref[k - 1, 1] if k else empty, in_ref[k, 1]], axis=1)
+        both += jnp.dot(fwd_ref[:, :block], pair, preferred_element_type=F32)
+        gs[k], gs[k + 1] = both[:, :chans], both[:, chans:]
 
     step = 8
 
@@ -82,11 +86,13 @@
             ys[i, re, :] = one - two
             ys[i, im, :] = three - (one + two)
 
-    for i in range(n):
-        conv = jnp.dot(inv_ref[...], ys[i].astype(BF16), preferred_element_type=F32)
-        mix = in_ref[i, 2].astype(F32) * (conv + skip_ref[...] * in_ref[i, 0].astype(F32))
-        chunk, place = places[i]
-        mix_ref[place, chunk] = mix.astype(BF16)
+    for k in range(0, n, 2):
+        pair = jnp.concatenate([ys[k].astype(BF16), ys[k + 1].astype(BF16)], axis=1)
+        both = jnp.dot(inv_ref[...], pair, preferred_element_type=F32)
+        for i, conv in ((k, both[:, :chans]), (k + 1, both[:, chans:])):
+            mix = in_ref[i, 2].astype(F32) * (conv + skip_ref[...] * in_ref[i, 0].astype(F32))
+            chunk, place = places[i]
+            mix_ref[place, chunk] = mix.astype(BF16)
     for b, ref in enumerate(mixes):
         ref[...] = mix_ref[lax.bitwise_xor(here_ref[1], b)]
 
@@ -146,7 +152,7 @@
         refs[0][...] = total
 
 
-def project(pieces, owners, total, here, weights, last=False):
+def project(pieces, owners, total, here, weights, last=False, grant=60):
     m, count = len(weights), len(pieces)
     _, chans, columns = weights[0].shape
     block = pieces[0][0].shape[-2]
@@ -176,7 +182,7 @@
             out_specs=[whole(size) for size, _ in outs],
         ),
         out_shape=[jax.ShapeDtypeStruct(*out) for out in outs],
-        compiler_params=pltpu.CompilerParams(vmem_limit_bytes=60 * MIB),
+        compiler_params=pltpu.CompilerParams(vmem_limit_bytes=grant * MIB),
         cost_estimate=pl.CostEstimate(flops=0, bytes_accessed=0, transcendentals=0),
         name="project",
     )(here, jnp.asarray(owners.reshape(-1)), *operands)
@@ -247,8 +253,9 @@
         if s < n // 2:
             arrived.append(([list(piece) for piece in zip(*tips)], [-s, s]))
     pieces, offsets = arrived[-1]
-    sums = project(pieces, owners(*offsets), sums, here, weights)
-    sent = project([[tips[0][0], tips[1][1]]], owners(n // 2), sums, here, weights, last=True)
+    sums = project(pieces, owners(*offsets), sums, here, weights, grant=44)
+    final = [[tips[0][0], tips[1][1]]]
+    sent = project(final, owners(n // 2), sums, here, weights, last=True, grant=44)
 
     found = []
     for e in range(2):

time: 122 us -> 122 us (level)
  Pallas kernels: 23.6 us -> 21.5 us
  local copies, waits for them, and re-layouts: 1.77 us -> 3.34 us
    pallas_call x4, Pallas kernels: 16.3 us -> 13.7 us  [project(): pl.pallas_call(lambda *refs: project_kernel(count, m, last, *refs), grid_...]
    ppermute x14, waiting for transfers between devices: 13 us -> 14.6 us  [per_device(): tips[h][way] = lax.ppermute(tips[h][way], 'ctx', routes[way])]
    unnamed x42 -> x34, local copies, waits for them, and re-layouts: 1.69 us -> 3.27 us
  transfers between devices with their start and end apart: 23 -> 23, of which waited for: 16 -> 16; matrix products, arithmetic and copies ran while one was open for 0% -> 0% of each run, Pallas kernels for 11% -> 9%
where the time goes in v3:
time: 122 us
  waiting for transfers between devices  69.6 us (57%)
  starting transfers between devices  26.1 us (21%)
  Pallas kernels  21.5 us (18%)
  local copies, waits for them, and re-layouts  3.34 us (3%)
    ppermute x1, waiting for transfers between devices, per_device(): far = lax.ppermute(even, 'ch', pairs)  24.1 us
    ppermute x14, waiting for transfers between devices, per_device(): tips[h][way] = lax.ppermute(tips[h][way], 'ctx', routes[way])  14.6 us
    ppermute x2, waiting for transfers between devices, per_device(): found.append(lax.ppermute(sent[e], ('ctx', 'ch'), route))  14.3 us
    ppermute x14, starting transfers between devices, per_device(): tips[h][way] = lax.ppermute(tips[h][way], 'ctx', routes[way])  14.3 us
    pallas_call x4, Pallas kernels, project(): pl.pallas_call(lambda *refs: project_kernel(count, m, last, *refs), grid_...  13.7 us
    all_to_all x1, waiting for transfers between devices, per_device(): packed = lax.all_to_all(packed, 'ctx', 0, 0)  9.62 us
    all_to_all x1, starting transfers between devices, per_device(): packed = lax.all_to_all(packed, 'ctx', 0, 0)  5.97 us
    pallas_call x1, Pallas kernels, convolve(): pl.pallas_call(lambda *refs: conv_kernel(places, *refs), grid_spec=pltpu....  5.01 us
  transfers between devices with their start and end apart: 23, of which 16 were waited for; matrix products, arithmetic and copies ran while one was open for 0% of the time, Pallas kernels for 9%

profile of v3, /device:TPU:2, one launch (start us, length us, event | category | flops | bytes accessed | tf_op | source)
XLA Modules:
  0.0 121.8 jit_solution(12570952251400411665)
XLA Ops:
  0.0 2.8 %pack.1 = bf16[8,3,256,128]{3,2,1,0:T(8,128)(2,1)} custom-call(bf16[256,1024]{1,0:T(8,128)(2,1)} %outer_ref.1, bf16[256,1024]{1,0:T(8,128)(2,1)} %inner_ref.1, bf16[256,1024]{1,0:T(8,128)(2,1)} %values_ref.1, f32[256,1024]{1,0:T(8,128)} %filters_ref.1), custom_call_target="tpu_custom_call" | custom-call | flops 262144 | bytes 4194304 | tf_op jit(solution)/shard_map/pack/pallas_call | solution.py:40
  2.8 6.0 %all-to-all-start = ((bf16[8,3,256,128]{3,2,1,0:T(8,128)(2,1)}), bf16[8,3,256,128]{3,2,1,0:T(8,128)(2,1)}, u32[]{:S(2)}, u32[]{:S(2)}) async-start(bf16[8,3,256,128]{3,2,1,0:T(8,128)(2,1)} %pack.1), calls=%async_computation | async-start | bytes 3145728 | tf_op jit(solution)/shard_map/all_to_all | solution.py:226
  9.4 24.1 %collective-permute-done.1.refs_6_.refs_12_.refs_18_.refs_7_.refs_13_ = bf16[8,128,512]{2,1,0:T(8,128)(2,1)S(1)} collective-permute-done((bf16[8,128,512]{2,1,0:T(8,128)(2,1)S(1)}, bf16[8,128,512]{2,1,0:T(8,128)(2,1)S(1)}, u32[]{:S(2)}, u32[]{:S(2)}) %collective-permute-start.1) | collective-permute-done | bytes 1048608 | tf_op jit(solution)/shard_map/ppermute | solution.py:222
  33.6 2.6 %collective-permute-done.2.refs_7_.refs_13_.refs_19_.refs_8_.refs_14_ = bf16[8,128,512]{2,1,0:T(8,128)(2,1)} collective-permute-done((bf16[8,128,512]{2,1,0:T(8,128)(2,1)S(1)}, bf16[8,128,512]{2,1,0:T(8,128)(2,1)}, u32[]{:S(2)}, u32[]{:S(2)}) %collective-permute-start.2) | collective-permute-done | bytes 1048608 | tf_op jit(solution)/shard_map/ppermute | solution.py:223
  36.2 9.6 %all-to-all-done.refs_1_ = bf16[8,3,256,128]{3,2,1,0:T(8,128)(2,1)} async-done(((bf16[8,3,256,128]{3,2,1,0:T(8,128)(2,1)}), bf16[8,3,256,128]{3,2,1,0:T(8,128)(2,1)}, u32[]{:S(2)}, u32[]{:S(2)}) %all-to-all-start) | async-done | bytes 1572896 | tf_op jit(solution)/shard_map/all_to_all | solution.py:226
  47.9 5.0 %convolve.1 = (bf16[2,256,128]{2,1,0:T(8,128)(2,1)S(1)}, bf16[2,256,128]{2,1,0:T(8,128)(2,1)S(1)}, bf16[2,256,128]{2,1,0:T(8,128)(2,1)S(1)}, bf16[2,256,128]{2,1,0:T(8,128)(2,1)S(1)}) custom-call(s32[2]{0:T(128)S(1)} %pad_add_fusion.refs_0_, bf16[8,3,256,128]{3,2,1,0:T(8,128)(2,1)} %all-to-all-done.refs_1_, f32[1,128]{1,0:T(1,128)S(1)} %dynamic-slice_bitcast_fusion.refs_2_, ...), custom_call_target="tpu_custom_call" | custom-call | flops 2147483648 | bytes 4194304 | tf_op jit(solution)/shard_map/convolve/pallas_call | solution.py:108
  55.0 2.0 %collective-permute-start.6 = (bf16[2,2,256,128]{3,2,1,0:T(8,128)(2,1)S(1)}, bf16[2,2,256,128]{3,2,1,0:T(8,128)(2,1)}, u32[]{:S(2)}, u32[]{:S(2)}) collective-permute-start(bf16[2,2,256,128]{3,2,1,0:T(8,128)(2,1)S(1)} %pad_maximum_fusion.refs_2_), channel_id=1, source_target_pairs={{8,0},{16,8},{24,16},{28,24},{20,28},{12,20},{4,12},{0,4},{9,1},{1... | collective-permute-start | bytes 786440 | tf_op jit(solution)/shard_map/ppermute | solution.py:252
  57.0 2.4 %collective-permute-done.8 = bf16[2,256,128]{2,1,0:T(8,128)(2,1)S(1)} collective-permute-done((bf16[2,256,128]{2,1,0:T(8,128)(2,1)S(1)}, bf16[2,256,128]{2,1,0:T(8,128)(2,1)S(1)}, u32[]{:S(2)}, u32[]{:S(2)}) %collective-permute-start.8) | collective-permute-done | bytes 131104 | tf_op jit(solution)/shard_map/ppermute | solution.py:231
  59.3 1.9 %collective-permute-done.9 = bf16[2,256,128]{2,1,0:T(8,128)(2,1)S(1)} collective-permute-done((bf16[2,256,128]{2,1,0:T(8,128)(2,1)S(1)}, bf16[2,256,128]{2,1,0:T(8,128)(2,1)S(1)}, u32[]{:S(2)}, u32[]{:S(2)}) %collective-permute-start.9) | collective-permute-done | bytes 131104 | tf_op jit(solution)/shard_map/ppermute | solution.py:231
  61.3 1.5 %collective-permute-start.11 = (bf16[2,2,256,128]{3,2,1,0:T(8,128)(2,1)S(1)}, bf16[2,2,256,128]{3,2,1,0:T(8,128)(2,1)}, u32[]{:S(2)}, u32[]{:S(2)}) collective-permute-start(bf16[2,2,256,128]{3,2,1,0:T(8,128)(2,1)S(1)} %pad_maximum_fusion.1.refs_3_), channel_id=1, source_target_pairs={{8,0},{16,8},{24,16},{28,24},{20,28},{12,20},{4,12},{0,4},{9,1},{1... | collective-permute-start | bytes 786440 | tf_op jit(solution)/shard_map/ppermute | solution.py:252
  63.8 1.7 %collective-permute-start.7 = (bf16[2,2,256,128]{3,2,1,0:T(8,128)(2,1)}, bf16[2,2,256,128]{3,2,1,0:T(8,128)(2,1)}, u32[]{:S(2)}, u32[]{:S(2)}) collective-permute-start(bf16[2,2,256,128]{3,2,1,0:T(8,128)(2,1)} %collective-permute-done.6.refs_14_), channel_id=1, source_target_pairs={{8,0},{16,8},{24,16},{28,24},{20,28},{12,20},{4,12},{0,4},{9,1},{1... | collective-permute-start | bytes 786440 | tf_op jit(solution)/shard_map/ppermute | solution.py:252
  65.5 5.1 %collective-permute-done.11.refs_15_ = bf16[2,2,256,128]{3,2,1,0:T(8,128)(2,1)} collective-permute-done((bf16[2,2,256,128]{3,2,1,0:T(8,128)(2,1)S(1)}, bf16[2,2,256,128]{3,2,1,0:T(8,128)(2,1)}, u32[]{:S(2)}, u32[]{:S(2)}) %collective-permute-start.11) | collective-permute-done | bytes 262176 | tf_op jit(solution)/shard_map/ppermute | solution.py:252
  72.7 4.5 %project.4.refs_2_ = f32[512,512]{1,0:T(8,128)} custom-call(s32[2]{0:T(128)} %copy-done.8, s32[24]{0:T(128)} %constant.52.clone.refs_1_, bf16[2,2,256,128]{3,2,1,0:T(8,128)(2,1)} %copy-done.14, bf16[2,2,256,128]{3,2,1,0:T(8,128)(2,1)} %copy-done.15, bf16[8,128,512]{2,1,0:T(8,128)(2,1)} %bitcast.9, bf16[8,128,512]{2,1,0:T(8,128)(2,1)} %copy-done.5, ...), custom_call_target="tpu_custom_call" | custom-call | tf_op jit(solution)/shard_map/project/pallas_call | solution.py:176
  78.2 1.4 %collective-permute-start.13 = (bf16[2,2,256,128]{3,2,1,0:T(8,128)(2,1)}, bf16[2,2,256,128]{3,2,1,0:T(8,128)(2,1)S(1)}, u32[]{:S(2)}, u32[]{:S(2)}) collective-permute-start(bf16[2,2,256,128]{3,2,1,0:T(8,128)(2,1)} %collective-permute-done.7.refs_9_), channel_id=1, source_target_pairs={{8,0},{16,8},{24,16},{28,24},{20,28},{12,20},{4,12},{0,4},{9,1},{1... | collective-permute-start | bytes 786440 | tf_op jit(solution)/shard_map/ppermute | solution.py:252
  79.6 2.2 %collective-permute-done.15.refs_10_ = bf16[2,2,256,128]{3,2,1,0:T(8,128)(2,1)} collective-permute-done((bf16[2,2,256,128]{3,2,1,0:T(8,128)(2,1)}, bf16[2,2,256,128]{3,2,1,0:T(8,128)(2,1)}, u32[]{:S(2)}, u32[]{:S(2)}) %collective-permute-start.15) | collective-permute-done | bytes 262176 | tf_op jit(solution)/shard_map/ppermute | solution.py:252
  81.9 1.4 %collective-permute-start.17 = (bf16[2,2,256,128]{3,2,1,0:T(8,128)(2,1)}, bf16[2,2,256,128]{3,2,1,0:T(8,128)(2,1)S(1)}, u32[]{:S(2)}, u32[]{:S(2)}) collective-permute-start(bf16[2,2,256,128]{3,2,1,0:T(8,128)(2,1)} %collective-permute-done.15.refs_10_), channel_id=1, source_target_pairs={{8,0},{16,8},{24,16},{28,24},{20,28},{12,20},{4,12},{0,4},{9,1},{1... | collective-permute-start | bytes 786440 | tf_op jit(solution)/shard_map/ppermute | solution.py:252
  83.9 4.3 %project.5.refs_2_ = f32[512,512]{1,0:T(8,128)} custom-call(s32[2]{0:T(128)} %copy-done.8, s32[16]{0:T(128)} %constant.53.clone.refs_1_, f32[512,512]{1,0:T(8,128)} %project.4.refs_2_, bf16[2,2,256,128]{3,2,1,0:T(8,128)(2,1)} %collective-permute-done.5.refs_3_, bf16[2,2,256,128]{3,2,1,0:T(8,128)(2,1)} %collective-permute-done.14.refs_4_, ...), custom_call_target="tpu_custom_call" | custom-call | tf_op jit(solution)/shard_map/project/pallas_call | solution.py:176
  89.3 3.4 %collective-permute-done.17.refs_10_ = bf16[2,2,256,128]{3,2,1,0:T(8,128)(2,1)S(1)} collective-permute-done((bf16[2,2,256,128]{3,2,1,0:T(8,128)(2,1)}, bf16[2,2,256,128]{3,2,1,0:T(8,128)(2,1)S(1)}, u32[]{:S(2)}, u32[]{:S(2)}) %collective-permute-start.17) | collective-permute-done | bytes 262176 | tf_op jit(solution)/shard_map/ppermute | solution.py:252
  95.7 2.3 %project.6.refs_2_ = f32[512,512]{1,0:T(8,128)S(1)} custom-call(s32[2]{0:T(128)S(1)} %copy-done.9, s32[16]{0:T(128)S(1)} %copy-done.11, f32[512,512]{1,0:T(8,128)S(1)} %copy-done.7, bf16[2,2,256,128]{3,2,1,0:T(8,128)(2,1)S(1)} %collective-permute-done.12.refs_3_, bf16[2,2,256,128]{3,2,1,0:T(8,128)(2,1)} %collective-permute-done.16.refs_4_, ...), custom_call_target="tpu_custom_call" | custom-call | tf_op jit(solution)/shard_map/project/pallas_call | solution.py:176
  98.0 1.5 %collective-permute-done.18.refs_3_ = bf16[2,2,256,128]{3,2,1,0:T(8,128)(2,1)S(1)} collective-permute-done((bf16[2,2,256,128]{3,2,1,0:T(8,128)(2,1)S(1)}, bf16[2,2,256,128]{3,2,1,0:T(8,128)(2,1)S(1)}, u32[]{:S(2)}, u32[]{:S(2)}) %collective-permute-start.18) | collective-permute-done | bytes 262176 | tf_op jit(solution)/shard_map/ppermute | solution.py:252
  100.5 2.6 %project.7 = (bf16[256,512]{1,0:T(8,128)(2,1)}, bf16[256,512]{1,0:T(8,128)(2,1)S(1)}) custom-call(s32[2]{0:T(128)S(1)} %copy-done.9, s32[8]{0:T(128)S(1)} %copy-done.10, f32[512,512]{1,0:T(8,128)S(1)} %project.6.refs_2_, bf16[2,2,256,128]{3,2,1,0:T(8,128)(2,1)S(1)} %collective-permute-done.18.refs_3_, ...), custom_call_target="tpu_custom_call" | custom-call | tf_op jit(solution)/shard_map/project/pallas_call | solution.py:176
  103.2 3.3 %collective-permute-start.20 = (bf16[256,512]{1,0:T(8,128)(2,1)}, bf16[256,512]{1,0:T(8,128)(2,1)S(1)}, u32[]{:S(2)}, u32[]{:S(2)}) collective-permute-start(bf16[256,512]{1,0:T(8,128)(2,1)} %get-tuple-element.35), channel_id=1, source_target_pairs={{0,0},{1,16},{2,4},{3,20},{4,8},{5,24},{6,12},{7,28},{8,1},{9,17},... | collective-permute-start | bytes 786440 | tf_op jit(solution)/shard_map/ppermute | solution.py:266
  106.6 12.1 %collective-permute-done.20 = bf16[256,512]{1,0:T(8,128)(2,1)S(1)} collective-permute-done((bf16[256,512]{1,0:T(8,128)(2,1)}, bf16[256,512]{1,0:T(8,128)(2,1)S(1)}, u32[]{:S(2)}, u32[]{:S(2)}) %collective-permute-start.20) | collective-permute-done | bytes 262176 | tf_op jit(solution)/shard_map/ppermute | solution.py:266
  118.6 2.3 %collective-permute-done.21 = bf16[256,512]{1,0:T(8,128)(2,1)S(1)} collective-permute-done((bf16[256,512]{1,0:T(8,128)(2,1)S(1)}, bf16[256,512]{1,0:T(8,128)(2,1)S(1)}, u32[]{:S(2)}, u32[]{:S(2)}) %collective-permute-start.21) | collective-permute-done | bytes 262176 | tf_op jit(solution)/shard_map/ppermute | solution.py:266
  (67 shorter events, 15.7 us)
Async XLA Ops:
  0.0 33.5 %copy-start = (f32[1024]{0:T(1024)S(1)}, f32[1024]{0:T(1024)}, u32[]{:S(2)}) copy-start(f32[1024]{0:T(1024)} %param.16) | copy-start | bytes 12292
  2.8 43.1 %all-to-all-start = ((bf16[8,3,256,128]{3,2,1,0:T(8,128)(2,1)}), bf16[8,3,256,128]{3,2,1,0:T(8,128)(2,1)}, u32[]{:S(2)}, u32[]{:S(2)}) async-start(bf16[8,3,256,128]{3,2,1,0:T(8,128)(2,1)} %pack.1), calls=%async_computation | async-start | bytes 3145728 | tf_op jit(solution)/shard_map/all_to_all | solution.py:226
  8.8 24.7 %collective-permute-start.1 = (bf16[8,128,512]{2,1,0:T(8,128)(2,1)S(1)}, bf16[8,128,512]{2,1,0:T(8,128)(2,1)S(1)}, u32[]{:S(2)}, u32[]{:S(2)}) collective-permute-start(bf16[8,128,512]{2,1,0:T(8,128)(2,1)S(1)} %bitcast.14), channel_id=1, source_target_pairs={{0,2},{1,3},{2,0},{3,1},{4,6},{5,7},{6,4},{7,5},{8,10},{9,11},{10,... | collective-permute-start | bytes 3145736 | tf_op jit(solution)/shard_map/ppermute | solution.py:222
  9.4 24.3 %collective-permute-start = (bf16[8,128,512]{2,1,0:T(8,128)(2,1)S(1)}, bf16[8,128,512]{2,1,0:T(8,128)(2,1)S(1)}, u32[]{:S(2)}, u32[]{:S(2)}) collective-permute-start(bf16[8,128,512]{2,1,0:T(8,128)(2,1)S(1)} %bitcast.15), channel_id=1, source_target_pairs={{0,1},{1,0},{2,3},{3,2},{4,5},{5,4},{6,7},{7,6},{8,9},{9,8},{10,11... | collective-permute-start | bytes 3145736 | tf_op jit(solution)/shard_map/ppermute | solution.py:219
  33.5 2.8 %collective-permute-start.2 = (bf16[8,128,512]{2,1,0:T(8,128)(2,1)S(1)}, bf16[8,128,512]{2,1,0:T(8,128)(2,1)}, u32[]{:S(2)}, u32[]{:S(2)}) collective-permute-start(bf16[8,128,512]{2,1,0:T(8,128)(2,1)S(1)} %collective-permute-done.1.refs_6_.refs_12_.refs_18_.refs_7_.refs_13_), channel_id=1, source_target_pairs={{0,1},{1,0},{2,3},{3,2},{4,5},{5,4},{6,7},{7,6},{8,9},{9,8},{10,11... | collective-permute-start | bytes 3145736 | tf_op jit(solution)/shard_map/ppermute | solution.py:223
  52.9 1.9 %collective-permute-start.3 = (bf16[2,256,128]{2,1,0:T(8,128)(2,1)S(1)}, bf16[2,256,128]{2,1,0:T(8,128)(2,1)S(1)}, u32[]{:S(2)}, u32[]{:S(2)}) collective-permute-start(bf16[2,256,128]{2,1,0:T(8,128)(2,1)S(1)} %get-tuple-element.23), channel_id=1, source_target_pairs={{0,1},{1,0},{2,3},{3,2},{4,5},{5,4},{6,7},{7,6},{8,9},{9,8},{10,11... | collective-permute-start | bytes 393224 | tf_op jit(solution)/shard_map/ppermute | solution.py:231
  53.0 6.4 %collective-permute-start.8 = (bf16[2,256,128]{2,1,0:T(8,128)(2,1)S(1)}, bf16[2,256,128]{2,1,0:T(8,128)(2,1)S(1)}, u32[]{:S(2)}, u32[]{:S(2)}) collective-permute-start(bf16[2,256,128]{2,1,0:T(8,128)(2,1)S(1)} %get-tuple-element.24), channel_id=1, source_target_pairs={{0,2},{1,3},{2,0},{3,1},{4,6},{5,7},{6,4},{7,5},{8,10},{9,11},{10,... | collective-permute-start | bytes 393224 | tf_op jit(solution)/shard_map/ppermute | solution.py:231
  53.6 7.7 %collective-permute-start.9 = (bf16[2,256,128]{2,1,0:T(8,128)(2,1)S(1)}, bf16[2,256,128]{2,1,0:T(8,128)(2,1)S(1)}, u32[]{:S(2)}, u32[]{:S(2)}) collective-permute-start(bf16[2,256,128]{2,1,0:T(8,128)(2,1)S(1)} %get-tuple-element.25), channel_id=1, source_target_pairs={{0,3},{1,2},{2,1},{3,0},{4,7},{5,6},{6,5},{7,4},{8,11},{9,10},{10,... | collective-permute-start | bytes 393224 | tf_op jit(solution)/shard_map/ppermute | solution.py:231
  54.9 8.6 %collective-permute-start.4 = (bf16[2,2,256,128]{3,2,1,0:T(8,128)(2,1)S(1)}, bf16[2,2,256,128]{3,2,1,0:T(8,128)(2,1)S(1)}, u32[]{:S(2)}, u32[]{:S(2)}) collective-permute-start(bf16[2,2,256,128]{3,2,1,0:T(8,128)(2,1)S(1)} %pad_maximum_fusion.refs_2_), channel_id=1, source_target_pairs={{8,16},{16,24},{24,28},{28,20},{20,12},{12,4},{4,0},{0,8},{9,17},{... | collective-permute-start | bytes 786440 | tf_op jit(solution)/shard_map/ppermute | solution.py:252
  55.0 8.8 %collective-permute-start.6 = (bf16[2,2,256,128]{3,2,1,0:T(8,128)(2,1)S(1)}, bf16[2,2,256,128]{3,2,1,0:T(8,128)(2,1)}, u32[]{:S(2)}, u32[]{:S(2)}) collective-permute-start(bf16[2,2,256,128]{3,2,1,0:T(8,128)(2,1)S(1)} %pad_maximum_fusion.refs_2_), channel_id=1, source_target_pairs={{8,0},{16,8},{24,16},{28,24},{20,28},{12,20},{4,12},{0,4},{9,1},{1... | collective-permute-start | bytes 786440 | tf_op jit(solution)/shard_map/ppermute | solution.py:252
  61.3 9.3 %collective-permute-start.11 = (bf16[2,2,256,128]{3,2,1,0:T(8,128)(2,1)S(1)}, bf16[2,2,256,128]{3,2,1,0:T(8,128)(2,1)}, u32[]{:S(2)}, u32[]{:S(2)}) collective-permute-start(bf16[2,2,256,128]{3,2,1,0:T(8,128)(2,1)S(1)} %pad_maximum_fusion.1.refs_3_), channel_id=1, source_target_pairs={{8,0},{16,8},{24,16},{28,24},{20,28},{12,20},{4,12},{0,4},{9,1},{1... | collective-permute-start | bytes 786440 | tf_op jit(solution)/shard_map/ppermute | solution.py:252
  62.8 9.3 %collective-permute-start.10 = (bf16[2,2,256,128]{3,2,1,0:T(8,128)(2,1)S(1)}, bf16[2,2,256,128]{3,2,1,0:T(8,128)(2,1)}, u32[]{:S(2)}, u32[]{:S(2)}) collective-permute-start(bf16[2,2,256,128]{3,2,1,0:T(8,128)(2,1)S(1)} %pad_maximum_fusion.1.refs_3_), channel_id=1, source_target_pairs={{8,16},{16,24},{24,28},{28,20},{20,12},{12,4},{4,0},{0,8},{9,17},{... | collective-permute-start | bytes 786440 | tf_op jit(solution)/shard_map/ppermute | solution.py:252
  63.5 14.1 %collective-permute-start.5 = (bf16[2,2,256,128]{3,2,1,0:T(8,128)(2,1)S(1)}, bf16[2,2,256,128]{3,2,1,0:T(8,128)(2,1)}, u32[]{:S(2)}, u32[]{:S(2)}) collective-permute-start(bf16[2,2,256,128]{3,2,1,0:T(8,128)(2,1)S(1)} %collective-permute-done.4.refs_8_), channel_id=1, source_target_pairs={{8,16},{16,24},{24,28},{28,20},{20,12},{12,4},{4,0},{0,8},{9,17},{... | collective-permute-start | bytes 786440 | tf_op jit(solution)/shard_map/ppermute | solution.py:252
  63.8 13.8 %collective-permute-start.7 = (bf16[2,2,256,128]{3,2,1,0:T(8,128)(2,1)}, bf16[2,2,256,128]{3,2,1,0:T(8,128)(2,1)}, u32[]{:S(2)}, u32[]{:S(2)}) collective-permute-start(bf16[2,2,256,128]{3,2,1,0:T(8,128)(2,1)} %collective-permute-done.6.refs_14_), channel_id=1, source_target_pairs={{8,0},{16,8},{24,16},{28,24},{20,28},{12,20},{4,12},{0,4},{9,1},{1... | collective-permute-start | bytes 786440 | tf_op jit(solution)/shard_map/ppermute | solution.py:252
  70.6 11.2 %collective-permute-start.15 = (bf16[2,2,256,128]{3,2,1,0:T(8,128)(2,1)}, bf16[2,2,256,128]{3,2,1,0:T(8,128)(2,1)}, u32[]{:S(2)}, u32[]{:S(2)}) collective-permute-start(bf16[2,2,256,128]{3,2,1,0:T(8,128)(2,1)} %collective-permute-done.11.refs_15_), channel_id=1, source_target_pairs={{8,0},{16,8},{24,16},{28,24},{20,28},{12,20},{4,12},{0,4},{9,1},{1... | collective-permute-start | bytes 786440 | tf_op jit(solution)/shard_map/ppermute | solution.py:252
  72.0 11.2 %collective-permute-start.14 = (bf16[2,2,256,128]{3,2,1,0:T(8,128)(2,1)}, bf16[2,2,256,128]{3,2,1,0:T(8,128)(2,1)}, u32[]{:S(2)}, u32[]{:S(2)}) collective-permute-start(bf16[2,2,256,128]{3,2,1,0:T(8,128)(2,1)} %collective-permute-done.10.refs_9_), channel_id=1, source_target_pairs={{8,16},{16,24},{24,28},{28,20},{20,12},{12,4},{4,0},{0,8},{9,17},{... | collective-permute-start | bytes 786440 | tf_op jit(solution)/shard_map/ppermute | solution.py:252
  77.6 11.1 %collective-permute-start.12 = (bf16[2,2,256,128]{3,2,1,0:T(8,128)(2,1)}, bf16[2,2,256,128]{3,2,1,0:T(8,128)(2,1)S(1)}, u32[]{:S(2)}, u32[]{:S(2)}) collective-permute-start(bf16[2,2,256,128]{3,2,1,0:T(8,128)(2,1)} %collective-permute-done.5.refs_3_), channel_id=1, source_target_pairs={{8,16},{16,24},{24,28},{28,20},{20,12},{12,4},{4,0},{0,8},{9,17},{... | collective-permute-start | bytes 786440 | tf_op jit(solution)/shard_map/ppermute | solution.py:252
  78.2 10.5 %collective-permute-start.13 = (bf16[2,2,256,128]{3,2,1,0:T(8,128)(2,1)}, bf16[2,2,256,128]{3,2,1,0:T(8,128)(2,1)S(1)}, u32[]{:S(2)}, u32[]{:S(2)}) collective-permute-start(bf16[2,2,256,128]{3,2,1,0:T(8,128)(2,1)} %collective-permute-done.7.refs_9_), channel_id=1, source_target_pairs={{8,0},{16,8},{24,16},{28,24},{20,28},{12,20},{4,12},{0,4},{9,1},{1... | collective-permute-start | bytes 786440 | tf_op jit(solution)/shard_map/ppermute | solution.py:252
  81.9 10.8 %collective-permute-start.17 = (bf16[2,2,256,128]{3,2,1,0:T(8,128)(2,1)}, bf16[2,2,256,128]{3,2,1,0:T(8,128)(2,1)S(1)}, u32[]{:S(2)}, u32[]{:S(2)}) collective-permute-start(bf16[2,2,256,128]{3,2,1,0:T(8,128)(2,1)} %collective-permute-done.15.refs_10_), channel_id=1, source_target_pairs={{8,0},{16,8},{24,16},{28,24},{20,28},{12,20},{4,12},{0,4},{9,1},{1... | collective-permute-start | bytes 786440 | tf_op jit(solution)/shard_map/ppermute | solution.py:252
  83.3 11.2 %collective-permute-start.16 = (bf16[2,2,256,128]{3,2,1,0:T(8,128)(2,1)}, bf16[2,2,256,128]{3,2,1,0:T(8,128)(2,1)}, u32[]{:S(2)}, u32[]{:S(2)}) collective-permute-start(bf16[2,2,256,128]{3,2,1,0:T(8,128)(2,1)} %collective-permute-done.14.refs_4_), channel_id=1, source_target_pairs={{8,16},{16,24},{24,28},{28,20},{20,12},{12,4},{4,0},{0,8},{9,17},{... | collective-permute-start | bytes 786440 | tf_op jit(solution)/shard_map/ppermute | solution.py:252
  88.7 10.8 %collective-permute-start.18 = (bf16[2,2,256,128]{3,2,1,0:T(8,128)(2,1)S(1)}, bf16[2,2,256,128]{3,2,1,0:T(8,128)(2,1)S(1)}, u32[]{:S(2)}, u32[]{:S(2)}) collective-permute-start(bf16[2,2,256,128]{3,2,1,0:T(8,128)(2,1)S(1)} %collective-permute-done.12.refs_3_), channel_id=1, source_target_pairs={{8,16},{16,24},{24,28},{28,20},{20,12},{12,4},{4,0},{0,8},{9,17},{... | collective-permute-start | bytes 786440 | tf_op jit(solution)/shard_map/ppermute | solution.py:252
  92.7 7.8 %collective-permute-start.19 = (bf16[2,2,256,128]{3,2,1,0:T(8,128)(2,1)S(1)}, bf16[2,2,256,128]{3,2,1,0:T(8,128)(2,1)S(1)}, u32[]{:S(2)}, u32[]{:S(2)}) collective-permute-start(bf16[2,2,256,128]{3,2,1,0:T(8,128)(2,1)S(1)} %collective-permute-done.17.refs_10_), channel_id=1, source_target_pairs={{8,0},{16,8},{24,16},{28,24},{20,28},{12,20},{4,12},{0,4},{9,1},{1... | collective-permute-start | bytes 786440 | tf_op jit(solution)/shard_map/ppermute | solution.py:252
  103.2 15.5 %collective-permute-start.20 = (bf16[256,512]{1,0:T(8,128)(2,1)}, bf16[256,512]{1,0:T(8,128)(2,1)S(1)}, u32[]{:S(2)}, u32[]{:S(2)}) collective-permute-start(bf16[256,512]{1,0:T(8,128)(2,1)} %get-tuple-element.35), channel_id=1, source_target_pairs={{0,0},{1,16},{2,4},{3,20},{4,8},{5,24},{6,12},{7,28},{8,1},{9,17},... | collective-permute-start | bytes 786440 | tf_op jit(solution)/shard_map/ppermute | solution.py:266
  106.5 14.4 %collective-permute-start.21 = (bf16[256,512]{1,0:T(8,128)(2,1)S(1)}, bf16[256,512]{1,0:T(8,128)(2,1)S(1)}, u32[]{:S(2)}, u32[]{:S(2)}) collective-permute-start(bf16[256,512]{1,0:T(8,128)(2,1)S(1)} %get-tuple-element.36), channel_id=1, source_target_pairs={{0,8},{1,24},{2,12},{3,28},{4,0},{5,16},{6,4},{7,20},{8,9},{9,25},... | collective-permute-start | bytes 786440 | tf_op jit(solution)/shard_map/ppermute | solution.py:266
  (16 other events, 208.8 us)

commit v4 on v3

--- a/solution.py
+++ b/solution.py
@@ -253,9 +253,9 @@
         if s < n // 2:
             arrived.append(([list(piece) for piece in zip(*tips)], [-s, s]))
     pieces, offsets = arrived[-1]
-    sums = project(pieces, owners(*offsets), sums, here, weights, grant=44)
+    sums = project(pieces, owners(*offsets), sums, here, weights, grant=51)
     final = [[tips[0][0], tips[1][1]]]
-    sent = project(final, owners(n // 2), sums, here, weights, last=True, grant=44)
+    sent = project(final, owners(n // 2), sums, here, weights, last=True, grant=51)
 
     found = []
     for e in range(2):

time: 122 us -> 118 us (0.967)
  local copies, waits for them, and re-layouts: 3.34 us -> 0.3 us
  Pallas kernels: 21.5 us -> 20 us
    unnamed x34 -> x36, local copies, waits for them, and re-layouts: 3.27 us -> 0.22 us
    pallas_call x1, Pallas kernels: 5.01 us -> 3.61 us  [convolve(): pl.pallas_call(lambda *refs: conv_kernel(places, *refs), grid_spec=pltpu....]
  transfers between devices with their start and end apart: 23 -> 23, of which waited for: 16 -> 16; matrix products, arithmetic and copies ran while one was open for 0% -> 0% of each run, Pallas kernels for 9% -> 10%
where the time goes in v4:
time: 118 us; the launch traced here: 117 us
  waiting for transfers between devices  69.7 us (59%)
  starting transfers between devices  26.2 us (22%)
  Pallas kernels  20 us (17%)
    ppermute x1, waiting for transfers between devices, per_device(): far = lax.ppermute(even, 'ch', pairs)  24.2 us
    ppermute x14, waiting for transfers between devices, per_device(): tips[h][way] = lax.ppermute(tips[h][way], 'ctx', routes[way])  15.2 us
    ppermute x14, starting transfers between devices, per_device(): tips[h][way] = lax.ppermute(tips[h][way], 'ctx', routes[way])  14.3 us
    ppermute x2, waiting for transfers between devices, per_device(): found.append(lax.ppermute(sent[e], ('ctx', 'ch'), route))  14 us
    pallas_call x4, Pallas kernels, project(): pl.pallas_call(lambda *refs: project_kernel(count, m, last, *refs), grid_...  13.6 us
    all_to_all x1, waiting for transfers between devices, per_device(): packed = lax.all_to_all(packed, 'ctx', 0, 0)  9.2 us
    all_to_all x1, starting transfers between devices, per_device(): packed = lax.all_to_all(packed, 'ctx', 0, 0)  5.98 us
    ppermute x3, waiting for transfers between devices, per_device(): lax.ppermute(part, 'ch', [(d, d ^ b) for d in range(m)])  4.28 us
  transfers between devices with their start and end apart: 23, of which 16 were waited for; matrix products, arithmetic and copies ran while one was open for 0% of the time, Pallas kernels for 10%

profile of v4, /device:TPU:2, one launch (start us, length us, event | category | flops | bytes accessed | tf_op | source)
XLA Modules:
  0.0 117.4 jit_solution(4235578997447850854)
XLA Ops:
  0.0 2.8 %pack.1 = bf16[8,3,256,128]{3,2,1,0:T(8,128)(2,1)} custom-call(bf16[256,1024]{1,0:T(8,128)(2,1)} %outer_ref.1, bf16[256,1024]{1,0:T(8,128)(2,1)} %inner_ref.1, bf16[256,1024]{1,0:T(8,128)(2,1)} %values_ref.1, f32[256,1024]{1,0:T(8,128)} %filters_ref.1), custom_call_target="tpu_custom_call" | custom-call | flops 262144 | bytes 4194304 | tf_op jit(solution)/shard_map/pack/pallas_call | solution.py:40
  2.8 6.0 %all-to-all-start = ((bf16[8,3,256,128]{3,2,1,0:T(8,128)(2,1)}), bf16[8,3,256,128]{3,2,1,0:T(8,128)(2,1)S(1)}, u32[]{:S(2)}, u32[]{:S(2)}) async-start(bf16[8,3,256,128]{3,2,1,0:T(8,128)(2,1)} %pack.1), calls=%async_computation | async-start | bytes 3145728 | tf_op jit(solution)/shard_map/all_to_all | solution.py:226
  9.4 24.2 %collective-permute-done.1.refs_6_.refs_12_.refs_18_.refs_7_.refs_13_ = bf16[8,128,512]{2,1,0:T(8,128)(2,1)} collective-permute-done((bf16[8,128,512]{2,1,0:T(8,128)(2,1)S(1)}, bf16[8,128,512]{2,1,0:T(8,128)(2,1)}, u32[]{:S(2)}, u32[]{:S(2)}) %collective-permute-start.1) | collective-permute-done | bytes 1048608 | tf_op jit(solution)/shard_map/ppermute | solution.py:222
  33.7 2.8 %collective-permute-done.2.refs_7_.refs_13_.refs_19_.refs_8_.refs_14_ = bf16[8,128,512]{2,1,0:T(8,128)(2,1)} collective-permute-done((bf16[8,128,512]{2,1,0:T(8,128)(2,1)}, bf16[8,128,512]{2,1,0:T(8,128)(2,1)}, u32[]{:S(2)}, u32[]{:S(2)}) %collective-permute-start.2) | collective-permute-done | bytes 1048608 | tf_op jit(solution)/shard_map/ppermute | solution.py:223
  36.5 9.2 %all-to-all-done.refs_1_ = bf16[8,3,256,128]{3,2,1,0:T(8,128)(2,1)S(1)} async-done(((bf16[8,3,256,128]{3,2,1,0:T(8,128)(2,1)}), bf16[8,3,256,128]{3,2,1,0:T(8,128)(2,1)S(1)}, u32[]{:S(2)}, u32[]{:S(2)}) %all-to-all-start) | async-done | bytes 1572896 | tf_op jit(solution)/shard_map/all_to_all | solution.py:226
  45.8 3.6 %convolve.1 = (bf16[2,256,128]{2,1,0:T(8,128)(2,1)S(1)}, bf16[2,256,128]{2,1,0:T(8,128)(2,1)S(1)}, bf16[2,256,128]{2,1,0:T(8,128)(2,1)S(1)}, bf16[2,256,128]{2,1,0:T(8,128)(2,1)S(1)}) custom-call(s32[2]{0:T(128)S(1)} %pad_add_fusion.refs_0_, bf16[8,3,256,128]{3,2,1,0:T(8,128)(2,1)S(1)} %all-to-all-done.refs_1_, ...), custom_call_target="tpu_custom_call" | custom-call | flops 2147483648 | bytes 4194304 | tf_op jit(solution)/shard_map/convolve/pallas_call | solution.py:108
  51.4 2.0 %collective-permute-start.6 = (bf16[2,2,256,128]{3,2,1,0:T(8,128)(2,1)S(1)}, bf16[2,2,256,128]{3,2,1,0:T(8,128)(2,1)S(1)}, u32[]{:S(2)}, u32[]{:S(2)}) collective-permute-start(bf16[2,2,256,128]{3,2,1,0:T(8,128)(2,1)S(1)} %pad_maximum_fusion.refs_2_), channel_id=1, source_target_pairs={{8,0},{16,8},{24,16},{28,24},{20,28},{12,20},{4,12},{0,4},{9,1},{1... | collective-permute-start | bytes 786440 | tf_op jit(solution)/shard_map/ppermute | solution.py:252
  53.4 2.4 %collective-permute-done.8 = bf16[2,256,128]{2,1,0:T(8,128)(2,1)S(1)} collective-permute-done((bf16[2,256,128]{2,1,0:T(8,128)(2,1)S(1)}, bf16[2,256,128]{2,1,0:T(8,128)(2,1)S(1)}, u32[]{:S(2)}, u32[]{:S(2)}) %collective-permute-start.8) | collective-permute-done | bytes 131104 | tf_op jit(solution)/shard_map/ppermute | solution.py:231
  55.8 1.9 %collective-permute-done.9 = bf16[2,256,128]{2,1,0:T(8,128)(2,1)S(1)} collective-permute-done((bf16[2,256,128]{2,1,0:T(8,128)(2,1)S(1)}, bf16[2,256,128]{2,1,0:T(8,128)(2,1)S(1)}, u32[]{:S(2)}, u32[]{:S(2)}) %collective-permute-start.9) | collective-permute-done | bytes 131104 | tf_op jit(solution)/shard_map/ppermute | solution.py:231
  57.8 1.5 %collective-permute-start.11 = (bf16[2,2,256,128]{3,2,1,0:T(8,128)(2,1)S(1)}, bf16[2,2,256,128]{3,2,1,0:T(8,128)(2,1)S(1)}, u32[]{:S(2)}, u32[]{:S(2)}) collective-permute-start(bf16[2,2,256,128]{3,2,1,0:T(8,128)(2,1)S(1)} %pad_maximum_fusion.1.refs_3_), channel_id=1, source_target_pairs={{8,0},{16,8},{24,16},{28,24},{20,28},{12,20},{4,12},{0,4},{9,1},{1... | collective-permute-start | bytes 786440 | tf_op jit(solution)/shard_map/ppermute | solution.py:252
  60.3 1.7 %collective-permute-start.7 = (bf16[2,2,256,128]{3,2,1,0:T(8,128)(2,1)S(1)}, bf16[2,2,256,128]{3,2,1,0:T(8,128)(2,1)S(1)}, u32[]{:S(2)}, u32[]{:S(2)}) collective-permute-start(bf16[2,2,256,128]{3,2,1,0:T(8,128)(2,1)S(1)} %collective-permute-done.6.refs_14_), channel_id=1, source_target_pairs={{8,0},{16,8},{24,16},{28,24},{20,28},{12,20},{4,12},{0,4},{9,1},{1... | collective-permute-start | bytes 786440 | tf_op jit(solution)/shard_map/ppermute | solution.py:252
  62.0 4.9 %collective-permute-done.11.refs_15_ = bf16[2,2,256,128]{3,2,1,0:T(8,128)(2,1)S(1)} collective-permute-done((bf16[2,2,256,128]{3,2,1,0:T(8,128)(2,1)S(1)}, bf16[2,2,256,128]{3,2,1,0:T(8,128)(2,1)S(1)}, u32[]{:S(2)}, u32[]{:S(2)}) %collective-permute-start.11) | collective-permute-done | bytes 262176 | tf_op jit(solution)/shard_map/ppermute | solution.py:252
  69.1 4.5 %project.4.refs_2_ = f32[512,512]{1,0:T(8,128)} custom-call(s32[2]{0:T(128)} %copy-done.1, s32[24]{0:T(128)} %constant.52.clone.refs_1_, bf16[2,2,256,128]{3,2,1,0:T(8,128)(2,1)} %copy-done.8, bf16[2,2,256,128]{3,2,1,0:T(8,128)(2,1)} %copy-done.9, bf16[8,128,512]{2,1,0:T(8,128)(2,1)} %bitcast.10, ...), custom_call_target="tpu_custom_call" | custom-call | tf_op jit(solution)/shard_map/project/pallas_call | solution.py:176
  74.6 1.4 %collective-permute-start.13 = (bf16[2,2,256,128]{3,2,1,0:T(8,128)(2,1)S(1)}, bf16[2,2,256,128]{3,2,1,0:T(8,128)(2,1)S(1)}, u32[]{:S(2)}, u32[]{:S(2)}) collective-permute-start(bf16[2,2,256,128]{3,2,1,0:T(8,128)(2,1)S(1)} %collective-permute-done.7.refs_9_), channel_id=1, source_target_pairs={{8,0},{16,8},{24,16},{28,24},{20,28},{12,20},{4,12},{0,4},{9,1},{1... | collective-permute-start | bytes 786440 | tf_op jit(solution)/shard_map/ppermute | solution.py:252
  76.1 2.1 %collective-permute-done.15.refs_10_ = bf16[2,2,256,128]{3,2,1,0:T(8,128)(2,1)S(1)} collective-permute-done((bf16[2,2,256,128]{3,2,1,0:T(8,128)(2,1)S(1)}, bf16[2,2,256,128]{3,2,1,0:T(8,128)(2,1)S(1)}, u32[]{:S(2)}, u32[]{:S(2)}) %collective-permute-start.15) | collective-permute-done | bytes 262176 | tf_op jit(solution)/shard_map/ppermute | solution.py:252
  78.1 1.4 %collective-permute-start.17 = (bf16[2,2,256,128]{3,2,1,0:T(8,128)(2,1)S(1)}, bf16[2,2,256,128]{3,2,1,0:T(8,128)(2,1)S(1)}, u32[]{:S(2)}, u32[]{:S(2)}) collective-permute-start(bf16[2,2,256,128]{3,2,1,0:T(8,128)(2,1)S(1)} %collective-permute-done.15.refs_10_), channel_id=1, source_target_pairs={{8,0},{16,8},{24,16},{28,24},{20,28},{12,20},{4,12},{0,4},{9,1},{1... | collective-permute-start | bytes 786440 | tf_op jit(solution)/shard_map/ppermute | solution.py:252
  80.3 4.2 %project.5.refs_2_ = f32[512,512]{1,0:T(8,128)} custom-call(s32[2]{0:T(128)} %copy-done.1, s32[16]{0:T(128)} %constant.53.clone.refs_1_, f32[512,512]{1,0:T(8,128)} %project.4.refs_2_, bf16[2,2,256,128]{3,2,1,0:T(8,128)(2,1)} %copy-done.14, bf16[2,2,256,128]{3,2,1,0:T(8,128)(2,1)} %copy-done.15, bf16[8,128,512]{2,1,0:T(8,128)(2,1)} %bitcast.13, ...), custom_call_target="tpu_custom_call" | custom-call | tf_op jit(solution)/shard_map/project/pallas_call | solution.py:176
  85.8 3.2 %collective-permute-done.17.refs_10_ = bf16[2,2,256,128]{3,2,1,0:T(8,128)(2,1)S(1)} collective-permute-done((bf16[2,2,256,128]{3,2,1,0:T(8,128)(2,1)S(1)}, bf16[2,2,256,128]{3,2,1,0:T(8,128)(2,1)S(1)}, u32[]{:S(2)}, u32[]{:S(2)}) %collective-permute-start.17) | collective-permute-done | bytes 262176 | tf_op jit(solution)/shard_map/ppermute | solution.py:252
  90.8 2.9 %project.6.refs_2_ = f32[512,512]{1,0:T(8,128)S(1)} custom-call(s32[2]{0:T(128)S(1)} %copy-done.2, s32[16]{0:T(128)S(1)} %copy-done.4, f32[512,512]{1,0:T(8,128)} %project.5.refs_2_, bf16[2,2,256,128]{3,2,1,0:T(8,128)(2,1)S(1)} %collective-permute-done.12.refs_3_, bf16[2,2,256,128]{3,2,1,0:T(8,128)(2,1)S(1)} %collective-permute-done.16.refs_4_, ...), custom_call_target="tpu_custom_call" | custom-call | tf_op jit(solution)/shard_map/project/pallas_call | solution.py:176
  93.7 2.1 %collective-permute-done.18.refs_3_ = bf16[2,2,256,128]{3,2,1,0:T(8,128)(2,1)S(1)} collective-permute-done((bf16[2,2,256,128]{3,2,1,0:T(8,128)(2,1)S(1)}, bf16[2,2,256,128]{3,2,1,0:T(8,128)(2,1)S(1)}, u32[]{:S(2)}, u32[]{:S(2)}) %collective-permute-start.18) | collective-permute-done | bytes 262176 | tf_op jit(solution)/shard_map/ppermute | solution.py:252
  97.0 2.1 %project.7 = (bf16[256,512]{1,0:T(8,128)(2,1)S(1)}, bf16[256,512]{1,0:T(8,128)(2,1)S(1)}) custom-call(s32[2]{0:T(128)S(1)} %copy-done.2, s32[8]{0:T(128)S(1)} %copy-done.3, f32[512,512]{1,0:T(8,128)S(1)} %project.6.refs_2_, bf16[2,2,256,128]{3,2,1,0:T(8,128)(2,1)S(1)} %collective-permute-done.18.refs_3_, ...), custom_call_target="tpu_custom_call" | custom-call | tf_op jit(solution)/shard_map/project/pallas_call | solution.py:176
  99.1 3.3 %collective-permute-start.20 = (bf16[256,512]{1,0:T(8,128)(2,1)S(1)}, bf16[256,512]{1,0:T(8,128)(2,1)S(1)}, u32[]{:S(2)}, u32[]{:S(2)}) collective-permute-start(bf16[256,512]{1,0:T(8,128)(2,1)S(1)} %get-tuple-element.35), channel_id=1, source_target_pairs={{0,0},{1,16},{2,4},{3,20},{4,8},{5,24},{6,12},{7,28},{8,1},{9,17},... | collective-permute-start | bytes 786440 | tf_op jit(solution)/shard_map/ppermute | solution.py:266
  102.5 12.0 %collective-permute-done.20 = bf16[256,512]{1,0:T(8,128)(2,1)S(1)} collective-permute-done((bf16[256,512]{1,0:T(8,128)(2,1)S(1)}, bf16[256,512]{1,0:T(8,128)(2,1)S(1)}, u32[]{:S(2)}, u32[]{:S(2)}) %collective-permute-start.20) | collective-permute-done | bytes 262176 | tf_op jit(solution)/shard_map/ppermute | solution.py:266
  114.5 2.0 %collective-permute-done.21 = bf16[256,512]{1,0:T(8,128)(2,1)S(1)} collective-permute-done((bf16[256,512]{1,0:T(8,128)(2,1)S(1)}, bf16[256,512]{1,0:T(8,128)(2,1)S(1)}, u32[]{:S(2)}, u32[]{:S(2)}) %collective-permute-start.21) | collective-permute-done | bytes 262176 | tf_op jit(solution)/shard_map/ppermute | solution.py:266
  (69 shorter events, 13.1 us)
Async XLA Ops:
  2.8 43.0 %copy-start.6 = (bf16[256,512]{1,0:T(8,128)(2,1)S(1)}, bf16[256,512]{1,0:T(8,128)(2,1)}, u32[]{:S(2)}) copy-start(bf16[256,512]{1,0:T(8,128)(2,1)} %constant.51.clone.refs_4_) | copy-start | bytes 786436
  2.8 43.0 %all-to-all-start = ((bf16[8,3,256,128]{3,2,1,0:T(8,128)(2,1)}), bf16[8,3,256,128]{3,2,1,0:T(8,128)(2,1)S(1)}, u32[]{:S(2)}, u32[]{:S(2)}) async-start(bf16[8,3,256,128]{3,2,1,0:T(8,128)(2,1)} %pack.1), calls=%async_computation | async-start | bytes 3145728 | tf_op jit(solution)/shard_map/all_to_all | solution.py:226
  8.8 24.8 %collective-permute-start.1 = (bf16[8,128,512]{2,1,0:T(8,128)(2,1)S(1)}, bf16[8,128,512]{2,1,0:T(8,128)(2,1)}, u32[]{:S(2)}, u32[]{:S(2)}) collective-permute-start(bf16[8,128,512]{2,1,0:T(8,128)(2,1)S(1)} %bitcast.18), channel_id=1, source_target_pairs={{0,2},{1,3},{2,0},{3,1},{4,6},{5,7},{6,4},{7,5},{8,10},{9,11},{10,... | collective-permute-start | bytes 3145736 | tf_op jit(solution)/shard_map/ppermute | solution.py:222
  9.4 24.3 %collective-permute-start = (bf16[8,128,512]{2,1,0:T(8,128)(2,1)S(1)}, bf16[8,128,512]{2,1,0:T(8,128)(2,1)}, u32[]{:S(2)}, u32[]{:S(2)}) collective-permute-start(bf16[8,128,512]{2,1,0:T(8,128)(2,1)S(1)} %bitcast.19), channel_id=1, source_target_pairs={{0,1},{1,0},{2,3},{3,2},{4,5},{5,4},{6,7},{7,6},{8,9},{9,8},{10,11... | collective-permute-start | bytes 3145736 | tf_op jit(solution)/shard_map/ppermute | solution.py:219
  33.5 3.0 %collective-permute-start.2 = (bf16[8,128,512]{2,1,0:T(8,128)(2,1)}, bf16[8,128,512]{2,1,0:T(8,128)(2,1)}, u32[]{:S(2)}, u32[]{:S(2)}) collective-permute-start(bf16[8,128,512]{2,1,0:T(8,128)(2,1)} %collective-permute-done.1.refs_6_.refs_12_.refs_18_.refs_7_.refs_13_), channel_id=1, source_target_pairs={{0,1},{1,0},{2,3},{3,2},{4,5},{5,4},{6,7},{7,6},{8,9},{9,8},{10,11... | collective-permute-start | bytes 3145736 | tf_op jit(solution)/shard_map/ppermute | solution.py:223
  49.4 1.9 %collective-permute-start.3 = (bf16[2,256,128]{2,1,0:T(8,128)(2,1)S(1)}, bf16[2,256,128]{2,1,0:T(8,128)(2,1)S(1)}, u32[]{:S(2)}, u32[]{:S(2)}) collective-permute-start(bf16[2,256,128]{2,1,0:T(8,128)(2,1)S(1)} %get-tuple-element.23), channel_id=1, source_target_pairs={{0,1},{1,0},{2,3},{3,2},{4,5},{5,4},{6,7},{7,6},{8,9},{9,8},{10,11... | collective-permute-start | bytes 393224 | tf_op jit(solution)/shard_map/ppermute | solution.py:231
  49.5 6.4 %collective-permute-start.8 = (bf16[2,256,128]{2,1,0:T(8,128)(2,1)S(1)}, bf16[2,256,128]{2,1,0:T(8,128)(2,1)S(1)}, u32[]{:S(2)}, u32[]{:S(2)}) collective-permute-start(bf16[2,256,128]{2,1,0:T(8,128)(2,1)S(1)} %get-tuple-element.24), channel_id=1, source_target_pairs={{0,2},{1,3},{2,0},{3,1},{4,6},{5,7},{6,4},{7,5},{8,10},{9,11},{10,... | collective-permute-start | bytes 393224 | tf_op jit(solution)/shard_map/ppermute | solution.py:231
  50.1 7.7 %collective-permute-start.9 = (bf16[2,256,128]{2,1,0:T(8,128)(2,1)S(1)}, bf16[2,256,128]{2,1,0:T(8,128)(2,1)S(1)}, u32[]{:S(2)}, u32[]{:S(2)}) collective-permute-start(bf16[2,256,128]{2,1,0:T(8,128)(2,1)S(1)} %get-tuple-element.25), channel_id=1, source_target_pairs={{0,3},{1,2},{2,1},{3,0},{4,7},{5,6},{6,5},{7,4},{8,11},{9,10},{10,... | collective-permute-start | bytes 393224 | tf_op jit(solution)/shard_map/ppermute | solution.py:231
  51.4 8.6 %collective-permute-start.4 = (bf16[2,2,256,128]{3,2,1,0:T(8,128)(2,1)S(1)}, bf16[2,2,256,128]{3,2,1,0:T(8,128)(2,1)S(1)}, u32[]{:S(2)}, u32[]{:S(2)}) collective-permute-start(bf16[2,2,256,128]{3,2,1,0:T(8,128)(2,1)S(1)} %pad_maximum_fusion.refs_2_), channel_id=1, source_target_pairs={{8,16},{16,24},{24,28},{28,20},{20,12},{12,4},{4,0},{0,8},{9,17},{... | collective-permute-start | bytes 786440 | tf_op jit(solution)/shard_map/ppermute | solution.py:252
  51.4 8.8 %collective-permute-start.6 = (bf16[2,2,256,128]{3,2,1,0:T(8,128)(2,1)S(1)}, bf16[2,2,256,128]{3,2,1,0:T(8,128)(2,1)S(1)}, u32[]{:S(2)}, u32[]{:S(2)}) collective-permute-start(bf16[2,2,256,128]{3,2,1,0:T(8,128)(2,1)S(1)} %pad_maximum_fusion.refs_2_), channel_id=1, source_target_pairs={{8,0},{16,8},{24,16},{28,24},{20,28},{12,20},{4,12},{0,4},{9,1},{1... | collective-permute-start | bytes 786440 | tf_op jit(solution)/shard_map/ppermute | solution.py:252
  57.8 9.1 %collective-permute-start.11 = (bf16[2,2,256,128]{3,2,1,0:T(8,128)(2,1)S(1)}, bf16[2,2,256,128]{3,2,1,0:T(8,128)(2,1)S(1)}, u32[]{:S(2)}, u32[]{:S(2)}) collective-permute-start(bf16[2,2,256,128]{3,2,1,0:T(8,128)(2,1)S(1)} %pad_maximum_fusion.1.refs_3_), channel_id=1, source_target_pairs={{8,0},{16,8},{24,16},{28,24},{20,28},{12,20},{4,12},{0,4},{9,1},{1... | collective-permute-start | bytes 786440 | tf_op jit(solution)/shard_map/ppermute | solution.py:252
  59.2 9.1 %collective-permute-start.10 = (bf16[2,2,256,128]{3,2,1,0:T(8,128)(2,1)S(1)}, bf16[2,2,256,128]{3,2,1,0:T(8,128)(2,1)S(1)}, u32[]{:S(2)}, u32[]{:S(2)}) collective-permute-start(bf16[2,2,256,128]{3,2,1,0:T(8,128)(2,1)S(1)} %pad_maximum_fusion.1.refs_3_), channel_id=1, source_target_pairs={{8,16},{16,24},{24,28},{28,20},{20,12},{12,4},{4,0},{0,8},{9,17},{... | collective-permute-start | bytes 786440 | tf_op jit(solution)/shard_map/ppermute | solution.py:252
  60.0 14.0 %collective-permute-start.5 = (bf16[2,2,256,128]{3,2,1,0:T(8,128)(2,1)S(1)}, bf16[2,2,256,128]{3,2,1,0:T(8,128)(2,1)S(1)}, u32[]{:S(2)}, u32[]{:S(2)}) collective-permute-start(bf16[2,2,256,128]{3,2,1,0:T(8,128)(2,1)S(1)} %collective-permute-done.4.refs_8_), channel_id=1, source_target_pairs={{8,16},{16,24},{24,28},{28,20},{20,12},{12,4},{4,0},{0,8},{9,17},{... | collective-permute-start | bytes 786440 | tf_op jit(solution)/shard_map/ppermute | solution.py:252
  60.3 13.7 %collective-permute-start.7 = (bf16[2,2,256,128]{3,2,1,0:T(8,128)(2,1)S(1)}, bf16[2,2,256,128]{3,2,1,0:T(8,128)(2,1)S(1)}, u32[]{:S(2)}, u32[]{:S(2)}) collective-permute-start(bf16[2,2,256,128]{3,2,1,0:T(8,128)(2,1)S(1)} %collective-permute-done.6.refs_14_), channel_id=1, source_target_pairs={{8,0},{16,8},{24,16},{28,24},{20,28},{12,20},{4,12},{0,4},{9,1},{1... | collective-permute-start | bytes 786440 | tf_op jit(solution)/shard_map/ppermute | solution.py:252
  66.9 11.2 %collective-permute-start.15 = (bf16[2,2,256,128]{3,2,1,0:T(8,128)(2,1)S(1)}, bf16[2,2,256,128]{3,2,1,0:T(8,128)(2,1)S(1)}, u32[]{:S(2)}, u32[]{:S(2)}) collective-permute-start(bf16[2,2,256,128]{3,2,1,0:T(8,128)(2,1)S(1)} %collective-permute-done.11.refs_15_), channel_id=1, source_target_pairs={{8,0},{16,8},{24,16},{28,24},{20,28},{12,20},{4,12},{0,4},{9,1},{1... | collective-permute-start | bytes 786440 | tf_op jit(solution)/shard_map/ppermute | solution.py:252
  68.4 11.2 %collective-permute-start.14 = (bf16[2,2,256,128]{3,2,1,0:T(8,128)(2,1)S(1)}, bf16[2,2,256,128]{3,2,1,0:T(8,128)(2,1)S(1)}, u32[]{:S(2)}, u32[]{:S(2)}) collective-permute-start(bf16[2,2,256,128]{3,2,1,0:T(8,128)(2,1)S(1)} %collective-permute-done.10.refs_9_), channel_id=1, source_target_pairs={{8,16},{16,24},{24,28},{28,20},{20,12},{12,4},{4,0},{0,8},{9,17},{... | collective-permute-start | bytes 786440 | tf_op jit(solution)/shard_map/ppermute | solution.py:252
  74.0 11.2 %collective-permute-start.12 = (bf16[2,2,256,128]{3,2,1,0:T(8,128)(2,1)S(1)}, bf16[2,2,256,128]{3,2,1,0:T(8,128)(2,1)S(1)}, u32[]{:S(2)}, u32[]{:S(2)}) collective-permute-start(bf16[2,2,256,128]{3,2,1,0:T(8,128)(2,1)S(1)} %collective-permute-done.5.refs_3_), channel_id=1, source_target_pairs={{8,16},{16,24},{24,28},{28,20},{20,12},{12,4},{4,0},{0,8},{9,17},{... | collective-permute-start | bytes 786440 | tf_op jit(solution)/shard_map/ppermute | solution.py:252
  74.6 10.6 %collective-permute-start.13 = (bf16[2,2,256,128]{3,2,1,0:T(8,128)(2,1)S(1)}, bf16[2,2,256,128]{3,2,1,0:T(8,128)(2,1)S(1)}, u32[]{:S(2)}, u32[]{:S(2)}) collective-permute-start(bf16[2,2,256,128]{3,2,1,0:T(8,128)(2,1)S(1)} %collective-permute-done.7.refs_9_), channel_id=1, source_target_pairs={{8,0},{16,8},{24,16},{28,24},{20,28},{12,20},{4,12},{0,4},{9,1},{1... | collective-permute-start | bytes 786440 | tf_op jit(solution)/shard_map/ppermute | solution.py:252
  78.1 10.9 %collective-permute-start.17 = (bf16[2,2,256,128]{3,2,1,0:T(8,128)(2,1)S(1)}, bf16[2,2,256,128]{3,2,1,0:T(8,128)(2,1)S(1)}, u32[]{:S(2)}, u32[]{:S(2)}) collective-permute-start(bf16[2,2,256,128]{3,2,1,0:T(8,128)(2,1)S(1)} %collective-permute-done.15.refs_10_), channel_id=1, source_target_pairs={{8,0},{16,8},{24,16},{28,24},{20,28},{12,20},{4,12},{0,4},{9,1},{1... | collective-permute-start | bytes 786440 | tf_op jit(solution)/shard_map/ppermute | solution.py:252
  79.6 11.2 %collective-permute-start.16 = (bf16[2,2,256,128]{3,2,1,0:T(8,128)(2,1)S(1)}, bf16[2,2,256,128]{3,2,1,0:T(8,128)(2,1)S(1)}, u32[]{:S(2)}, u32[]{:S(2)}) collective-permute-start(bf16[2,2,256,128]{3,2,1,0:T(8,128)(2,1)S(1)} %collective-permute-done.14.refs_4_), channel_id=1, source_target_pairs={{8,16},{16,24},{24,28},{28,20},{20,12},{12,4},{4,0},{0,8},{9,17},{... | collective-permute-start | bytes 786440 | tf_op jit(solution)/shard_map/ppermute | solution.py:252
  85.2 10.6 %collective-permute-start.18 = (bf16[2,2,256,128]{3,2,1,0:T(8,128)(2,1)S(1)}, bf16[2,2,256,128]{3,2,1,0:T(8,128)(2,1)S(1)}, u32[]{:S(2)}, u32[]{:S(2)}) collective-permute-start(bf16[2,2,256,128]{3,2,1,0:T(8,128)(2,1)S(1)} %collective-permute-done.12.refs_3_), channel_id=1, source_target_pairs={{8,16},{16,24},{24,28},{28,20},{20,12},{12,4},{4,0},{0,8},{9,17},{... | collective-permute-start | bytes 786440 | tf_op jit(solution)/shard_map/ppermute | solution.py:252
  89.1 7.9 %collective-permute-start.19 = (bf16[2,2,256,128]{3,2,1,0:T(8,128)(2,1)S(1)}, bf16[2,2,256,128]{3,2,1,0:T(8,128)(2,1)S(1)}, u32[]{:S(2)}, u32[]{:S(2)}) collective-permute-start(bf16[2,2,256,128]{3,2,1,0:T(8,128)(2,1)S(1)} %collective-permute-done.17.refs_10_), channel_id=1, source_target_pairs={{8,0},{16,8},{24,16},{28,24},{20,28},{12,20},{4,12},{0,4},{9,1},{1... | collective-permute-start | bytes 786440 | tf_op jit(solution)/shard_map/ppermute | solution.py:252
  99.1 15.4 %collective-permute-start.20 = (bf16[256,512]{1,0:T(8,128)(2,1)S(1)}, bf16[256,512]{1,0:T(8,128)(2,1)S(1)}, u32[]{:S(2)}, u32[]{:S(2)}) collective-permute-start(bf16[256,512]{1,0:T(8,128)(2,1)S(1)} %get-tuple-element.35), channel_id=1, source_target_pairs={{0,0},{1,16},{2,4},{3,20},{4,8},{5,24},{6,12},{7,28},{8,1},{9,17},... | collective-permute-start | bytes 786440 | tf_op jit(solution)/shard_map/ppermute | solution.py:266
  102.4 14.1 %collective-permute-start.21 = (bf16[256,512]{1,0:T(8,128)(2,1)S(1)}, bf16[256,512]{1,0:T(8,128)(2,1)S(1)}, u32[]{:S(2)}, u32[]{:S(2)}) collective-permute-start(bf16[256,512]{1,0:T(8,128)(2,1)S(1)} %get-tuple-element.36), channel_id=1, source_target_pairs={{0,8},{1,24},{2,12},{3,28},{4,0},{5,16},{6,4},{7,20},{8,9},{9,25},... | collective-permute-start | bytes 786440 | tf_op jit(solution)/shard_map/ppermute | solution.py:266
  (17 other events, 209.9 us)

commit v5 on v4

--- a/solution.py
+++ b/solution.py
@@ -102,16 +102,14 @@
     m = n // 2
     forward, inverse = tables(block)
 
-    def whole(*shape):
-        return pl.BlockSpec(shape, lambda t, here: (0,) * len(shape))
-
+    held = pl.BlockSpec(memory_space=pltpu.VMEM)
     return pl.pallas_call(
         lambda *refs: conv_kernel(places, *refs),
         grid_spec=pltpu.PrefetchScalarGridSpec(
             num_scalar_prefetch=1,
             grid=(1,),
-            in_specs=[whole(*a.shape) for a in (packed, skip, forward, inverse)],
-            out_specs=[whole(2, block, chans)] * m,
+            in_specs=[held] * 4,
+            out_specs=[held] * m,
             scratch_shapes=[pltpu.VMEM((n, 2 * block, chans), F32)] * 3
             + [pltpu.VMEM((m, 2, block, chans), BF16)],
         ),
@@ -159,6 +157,8 @@
     operands, specs = [], []
 
     def whole(shape):
+        if last:
+            return pl.BlockSpec(memory_space=pltpu.VMEM)
         return pl.BlockSpec(shape, lambda t, *_: (0,) * len(shape))
 
     if total is not None:

time: 118 us -> 118 us (level)
  no operation moved by 1% of the time
where the time goes in v5:
time: 118 us; the launch traced here: 117 us
  waiting for transfers between devices  69.7 us (59%)
  starting transfers between devices  26.2 us (22%)
  Pallas kernels  20 us (17%)
    ppermute x1, waiting for transfers between devices, per_device(): far = lax.ppermute(even, 'ch', pairs)  24.2 us
    ppermute x14, waiting for transfers between devices, per_device(): tips[h][way] = lax.ppermute(tips[h][way], 'ctx', routes[way])  15.2 us
    ppermute x14, starting transfers between devices, per_device(): tips[h][way] = lax.ppermute(tips[h][way], 'ctx', routes[way])  14.3 us
    ppermute x2, waiting for transfers between devices, per_device(): found.append(lax.ppermute(sent[e], ('ctx', 'ch'), route))  14 us
    pallas_call x4, Pallas kernels, project(): pl.pallas_call(lambda *refs: project_kernel(count, m, last, *refs), grid_...  13.6 us
    all_to_all x1, waiting for transfers between devices, per_device(): packed = lax.all_to_all(packed, 'ctx', 0, 0)  9.2 us
    all_to_all x1, starting transfers between devices, per_device(): packed = lax.all_to_all(packed, 'ctx', 0, 0)  5.98 us
    ppermute x3, waiting for transfers between devices, per_device(): lax.ppermute(part, 'ch', [(d, d ^ b) for d in range(m)])  4.28 us
  transfers between devices with their start and end apart: 23, of which 16 were waited for; matrix products, arithmetic and copies ran while one was open for 0% of the time, Pallas kernels for 10%

profile of v5, /device:TPU:2, one launch (start us, length us, event | category | flops | bytes accessed | tf_op | source)
XLA Modules:
  0.0 117.4 jit_solution(4235578997447850854)
XLA Ops:
  0.0 2.8 %pack.1 = bf16[8,3,256,128]{3,2,1,0:T(8,128)(2,1)} custom-call(bf16[256,1024]{1,0:T(8,128)(2,1)} %outer_ref.1, bf16[256,1024]{1,0:T(8,128)(2,1)} %inner_ref.1, bf16[256,1024]{1,0:T(8,128)(2,1)} %values_ref.1, f32[256,1024]{1,0:T(8,128)} %filters_ref.1), custom_call_target="tpu_custom_call" | custom-call | flops 262144 | bytes 4194304 | tf_op jit(solution)/shard_map/pack/pallas_call | solution.py:40
  2.8 6.0 %all-to-all-start = ((bf16[8,3,256,128]{3,2,1,0:T(8,128)(2,1)}), bf16[8,3,256,128]{3,2,1,0:T(8,128)(2,1)S(1)}, u32[]{:S(2)}, u32[]{:S(2)}) async-start(bf16[8,3,256,128]{3,2,1,0:T(8,128)(2,1)} %pack.1), calls=%async_computation | async-start | bytes 3145728 | tf_op jit(solution)/shard_map/all_to_all | solution.py:226
  9.4 24.2 %collective-permute-done.1.refs_6_.refs_12_.refs_18_.refs_7_.refs_13_ = bf16[8,128,512]{2,1,0:T(8,128)(2,1)} collective-permute-done((bf16[8,128,512]{2,1,0:T(8,128)(2,1)S(1)}, bf16[8,128,512]{2,1,0:T(8,128)(2,1)}, u32[]{:S(2)}, u32[]{:S(2)}) %collective-permute-start.1) | collective-permute-done | bytes 1048608 | tf_op jit(solution)/shard_map/ppermute | solution.py:222
  33.7 2.8 %collective-permute-done.2.refs_7_.refs_13_.refs_19_.refs_8_.refs_14_ = bf16[8,128,512]{2,1,0:T(8,128)(2,1)} collective-permute-done((bf16[8,128,512]{2,1,0:T(8,128)(2,1)}, bf16[8,128,512]{2,1,0:T(8,128)(2,1)}, u32[]{:S(2)}, u32[]{:S(2)}) %collective-permute-start.2) | collective-permute-done | bytes 1048608 | tf_op jit(solution)/shard_map/ppermute | solution.py:223
  36.5 9.2 %all-to-all-done.refs_1_ = bf16[8,3,256,128]{3,2,1,0:T(8,128)(2,1)S(1)} async-done(((bf16[8,3,256,128]{3,2,1,0:T(8,128)(2,1)}), bf16[8,3,256,128]{3,2,1,0:T(8,128)(2,1)S(1)}, u32[]{:S(2)}, u32[]{:S(2)}) %all-to-all-start) | async-done | bytes 1572896 | tf_op jit(solution)/shard_map/all_to_all | solution.py:226
  45.8 3.6 %convolve.1 = (bf16[2,256,128]{2,1,0:T(8,128)(2,1)S(1)}, bf16[2,256,128]{2,1,0:T(8,128)(2,1)S(1)}, bf16[2,256,128]{2,1,0:T(8,128)(2,1)S(1)}, bf16[2,256,128]{2,1,0:T(8,128)(2,1)S(1)}) custom-call(s32[2]{0:T(128)S(1)} %pad_add_fusion.refs_0_, bf16[8,3,256,128]{3,2,1,0:T(8,128)(2,1)S(1)} %all-to-all-done.refs_1_, ...), custom_call_target="tpu_custom_call" | custom-call | flops 2147483648 | bytes 4194304 | tf_op jit(solution)/shard_map/convolve/pallas_call | solution.py:106
  51.4 2.0 %collective-permute-start.6 = (bf16[2,2,256,128]{3,2,1,0:T(8,128)(2,1)S(1)}, bf16[2,2,256,128]{3,2,1,0:T(8,128)(2,1)S(1)}, u32[]{:S(2)}, u32[]{:S(2)}) collective-permute-start(bf16[2,2,256,128]{3,2,1,0:T(8,128)(2,1)S(1)} %pad_maximum_fusion.refs_2_), channel_id=1, source_target_pairs={{8,0},{16,8},{24,16},{28,24},{20,28},{12,20},{4,12},{0,4},{9,1},{1... | collective-permute-start | bytes 786440 | tf_op jit(solution)/shard_map/ppermute | solution.py:252
  53.4 2.4 %collective-permute-done.8 = bf16[2,256,128]{2,1,0:T(8,128)(2,1)S(1)} collective-permute-done((bf16[2,256,128]{2,1,0:T(8,128)(2,1)S(1)}, bf16[2,256,128]{2,1,0:T(8,128)(2,1)S(1)}, u32[]{:S(2)}, u32[]{:S(2)}) %collective-permute-start.8) | collective-permute-done | bytes 131104 | tf_op jit(solution)/shard_map/ppermute | solution.py:231
  55.8 1.9 %collective-permute-done.9 = bf16[2,256,128]{2,1,0:T(8,128)(2,1)S(1)} collective-permute-done((bf16[2,256,128]{2,1,0:T(8,128)(2,1)S(1)}, bf16[2,256,128]{2,1,0:T(8,128)(2,1)S(1)}, u32[]{:S(2)}, u32[]{:S(2)}) %collective-permute-start.9) | collective-permute-done | bytes 131104 | tf_op jit(solution)/shard_map/ppermute | solution.py:231
  57.8 1.5 %collective-permute-start.11 = (bf16[2,2,256,128]{3,2,1,0:T(8,128)(2,1)S(1)}, bf16[2,2,256,128]{3,2,1,0:T(8,128)(2,1)S(1)}, u32[]{:S(2)}, u32[]{:S(2)}) collective-permute-start(bf16[2,2,256,128]{3,2,1,0:T(8,128)(2,1)S(1)} %pad_maximum_fusion.1.refs_3_), channel_id=1, source_target_pairs={{8,0},{16,8},{24,16},{28,24},{20,28},{12,20},{4,12},{0,4},{9,1},{1... | collective-permute-start | bytes 786440 | tf_op jit(solution)/shard_map/ppermute | solution.py:252
  60.3 1.7 %collective-permute-start.7 = (bf16[2,2,256,128]{3,2,1,0:T(8,128)(2,1)S(1)}, bf16[2,2,256,128]{3,2,1,0:T(8,128)(2,1)S(1)}, u32[]{:S(2)}, u32[]{:S(2)}) collective-permute-start(bf16[2,2,256,128]{3,2,1,0:T(8,128)(2,1)S(1)} %collective-permute-done.6.refs_14_), channel_id=1, source_target_pairs={{8,0},{16,8},{24,16},{28,24},{20,28},{12,20},{4,12},{0,4},{9,1},{1... | collective-permute-start | bytes 786440 | tf_op jit(solution)/shard_map/ppermute | solution.py:252
  62.0 4.9 %collective-permute-done.11.refs_15_ = bf16[2,2,256,128]{3,2,1,0:T(8,128)(2,1)S(1)} collective-permute-done((bf16[2,2,256,128]{3,2,1,0:T(8,128)(2,1)S(1)}, bf16[2,2,256,128]{3,2,1,0:T(8,128)(2,1)S(1)}, u32[]{:S(2)}, u32[]{:S(2)}) %collective-permute-start.11) | collective-permute-done | bytes 262176 | tf_op jit(solution)/shard_map/ppermute | solution.py:252
  69.1 4.5 %project.4.refs_2_ = f32[512,512]{1,0:T(8,128)} custom-call(s32[2]{0:T(128)} %copy-done.1, s32[24]{0:T(128)} %constant.52.clone.refs_1_, bf16[2,2,256,128]{3,2,1,0:T(8,128)(2,1)} %copy-done.8, bf16[2,2,256,128]{3,2,1,0:T(8,128)(2,1)} %copy-done.9, bf16[8,128,512]{2,1,0:T(8,128)(2,1)} %bitcast.10, ...), custom_call_target="tpu_custom_call" | custom-call | tf_op jit(solution)/shard_map/project/pallas_call | solution.py:176
  74.6 1.4 %collective-permute-start.13 = (bf16[2,2,256,128]{3,2,1,0:T(8,128)(2,1)S(1)}, bf16[2,2,256,128]{3,2,1,0:T(8,128)(2,1)S(1)}, u32[]{:S(2)}, u32[]{:S(2)}) collective-permute-start(bf16[2,2,256,128]{3,2,1,0:T(8,128)(2,1)S(1)} %collective-permute-done.7.refs_9_), channel_id=1, source_target_pairs={{8,0},{16,8},{24,16},{28,24},{20,28},{12,20},{4,12},{0,4},{9,1},{1... | collective-permute-start | bytes 786440 | tf_op jit(solution)/shard_map/ppermute | solution.py:252
  76.1 2.1 %collective-permute-done.15.refs_10_ = bf16[2,2,256,128]{3,2,1,0:T(8,128)(2,1)S(1)} collective-permute-done((bf16[2,2,256,128]{3,2,1,0:T(8,128)(2,1)S(1)}, bf16[2,2,256,128]{3,2,1,0:T(8,128)(2,1)S(1)}, u32[]{:S(2)}, u32[]{:S(2)}) %collective-permute-start.15) | collective-permute-done | bytes 262176 | tf_op jit(solution)/shard_map/ppermute | solution.py:252
  78.1 1.4 %collective-permute-start.17 = (bf16[2,2,256,128]{3,2,1,0:T(8,128)(2,1)S(1)}, bf16[2,2,256,128]{3,2,1,0:T(8,128)(2,1)S(1)}, u32[]{:S(2)}, u32[]{:S(2)}) collective-permute-start(bf16[2,2,256,128]{3,2,1,0:T(8,128)(2,1)S(1)} %collective-permute-done.15.refs_10_), channel_id=1, source_target_pairs={{8,0},{16,8},{24,16},{28,24},{20,28},{12,20},{4,12},{0,4},{9,1},{1... | collective-permute-start | bytes 786440 | tf_op jit(solution)/shard_map/ppermute | solution.py:252
  80.3 4.2 %project.5.refs_2_ = f32[512,512]{1,0:T(8,128)} custom-call(s32[2]{0:T(128)} %copy-done.1, s32[16]{0:T(128)} %constant.53.clone.refs_1_, f32[512,512]{1,0:T(8,128)} %project.4.refs_2_, bf16[2,2,256,128]{3,2,1,0:T(8,128)(2,1)} %copy-done.14, bf16[2,2,256,128]{3,2,1,0:T(8,128)(2,1)} %copy-done.15, bf16[8,128,512]{2,1,0:T(8,128)(2,1)} %bitcast.13, ...), custom_call_target="tpu_custom_call" | custom-call | tf_op jit(solution)/shard_map/project/pallas_call | solution.py:176
  85.8 3.2 %collective-permute-done.17.refs_10_ = bf16[2,2,256,128]{3,2,1,0:T(8,128)(2,1)S(1)} collective-permute-done((bf16[2,2,256,128]{3,2,1,0:T(8,128)(2,1)S(1)}, bf16[2,2,256,128]{3,2,1,0:T(8,128)(2,1)S(1)}, u32[]{:S(2)}, u32[]{:S(2)}) %collective-permute-start.17) | collective-permute-done | bytes 262176 | tf_op jit(solution)/shard_map/ppermute | solution.py:252
  90.8 2.9 %project.6.refs_2_ = f32[512,512]{1,0:T(8,128)S(1)} custom-call(s32[2]{0:T(128)S(1)} %copy-done.2, s32[16]{0:T(128)S(1)} %copy-done.4, f32[512,512]{1,0:T(8,128)} %project.5.refs_2_, bf16[2,2,256,128]{3,2,1,0:T(8,128)(2,1)S(1)} %collective-permute-done.12.refs_3_, bf16[2,2,256,128]{3,2,1,0:T(8,128)(2,1)S(1)} %collective-permute-done.16.refs_4_, ...), custom_call_target="tpu_custom_call" | custom-call | tf_op jit(solution)/shard_map/project/pallas_call | solution.py:176
  93.7 2.1 %collective-permute-done.18.refs_3_ = bf16[2,2,256,128]{3,2,1,0:T(8,128)(2,1)S(1)} collective-permute-done((bf16[2,2,256,128]{3,2,1,0:T(8,128)(2,1)S(1)}, bf16[2,2,256,128]{3,2,1,0:T(8,128)(2,1)S(1)}, u32[]{:S(2)}, u32[]{:S(2)}) %collective-permute-start.18) | collective-permute-done | bytes 262176 | tf_op jit(solution)/shard_map/ppermute | solution.py:252
  97.0 2.1 %project.7 = (bf16[256,512]{1,0:T(8,128)(2,1)S(1)}, bf16[256,512]{1,0:T(8,128)(2,1)S(1)}) custom-call(s32[2]{0:T(128)S(1)} %copy-done.2, s32[8]{0:T(128)S(1)} %copy-done.3, f32[512,512]{1,0:T(8,128)S(1)} %project.6.refs_2_, bf16[2,2,256,128]{3,2,1,0:T(8,128)(2,1)S(1)} %collective-permute-done.18.refs_3_, ...), custom_call_target="tpu_custom_call" | custom-call | tf_op jit(solution)/shard_map/project/pallas_call | solution.py:176
  99.1 3.3 %collective-permute-start.20 = (bf16[256,512]{1,0:T(8,128)(2,1)S(1)}, bf16[256,512]{1,0:T(8,128)(2,1)S(1)}, u32[]{:S(2)}, u32[]{:S(2)}) collective-permute-start(bf16[256,512]{1,0:T(8,128)(2,1)S(1)} %get-tuple-element.35), channel_id=1, source_target_pairs={{0,0},{1,16},{2,4},{3,20},{4,8},{5,24},{6,12},{7,28},{8,1},{9,17},... | collective-permute-start | bytes 786440 | tf_op jit(solution)/shard_map/ppermute | solution.py:266
  102.5 12.0 %collective-permute-done.20 = bf16[256,512]{1,0:T(8,128)(2,1)S(1)} collective-permute-done((bf16[256,512]{1,0:T(8,128)(2,1)S(1)}, bf16[256,512]{1,0:T(8,128)(2,1)S(1)}, u32[]{:S(2)}, u32[]{:S(2)}) %collective-permute-start.20) | collective-permute-done | bytes 262176 | tf_op jit(solution)/shard_map/ppermute | solution.py:266
  114.5 2.0 %collective-permute-done.21 = bf16[256,512]{1,0:T(8,128)(2,1)S(1)} collective-permute-done((bf16[256,512]{1,0:T(8,128)(2,1)S(1)}, bf16[256,512]{1,0:T(8,128)(2,1)S(1)}, u32[]{:S(2)}, u32[]{:S(2)}) %collective-permute-start.21) | collective-permute-done | bytes 262176 | tf_op jit(solution)/shard_map/ppermute | solution.py:266
  (69 shorter events, 13.1 us)
Async XLA Ops:
  2.8 43.0 %copy-start.6 = (bf16[256,512]{1,0:T(8,128)(2,1)S(1)}, bf16[256,512]{1,0:T(8,128)(2,1)}, u32[]{:S(2)}) copy-start(bf16[256,512]{1,0:T(8,128)(2,1)} %constant.51.clone.refs_4_) | copy-start | bytes 786436
  2.8 43.0 %all-to-all-start = ((bf16[8,3,256,128]{3,2,1,0:T(8,128)(2,1)}), bf16[8,3,256,128]{3,2,1,0:T(8,128)(2,1)S(1)}, u32[]{:S(2)}, u32[]{:S(2)}) async-start(bf16[8,3,256,128]{3,2,1,0:T(8,128)(2,1)} %pack.1), calls=%async_computation | async-start | bytes 3145728 | tf_op jit(solution)/shard_map/all_to_all | solution.py:226
  8.8 24.8 %collective-permute-start.1 = (bf16[8,128,512]{2,1,0:T(8,128)(2,1)S(1)}, bf16[8,128,512]{2,1,0:T(8,128)(2,1)}, u32[]{:S(2)}, u32[]{:S(2)}) collective-permute-start(bf16[8,128,512]{2,1,0:T(8,128)(2,1)S(1)} %bitcast.18), channel_id=1, source_target_pairs={{0,2},{1,3},{2,0},{3,1},{4,6},{5,7},{6,4},{7,5},{8,10},{9,11},{10,... | collective-permute-start | bytes 3145736 | tf_op jit(solution)/shard_map/ppermute | solution.py:222
  9.4 24.3 %collective-permute-start = (bf16[8,128,512]{2,1,0:T(8,128)(2,1)S(1)}, bf16[8,128,512]{2,1,0:T(8,128)(2,1)}, u32[]{:S(2)}, u32[]{:S(2)}) collective-permute-start(bf16[8,128,512]{2,1,0:T(8,128)(2,1)S(1)} %bitcast.19), channel_id=1, source_target_pairs={{0,1},{1,0},{2,3},{3,2},{4,5},{5,4},{6,7},{7,6},{8,9},{9,8},{10,11... | collective-permute-start | bytes 3145736 | tf_op jit(solution)/shard_map/ppermute | solution.py:219
  33.5 3.0 %collective-permute-start.2 = (bf16[8,128,512]{2,1,0:T(8,128)(2,1)}, bf16[8,128,512]{2,1,0:T(8,128)(2,1)}, u32[]{:S(2)}, u32[]{:S(2)}) collective-permute-start(bf16[8,128,512]{2,1,0:T(8,128)(2,1)} %collective-permute-done.1.refs_6_.refs_12_.refs_18_.refs_7_.refs_13_), channel_id=1, source_target_pairs={{0,1},{1,0},{2,3},{3,2},{4,5},{5,4},{6,7},{7,6},{8,9},{9,8},{10,11... | collective-permute-start | bytes 3145736 | tf_op jit(solution)/shard_map/ppermute | solution.py:223
  49.4 1.9 %collective-permute-start.3 = (bf16[2,256,128]{2,1,0:T(8,128)(2,1)S(1)}, bf16[2,256,128]{2,1,0:T(8,128)(2,1)S(1)}, u32[]{:S(2)}, u32[]{:S(2)}) collective-permute-start(bf16[2,256,128]{2,1,0:T(8,128)(2,1)S(1)} %get-tuple-element.23), channel_id=1, source_target_pairs={{0,1},{1,0},{2,3},{3,2},{4,5},{5,4},{6,7},{7,6},{8,9},{9,8},{10,11... | collective-permute-start | bytes 393224 | tf_op jit(solution)/shard_map/ppermute | solution.py:231
  49.5 6.4 %collective-permute-start.8 = (bf16[2,256,128]{2,1,0:T(8,128)(2,1)S(1)}, bf16[2,256,128]{2,1,0:T(8,128)(2,1)S(1)}, u32[]{:S(2)}, u32[]{:S(2)}) collective-permute-start(bf16[2,256,128]{2,1,0:T(8,128)(2,1)S(1)} %get-tuple-element.24), channel_id=1, source_target_pairs={{0,2},{1,3},{2,0},{3,1},{4,6},{5,7},{6,4},{7,5},{8,10},{9,11},{10,... | collective-permute-start | bytes 393224 | tf_op jit(solution)/shard_map/ppermute | solution.py:231
  50.1 7.7 %collective-permute-start.9 = (bf16[2,256,128]{2,1,0:T(8,128)(2,1)S(1)}, bf16[2,256,128]{2,1,0:T(8,128)(2,1)S(1)}, u32[]{:S(2)}, u32[]{:S(2)}) collective-permute-start(bf16[2,256,128]{2,1,0:T(8,128)(2,1)S(1)} %get-tuple-element.25), channel_id=1, source_target_pairs={{0,3},{1,2},{2,1},{3,0},{4,7},{5,6},{6,5},{7,4},{8,11},{9,10},{10,... | collective-permute-start | bytes 393224 | tf_op jit(solution)/shard_map/ppermute | solution.py:231
  51.4 8.6 %collective-permute-start.4 = (bf16[2,2,256,128]{3,2,1,0:T(8,128)(2,1)S(1)}, bf16[2,2,256,128]{3,2,1,0:T(8,128)(2,1)S(1)}, u32[]{:S(2)}, u32[]{:S(2)}) collective-permute-start(bf16[2,2,256,128]{3,2,1,0:T(8,128)(2,1)S(1)} %pad_maximum_fusion.refs_2_), channel_id=1, source_target_pairs={{8,16},{16,24},{24,28},{28,20},{20,12},{12,4},{4,0},{0,8},{9,17},{... | collective-permute-start | bytes 786440 | tf_op jit(solution)/shard_map/ppermute | solution.py:252
  51.4 8.8 %collective-permute-start.6 = (bf16[2,2,256,128]{3,2,1,0:T(8,128)(2,1)S(1)}, bf16[2,2,256,128]{3,2,1,0:T(8,128)(2,1)S(1)}, u32[]{:S(2)}, u32[]{:S(2)}) collective-permute-start(bf16[2,2,256,128]{3,2,1,0:T(8,128)(2,1)S(1)} %pad_maximum_fusion.refs_2_), channel_id=1, source_target_pairs={{8,0},{16,8},{24,16},{28,24},{20,28},{12,20},{4,12},{0,4},{9,1},{1... | collective-permute-start | bytes 786440 | tf_op jit(solution)/shard_map/ppermute | solution.py:252
  57.8 9.1 %collective-permute-start.11 = (bf16[2,2,256,128]{3,2,1,0:T(8,128)(2,1)S(1)}, bf16[2,2,256,128]{3,2,1,0:T(8,128)(2,1)S(1)}, u32[]{:S(2)}, u32[]{:S(2)}) collective-permute-start(bf16[2,2,256,128]{3,2,1,0:T(8,128)(2,1)S(1)} %pad_maximum_fusion.1.refs_3_), channel_id=1, source_target_pairs={{8,0},{16,8},{24,16},{28,24},{20,28},{12,20},{4,12},{0,4},{9,1},{1... | collective-permute-start | bytes 786440 | tf_op jit(solution)/shard_map/ppermute | solution.py:252
  59.2 9.1 %collective-permute-start.10 = (bf16[2,2,256,128]{3,2,1,0:T(8,128)(2,1)S(1)}, bf16[2,2,256,128]{3,2,1,0:T(8,128)(2,1)S(1)}, u32[]{:S(2)}, u32[]{:S(2)}) collective-permute-start(bf16[2,2,256,128]{3,2,1,0:T(8,128)(2,1)S(1)} %pad_maximum_fusion.1.refs_3_), channel_id=1, source_target_pairs={{8,16},{16,24},{24,28},{28,20},{20,12},{12,4},{4,0},{0,8},{9,17},{... | collective-permute-start | bytes 786440 | tf_op jit(solution)/shard_map/ppermute | solution.py:252
  60.0 14.0 %collective-permute-start.5 = (bf16[2,2,256,128]{3,2,1,0:T(8,128)(2,1)S(1)}, bf16[2,2,256,128]{3,2,1,0:T(8,128)(2,1)S(1)}, u32[]{:S(2)}, u32[]{:S(2)}) collective-permute-start(bf16[2,2,256,128]{3,2,1,0:T(8,128)(2,1)S(1)} %collective-permute-done.4.refs_8_), channel_id=1, source_target_pairs={{8,16},{16,24},{24,28},{28,20},{20,12},{12,4},{4,0},{0,8},{9,17},{... | collective-permute-start | bytes 786440 | tf_op jit(solution)/shard_map/ppermute | solution.py:252
  60.3 13.7 %collective-permute-start.7 = (bf16[2,2,256,128]{3,2,1,0:T(8,128)(2,1)S(1)}, bf16[2,2,256,128]{3,2,1,0:T(8,128)(2,1)S(1)}, u32[]{:S(2)}, u32[]{:S(2)}) collective-permute-start(bf16[2,2,256,128]{3,2,1,0:T(8,128)(2,1)S(1)} %collective-permute-done.6.refs_14_), channel_id=1, source_target_pairs={{8,0},{16,8},{24,16},{28,24},{20,28},{12,20},{4,12},{0,4},{9,1},{1... | collective-permute-start | bytes 786440 | tf_op jit(solution)/shard_map/ppermute | solution.py:252
  66.9 11.2 %collective-permute-start.15 = (bf16[2,2,256,128]{3,2,1,0:T(8,128)(2,1)S(1)}, bf16[2,2,256,128]{3,2,1,0:T(8,128)(2,1)S(1)}, u32[]{:S(2)}, u32[]{:S(2)}) collective-permute-start(bf16[2,2,256,128]{3,2,1,0:T(8,128)(2,1)S(1)} %collective-permute-done.11.refs_15_), channel_id=1, source_target_pairs={{8,0},{16,8},{24,16},{28,24},{20,28},{12,20},{4,12},{0,4},{9,1},{1... | collective-permute-start | bytes 786440 | tf_op jit(solution)/shard_map/ppermute | solution.py:252
  68.4 11.2 %collective-permute-start.14 = (bf16[2,2,256,128]{3,2,1,0:T(8,128)(2,1)S(1)}, bf16[2,2,256,128]{3,2,1,0:T(8,128)(2,1)S(1)}, u32[]{:S(2)}, u32[]{:S(2)}) collective-permute-start(bf16[2,2,256,128]{3,2,1,0:T(8,128)(2,1)S(1)} %collective-permute-done.10.refs_9_), channel_id=1, source_target_pairs={{8,16},{16,24},{24,28},{28,20},{20,12},{12,4},{4,0},{0,8},{9,17},{... | collective-permute-start | bytes 786440 | tf_op jit(solution)/shard_map/ppermute | solution.py:252
  74.0 11.2 %collective-permute-start.12 = (bf16[2,2,256,128]{3,2,1,0:T(8,128)(2,1)S(1)}, bf16[2,2,256,128]{3,2,1,0:T(8,128)(2,1)S(1)}, u32[]{:S(2)}, u32[]{:S(2)}) collective-permute-start(bf16[2,2,256,128]{3,2,1,0:T(8,128)(2,1)S(1)} %collective-permute-done.5.refs_3_), channel_id=1, source_target_pairs={{8,16},{16,24},{24,28},{28,20},{20,12},{12,4},{4,0},{0,8},{9,17},{... | collective-permute-start | bytes 786440 | tf_op jit(solution)/shard_map/ppermute | solution.py:252
  74.6 10.6 %collective-permute-start.13 = (bf16[2,2,256,128]{3,2,1,0:T(8,128)(2,1)S(1)}, bf16[2,2,256,128]{3,2,1,0:T(8,128)(2,1)S(1)}, u32[]{:S(2)}, u32[]{:S(2)}) collective-permute-start(bf16[2,2,256,128]{3,2,1,0:T(8,128)(2,1)S(1)} %collective-permute-done.7.refs_9_), channel_id=1, source_target_pairs={{8,0},{16,8},{24,16},{28,24},{20,28},{12,20},{4,12},{0,4},{9,1},{1... | collective-permute-start | bytes 786440 | tf_op jit(solution)/shard_map/ppermute | solution.py:252
  78.1 10.9 %collective-permute-start.17 = (bf16[2,2,256,128]{3,2,1,0:T(8,128)(2,1)S(1)}, bf16[2,2,256,128]{3,2,1,0:T(8,128)(2,1)S(1)}, u32[]{:S(2)}, u32[]{:S(2)}) collective-permute-start(bf16[2,2,256,128]{3,2,1,0:T(8,128)(2,1)S(1)} %collective-permute-done.15.refs_10_), channel_id=1, source_target_pairs={{8,0},{16,8},{24,16},{28,24},{20,28},{12,20},{4,12},{0,4},{9,1},{1... | collective-permute-start | bytes 786440 | tf_op jit(solution)/shard_map/ppermute | solution.py:252
  79.6 11.2 %collective-permute-start.16 = (bf16[2,2,256,128]{3,2,1,0:T(8,128)(2,1)S(1)}, bf16[2,2,256,128]{3,2,1,0:T(8,128)(2,1)S(1)}, u32[]{:S(2)}, u32[]{:S(2)}) collective-permute-start(bf16[2,2,256,128]{3,2,1,0:T(8,128)(2,1)S(1)} %collective-permute-done.14.refs_4_), channel_id=1, source_target_pairs={{8,16},{16,24},{24,28},{28,20},{20,12},{12,4},{4,0},{0,8},{9,17},{... | collective-permute-start | bytes 786440 | tf_op jit(solution)/shard_map/ppermute | solution.py:252
  85.2 10.6 %collective-permute-start.18 = (bf16[2,2,256,128]{3,2,1,0:T(8,128)(2,1)S(1)}, bf16[2,2,256,128]{3,2,1,0:T(8,128)(2,1)S(1)}, u32[]{:S(2)}, u32[]{:S(2)}) collective-permute-start(bf16[2,2,256,128]{3,2,1,0:T(8,128)(2,1)S(1)} %collective-permute-done.12.refs_3_), channel_id=1, source_target_pairs={{8,16},{16,24},{24,28},{28,20},{20,12},{12,4},{4,0},{0,8},{9,17},{... | collective-permute-start | bytes 786440 | tf_op jit(solution)/shard_map/ppermute | solution.py:252
  89.1 7.9 %collective-permute-start.19 = (bf16[2,2,256,128]{3,2,1,0:T(8,128)(2,1)S(1)}, bf16[2,2,256,128]{3,2,1,0:T(8,128)(2,1)S(1)}, u32[]{:S(2)}, u32[]{:S(2)}) collective-permute-start(bf16[2,2,256,128]{3,2,1,0:T(8,128)(2,1)S(1)} %collective-permute-done.17.refs_10_), channel_id=1, source_target_pairs={{8,0},{16,8},{24,16},{28,24},{20,28},{12,20},{4,12},{0,4},{9,1},{1... | collective-permute-start | bytes 786440 | tf_op jit(solution)/shard_map/ppermute | solution.py:252
  99.1 15.4 %collective-permute-start.20 = (bf16[256,512]{1,0:T(8,128)(2,1)S(1)}, bf16[256,512]{1,0:T(8,128)(2,1)S(1)}, u32[]{:S(2)}, u32[]{:S(2)}) collective-permute-start(bf16[256,512]{1,0:T(8,128)(2,1)S(1)} %get-tuple-element.35), channel_id=1, source_target_pairs={{0,0},{1,16},{2,4},{3,20},{4,8},{5,24},{6,12},{7,28},{8,1},{9,17},... | collective-permute-start | bytes 786440 | tf_op jit(solution)/shard_map/ppermute | solution.py:266
  102.4 14.1 %collective-permute-start.21 = (bf16[256,512]{1,0:T(8,128)(2,1)S(1)}, bf16[256,512]{1,0:T(8,128)(2,1)S(1)}, u32[]{:S(2)}, u32[]{:S(2)}) collective-permute-start(bf16[256,512]{1,0:T(8,128)(2,1)S(1)} %get-tuple-element.36), channel_id=1, source_target_pairs={{0,8},{1,24},{2,12},{3,28},{4,0},{5,16},{6,4},{7,20},{8,9},{9,25},... | collective-permute-start | bytes 786440 | tf_op jit(solution)/shard_map/ppermute | solution.py:266
  (17 other events, 209.9 us)

commit v6 on v5

--- a/solution.py
+++ b/solution.py
@@ -208,7 +208,7 @@
     here = jnp.stack([j, k]).astype(jnp.int32)
 
     def row_block(h, d):
-        return (h + 2 * (d % 2)) * across + d // 2
+        return 2 * (d % 2 * half + d // 2) + h
 
     places = {row_block(h, d): (h, d) for h in range(2) for d in range(m)}
 
@@ -264,7 +264,7 @@
             for b in range(m):
                 route.append((a * m + b, row_block((a + e) % 2, b) * m + a // 2))
         found.append(lax.ppermute(sent[e], ("ctx", "ch"), route))
-    even = (j // across) % 2 == 0
+    even = j % 2 == 0
     return jnp.where(even, jnp.concatenate(found, axis=1), jnp.concatenate(found[::-1], axis=1))
 
 

time: 118 us -> 123 us (1.042)
  the two profiles are of different devices: /device:TPU:2 before, /device:TPU:1 now
where the time goes in v6:
time: 123 us
  waiting for transfers between devices  67.5 us (55%)
  starting transfers between devices  32.9 us (27%)
  Pallas kernels  20 us (16%)
    ppermute x1, waiting for transfers between devices, per_device(): far = lax.ppermute(even, 'ch', pairs)  21.4 us
    ppermute x14, waiting for transfers between devices, per_device(): tips[h][way] = lax.ppermute(tips[h][way], 'ctx', routes[way])  16.2 us
    ppermute x2, waiting for transfers between devices, per_device(): found.append(lax.ppermute(sent[e], ('ctx', 'ch'), route))  14.7 us
    pallas_call x4, Pallas kernels, project(): pl.pallas_call(lambda *refs: project_kernel(count, m, last, *refs), grid_...  13.6 us
    ppermute x14, starting transfers between devices, per_device(): tips[h][way] = lax.ppermute(tips[h][way], 'ctx', routes[way])  10.4 us
    ppermute x2, starting transfers between devices, per_device(): found.append(lax.ppermute(sent[e], ('ctx', 'ch'), route))  8.01 us
    all_to_all x1, waiting for transfers between devices, per_device(): packed = lax.all_to_all(packed, 'ctx', 0, 0)  7.76 us
    all_to_all x1, starting transfers between devices, per_device(): packed = lax.all_to_all(packed, 'ctx', 0, 0)  6.53 us
  transfers between devices with their start and end apart: 23, of which 13 were waited for; matrix products, arithmetic and copies ran while one was open for 0% of the time, Pallas kernels for 9%

profile of v6, /device:TPU:1, one launch (start us, length us, event | category | flops | bytes accessed | tf_op | source)
XLA Modules:
  0.0 122.5 jit_solution(8762699681689056306)
XLA Ops:
  0.0 2.8 %pack.1 = bf16[8,3,256,128]{3,2,1,0:T(8,128)(2,1)} custom-call(bf16[256,1024]{1,0:T(8,128)(2,1)} %outer_ref.1, bf16[256,1024]{1,0:T(8,128)(2,1)} %inner_ref.1, bf16[256,1024]{1,0:T(8,128)(2,1)} %values_ref.1, f32[256,1024]{1,0:T(8,128)} %filters_ref.1), custom_call_target="tpu_custom_call" | custom-call | flops 262144 | bytes 4194304 | tf_op jit(solution)/shard_map/pack/pallas_call | solution.py:40
  2.8 6.5 %all-to-all-start = ((bf16[8,3,256,128]{3,2,1,0:T(8,128)(2,1)}), bf16[8,3,256,128]{3,2,1,0:T(8,128)(2,1)S(1)}, u32[]{:S(2)}, u32[]{:S(2)}) async-start(bf16[8,3,256,128]{3,2,1,0:T(8,128)(2,1)} %pack.1), calls=%async_computation | async-start | bytes 3145728 | tf_op jit(solution)/shard_map/all_to_all | solution.py:226
  9.3 1.3 %collective-permute-start.1 = (bf16[8,128,512]{2,1,0:T(8,128)(2,1)S(1)}, bf16[8,128,512]{2,1,0:T(8,128)(2,1)}, u32[]{:S(2)}, u32[]{:S(2)}) collective-permute-start(bf16[8,128,512]{2,1,0:T(8,128)(2,1)S(1)} %bitcast.18), channel_id=1, source_target_pairs={{0,2},{1,3},{2,0},{3,1},{4,6},{5,7},{6,4},{7,5},{8,10},{9,11},{10,... | collective-permute-start | bytes 3145736 | tf_op jit(solution)/shard_map/ppermute | solution.py:222
  11.8 21.4 %collective-permute-done.1.refs_6_.refs_12_.refs_18_.refs_7_.refs_13_ = bf16[8,128,512]{2,1,0:T(8,128)(2,1)} collective-permute-done((bf16[8,128,512]{2,1,0:T(8,128)(2,1)S(1)}, bf16[8,128,512]{2,1,0:T(8,128)(2,1)}, u32[]{:S(2)}, u32[]{:S(2)}) %collective-permute-start.1) | collective-permute-done | bytes 1048608 | tf_op jit(solution)/shard_map/ppermute | solution.py:222
  33.2 1.9 %collective-permute-start.2 = (bf16[8,128,512]{2,1,0:T(8,128)(2,1)}, bf16[8,128,512]{2,1,0:T(8,128)(2,1)}, u32[]{:S(2)}, u32[]{:S(2)}) collective-permute-start(bf16[8,128,512]{2,1,0:T(8,128)(2,1)} %collective-permute-done.1.refs_6_.refs_12_.refs_18_.refs_7_.refs_13_), channel_id=1, source_target_pairs={{0,1},{1,0},{2,3},{3,2},{4,5},{5,4},{6,7},{7,6},{8,9},{9,8},{10,11... | collective-permute-start | bytes 3145736 | tf_op jit(solution)/shard_map/ppermute | solution.py:223
  35.2 2.5 %collective-permute-done.2.refs_7_.refs_13_.refs_19_.refs_8_.refs_14_ = bf16[8,128,512]{2,1,0:T(8,128)(2,1)} collective-permute-done((bf16[8,128,512]{2,1,0:T(8,128)(2,1)}, bf16[8,128,512]{2,1,0:T(8,128)(2,1)}, u32[]{:S(2)}, u32[]{:S(2)}) %collective-permute-start.2) | collective-permute-done | bytes 1048608 | tf_op jit(solution)/shard_map/ppermute | solution.py:223
  37.7 7.8 %all-to-all-done.refs_1_ = bf16[8,3,256,128]{3,2,1,0:T(8,128)(2,1)S(1)} async-done(((bf16[8,3,256,128]{3,2,1,0:T(8,128)(2,1)}), bf16[8,3,256,128]{3,2,1,0:T(8,128)(2,1)S(1)}, u32[]{:S(2)}, u32[]{:S(2)}) %all-to-all-start) | async-done | bytes 1572896 | tf_op jit(solution)/shard_map/all_to_all | solution.py:226
  45.4 3.6 %convolve.1 = (bf16[2,256,128]{2,1,0:T(8,128)(2,1)S(1)}, bf16[2,256,128]{2,1,0:T(8,128)(2,1)S(1)}, bf16[2,256,128]{2,1,0:T(8,128)(2,1)S(1)}, bf16[2,256,128]{2,1,0:T(8,128)(2,1)S(1)}) custom-call(s32[2]{0:T(128)S(1)} %pad_add_fusion.refs_0_, bf16[8,3,256,128]{3,2,1,0:T(8,128)(2,1)S(1)} %all-to-all-done.refs_1_, ...), custom_call_target="tpu_custom_call" | custom-call | flops 2147483648 | bytes 4194304 | tf_op jit(solution)/shard_map/convolve/pallas_call | solution.py:106
  49.1 1.9 %collective-permute-start.3 = (bf16[2,256,128]{2,1,0:T(8,128)(2,1)S(1)}, bf16[2,256,128]{2,1,0:T(8,128)(2,1)S(1)}, u32[]{:S(2)}, u32[]{:S(2)}) collective-permute-start(bf16[2,256,128]{2,1,0:T(8,128)(2,1)S(1)} %get-tuple-element.23), channel_id=1, source_target_pairs={{0,1},{1,0},{2,3},{3,2},{4,5},{5,4},{6,7},{7,6},{8,9},{9,8},{10,11... | collective-permute-start | bytes 393224 | tf_op jit(solution)/shard_map/ppermute | solution.py:231
  52.8 1.5 %collective-permute-start.6 = (bf16[2,2,256,128]{3,2,1,0:T(8,128)(2,1)S(1)}, bf16[2,2,256,128]{3,2,1,0:T(8,128)(2,1)S(1)}, u32[]{:S(2)}, u32[]{:S(2)}) collective-permute-start(bf16[2,2,256,128]{3,2,1,0:T(8,128)(2,1)S(1)} %pad_maximum_fusion.refs_2_), channel_id=1, source_target_pairs={{8,0},{16,8},{24,16},{28,24},{20,28},{12,20},{4,12},{0,4},{9,1},{1... | collective-permute-start | bytes 786440 | tf_op jit(solution)/shard_map/ppermute | solution.py:252
  54.2 1.8 %collective-permute-done.8 = bf16[2,256,128]{2,1,0:T(8,128)(2,1)S(1)} collective-permute-done((bf16[2,256,128]{2,1,0:T(8,128)(2,1)S(1)}, bf16[2,256,128]{2,1,0:T(8,128)(2,1)S(1)}, u32[]{:S(2)}, u32[]{:S(2)}) %collective-permute-start.8) | collective-permute-done | bytes 131104 | tf_op jit(solution)/shard_map/ppermute | solution.py:231
  56.0 3.3 %collective-permute-done.9 = bf16[2,256,128]{2,1,0:T(8,128)(2,1)S(1)} collective-permute-done((bf16[2,256,128]{2,1,0:T(8,128)(2,1)S(1)}, bf16[2,256,128]{2,1,0:T(8,128)(2,1)S(1)}, u32[]{:S(2)}, u32[]{:S(2)}) %collective-permute-start.9) | collective-permute-done | bytes 131104 | tf_op jit(solution)/shard_map/ppermute | solution.py:231
  60.9 1.4 %collective-permute-start.7 = (bf16[2,2,256,128]{3,2,1,0:T(8,128)(2,1)S(1)}, bf16[2,2,256,128]{3,2,1,0:T(8,128)(2,1)S(1)}, u32[]{:S(2)}, u32[]{:S(2)}) collective-permute-start(bf16[2,2,256,128]{3,2,1,0:T(8,128)(2,1)S(1)} %collective-permute-done.6.refs_14_), channel_id=1, source_target_pairs={{8,0},{16,8},{24,16},{28,24},{20,28},{12,20},{4,12},{0,4},{9,1},{1... | collective-permute-start | bytes 786440 | tf_op jit(solution)/shard_map/ppermute | solution.py:252
  62.3 5.1 %collective-permute-done.11.refs_15_ = bf16[2,2,256,128]{3,2,1,0:T(8,128)(2,1)S(1)} collective-permute-done((bf16[2,2,256,128]{3,2,1,0:T(8,128)(2,1)S(1)}, bf16[2,2,256,128]{3,2,1,0:T(8,128)(2,1)S(1)}, u32[]{:S(2)}, u32[]{:S(2)}) %collective-permute-start.11) | collective-permute-done | bytes 262176 | tf_op jit(solution)/shard_map/ppermute | solution.py:252
  69.3 4.5 %project.4.refs_2_ = f32[512,512]{1,0:T(8,128)} custom-call(s32[2]{0:T(128)} %copy-done.1, s32[24]{0:T(128)} %constant.41.clone.refs_1_, bf16[2,2,256,128]{3,2,1,0:T(8,128)(2,1)} %copy-done.8, bf16[2,2,256,128]{3,2,1,0:T(8,128)(2,1)} %copy-done.9, bf16[8,128,512]{2,1,0:T(8,128)(2,1)} %bitcast.10, ...), custom_call_target="tpu_custom_call" | custom-call | tf_op jit(solution)/shard_map/project/pallas_call | solution.py:176
  75.4 3.3 %collective-permute-done.15.refs_10_ = bf16[2,2,256,128]{3,2,1,0:T(8,128)(2,1)S(1)} collective-permute-done((bf16[2,2,256,128]{3,2,1,0:T(8,128)(2,1)S(1)}, bf16[2,2,256,128]{3,2,1,0:T(8,128)(2,1)S(1)}, u32[]{:S(2)}, u32[]{:S(2)}) %collective-permute-start.15) | collective-permute-done | bytes 262176 | tf_op jit(solution)/shard_map/ppermute | solution.py:252
  80.5 4.2 %project.5.refs_2_ = f32[512,512]{1,0:T(8,128)} custom-call(s32[2]{0:T(128)} %copy-done.1, s32[16]{0:T(128)} %constant.42.clone.refs_1_, f32[512,512]{1,0:T(8,128)} %project.4.refs_2_, bf16[2,2,256,128]{3,2,1,0:T(8,128)(2,1)} %copy-done.14, bf16[2,2,256,128]{3,2,1,0:T(8,128)(2,1)} %copy-done.15, bf16[8,128,512]{2,1,0:T(8,128)(2,1)} %bitcast.13, ...), custom_call_target="tpu_custom_call" | custom-call | tf_op jit(solution)/shard_map/project/pallas_call | solution.py:176
  85.4 4.3 %collective-permute-done.17.refs_10_ = bf16[2,2,256,128]{3,2,1,0:T(8,128)(2,1)S(1)} collective-permute-done((bf16[2,2,256,128]{3,2,1,0:T(8,128)(2,1)S(1)}, bf16[2,2,256,128]{3,2,1,0:T(8,128)(2,1)S(1)}, u32[]{:S(2)}, u32[]{:S(2)}) %collective-permute-start.17) | collective-permute-done | bytes 262176 | tf_op jit(solution)/shard_map/ppermute | solution.py:252
  90.9 2.9 %project.6.refs_2_ = f32[512,512]{1,0:T(8,128)S(1)} custom-call(s32[2]{0:T(128)S(1)} %copy-done.2, s32[16]{0:T(128)S(1)} %copy-done.4, f32[512,512]{1,0:T(8,128)} %project.5.refs_2_, bf16[2,2,256,128]{3,2,1,0:T(8,128)(2,1)S(1)} %collective-permute-done.12.refs_3_, bf16[2,2,256,128]{3,2,1,0:T(8,128)(2,1)S(1)} %collective-permute-done.16.refs_4_, ...), custom_call_target="tpu_custom_call" | custom-call | tf_op jit(solution)/shard_map/project/pallas_call | solution.py:176
  93.8 2.5 %collective-permute-done.18.refs_3_ = bf16[2,2,256,128]{3,2,1,0:T(8,128)(2,1)S(1)} collective-permute-done((bf16[2,2,256,128]{3,2,1,0:T(8,128)(2,1)S(1)}, bf16[2,2,256,128]{3,2,1,0:T(8,128)(2,1)S(1)}, u32[]{:S(2)}, u32[]{:S(2)}) %collective-permute-start.18) | collective-permute-done | bytes 262176 | tf_op jit(solution)/shard_map/ppermute | solution.py:252
  96.7 2.1 %project.7 = (bf16[256,512]{1,0:T(8,128)(2,1)S(1)}, bf16[256,512]{1,0:T(8,128)(2,1)S(1)}) custom-call(s32[2]{0:T(128)S(1)} %copy-done.2, s32[8]{0:T(128)S(1)} %copy-done.3, f32[512,512]{1,0:T(8,128)S(1)} %project.6.refs_2_, bf16[2,2,256,128]{3,2,1,0:T(8,128)(2,1)S(1)} %collective-permute-done.18.refs_3_, ...), custom_call_target="tpu_custom_call" | custom-call | tf_op jit(solution)/shard_map/project/pallas_call | solution.py:176
  98.9 4.3 %collective-permute-start.20 = (bf16[256,512]{1,0:T(8,128)(2,1)S(1)}, bf16[256,512]{1,0:T(8,128)(2,1)S(1)}, u32[]{:S(2)}, u32[]{:S(2)}) collective-permute-start(bf16[256,512]{1,0:T(8,128)(2,1)S(1)} %get-tuple-element.35), channel_id=1, source_target_pairs={{0,0},{1,16},{2,8},{3,24},{4,4},{5,20},{6,12},{7,28},{8,1},{9,17},... | collective-permute-start | bytes 786440 | tf_op jit(solution)/shard_map/ppermute | solution.py:266
  103.2 3.7 %collective-permute-start.21 = (bf16[256,512]{1,0:T(8,128)(2,1)S(1)}, bf16[256,512]{1,0:T(8,128)(2,1)S(1)}, u32[]{:S(2)}, u32[]{:S(2)}) collective-permute-start(bf16[256,512]{1,0:T(8,128)(2,1)S(1)} %get-tuple-element.36), channel_id=1, source_target_pairs={{0,4},{1,20},{2,12},{3,28},{4,0},{5,16},{6,8},{7,24},{8,5},{9,21},... | collective-permute-start | bytes 786440 | tf_op jit(solution)/shard_map/ppermute | solution.py:266
  106.9 14.7 %collective-permute-done.21 = bf16[256,512]{1,0:T(8,128)(2,1)S(1)} collective-permute-done((bf16[256,512]{1,0:T(8,128)(2,1)S(1)}, bf16[256,512]{1,0:T(8,128)(2,1)S(1)}, u32[]{:S(2)}, u32[]{:S(2)}) %collective-permute-start.21) | collective-permute-done | bytes 262176 | tf_op jit(solution)/shard_map/ppermute | solution.py:266
  (69 shorter events, 13.4 us)
Async XLA Ops:
  2.8 42.7 %copy-start.6 = (bf16[256,512]{1,0:T(8,128)(2,1)S(1)}, bf16[256,512]{1,0:T(8,128)(2,1)}, u32[]{:S(2)}) copy-start(bf16[256,512]{1,0:T(8,128)(2,1)} %constant.40.clone.refs_4_) | copy-start | bytes 786436
  2.8 42.7 %all-to-all-start = ((bf16[8,3,256,128]{3,2,1,0:T(8,128)(2,1)}), bf16[8,3,256,128]{3,2,1,0:T(8,128)(2,1)S(1)}, u32[]{:S(2)}, u32[]{:S(2)}) async-start(bf16[8,3,256,128]{3,2,1,0:T(8,128)(2,1)} %pack.1), calls=%async_computation | async-start | bytes 3145728 | tf_op jit(solution)/shard_map/all_to_all | solution.py:226
  9.3 23.9 %collective-permute-start.1 = (bf16[8,128,512]{2,1,0:T(8,128)(2,1)S(1)}, bf16[8,128,512]{2,1,0:T(8,128)(2,1)}, u32[]{:S(2)}, u32[]{:S(2)}) collective-permute-start(bf16[8,128,512]{2,1,0:T(8,128)(2,1)S(1)} %bitcast.18), channel_id=1, source_target_pairs={{0,2},{1,3},{2,0},{3,1},{4,6},{5,7},{6,4},{7,5},{8,10},{9,11},{10,... | collective-permute-start | bytes 3145736 | tf_op jit(solution)/shard_map/ppermute | solution.py:222
  10.6 24.6 %collective-permute-start = (bf16[8,128,512]{2,1,0:T(8,128)(2,1)S(1)}, bf16[8,128,512]{2,1,0:T(8,128)(2,1)}, u32[]{:S(2)}, u32[]{:S(2)}) collective-permute-start(bf16[8,128,512]{2,1,0:T(8,128)(2,1)S(1)} %bitcast.19), channel_id=1, source_target_pairs={{0,1},{1,0},{2,3},{3,2},{4,5},{5,4},{6,7},{7,6},{8,9},{9,8},{10,11... | collective-permute-start | bytes 3145736 | tf_op jit(solution)/shard_map/ppermute | solution.py:219
  33.2 4.5 %collective-permute-start.2 = (bf16[8,128,512]{2,1,0:T(8,128)(2,1)}, bf16[8,128,512]{2,1,0:T(8,128)(2,1)}, u32[]{:S(2)}, u32[]{:S(2)}) collective-permute-start(bf16[8,128,512]{2,1,0:T(8,128)(2,1)} %collective-permute-done.1.refs_6_.refs_12_.refs_18_.refs_7_.refs_13_), channel_id=1, source_target_pairs={{0,1},{1,0},{2,3},{3,2},{4,5},{5,4},{6,7},{7,6},{8,9},{9,8},{10,11... | collective-permute-start | bytes 3145736 | tf_op jit(solution)/shard_map/ppermute | solution.py:223
  49.1 3.6 %collective-permute-start.3 = (bf16[2,256,128]{2,1,0:T(8,128)(2,1)S(1)}, bf16[2,256,128]{2,1,0:T(8,128)(2,1)S(1)}, u32[]{:S(2)}, u32[]{:S(2)}) collective-permute-start(bf16[2,256,128]{2,1,0:T(8,128)(2,1)S(1)} %get-tuple-element.23), channel_id=1, source_target_pairs={{0,1},{1,0},{2,3},{3,2},{4,5},{5,4},{6,7},{7,6},{8,9},{9,8},{10,11... | collective-permute-start | bytes 393224 | tf_op jit(solution)/shard_map/ppermute | solution.py:231
  51.0 5.1 %collective-permute-start.8 = (bf16[2,256,128]{2,1,0:T(8,128)(2,1)S(1)}, bf16[2,256,128]{2,1,0:T(8,128)(2,1)S(1)}, u32[]{:S(2)}, u32[]{:S(2)}) collective-permute-start(bf16[2,256,128]{2,1,0:T(8,128)(2,1)S(1)} %get-tuple-element.24), channel_id=1, source_target_pairs={{0,2},{1,3},{2,0},{3,1},{4,6},{5,7},{6,4},{7,5},{8,10},{9,11},{10,... | collective-permute-start | bytes 393224 | tf_op jit(solution)/shard_map/ppermute | solution.py:231
  52.2 7.1 %collective-permute-start.9 = (bf16[2,256,128]{2,1,0:T(8,128)(2,1)S(1)}, bf16[2,256,128]{2,1,0:T(8,128)(2,1)S(1)}, u32[]{:S(2)}, u32[]{:S(2)}) collective-permute-start(bf16[2,256,128]{2,1,0:T(8,128)(2,1)S(1)} %get-tuple-element.25), channel_id=1, source_target_pairs={{0,3},{1,2},{2,1},{3,0},{4,7},{5,6},{6,5},{7,4},{8,11},{9,10},{10,... | collective-permute-start | bytes 393224 | tf_op jit(solution)/shard_map/ppermute | solution.py:231
  52.7 8.1 %collective-permute-start.4 = (bf16[2,2,256,128]{3,2,1,0:T(8,128)(2,1)S(1)}, bf16[2,2,256,128]{3,2,1,0:T(8,128)(2,1)S(1)}, u32[]{:S(2)}, u32[]{:S(2)}) collective-permute-start(bf16[2,2,256,128]{3,2,1,0:T(8,128)(2,1)S(1)} %pad_maximum_fusion.refs_2_), channel_id=1, source_target_pairs={{8,16},{16,24},{24,28},{28,20},{20,12},{12,4},{4,0},{0,8},{9,17},{... | collective-permute-start | bytes 786440 | tf_op jit(solution)/shard_map/ppermute | solution.py:252
  52.8 8.1 %collective-permute-start.6 = (bf16[2,2,256,128]{3,2,1,0:T(8,128)(2,1)S(1)}, bf16[2,2,256,128]{3,2,1,0:T(8,128)(2,1)S(1)}, u32[]{:S(2)}, u32[]{:S(2)}) collective-permute-start(bf16[2,2,256,128]{3,2,1,0:T(8,128)(2,1)S(1)} %pad_maximum_fusion.refs_2_), channel_id=1, source_target_pairs={{8,0},{16,8},{24,16},{28,24},{20,28},{12,20},{4,12},{0,4},{9,1},{1... | collective-permute-start | bytes 786440 | tf_op jit(solution)/shard_map/ppermute | solution.py:252
  59.3 8.1 %collective-permute-start.11 = (bf16[2,2,256,128]{3,2,1,0:T(8,128)(2,1)S(1)}, bf16[2,2,256,128]{3,2,1,0:T(8,128)(2,1)S(1)}, u32[]{:S(2)}, u32[]{:S(2)}) collective-permute-start(bf16[2,2,256,128]{3,2,1,0:T(8,128)(2,1)S(1)} %pad_maximum_fusion.1.refs_3_), channel_id=1, source_target_pairs={{8,0},{16,8},{24,16},{28,24},{20,28},{12,20},{4,12},{0,4},{9,1},{1... | collective-permute-start | bytes 786440 | tf_op jit(solution)/shard_map/ppermute | solution.py:252
  60.5 8.0 %collective-permute-start.10 = (bf16[2,2,256,128]{3,2,1,0:T(8,128)(2,1)S(1)}, bf16[2,2,256,128]{3,2,1,0:T(8,128)(2,1)S(1)}, u32[]{:S(2)}, u32[]{:S(2)}) collective-permute-start(bf16[2,2,256,128]{3,2,1,0:T(8,128)(2,1)S(1)} %pad_maximum_fusion.1.refs_3_), channel_id=1, source_target_pairs={{8,16},{16,24},{24,28},{28,20},{20,12},{12,4},{4,0},{0,8},{9,17},{... | collective-permute-start | bytes 786440 | tf_op jit(solution)/shard_map/ppermute | solution.py:252
  60.9 13.0 %collective-permute-start.5 = (bf16[2,2,256,128]{3,2,1,0:T(8,128)(2,1)S(1)}, bf16[2,2,256,128]{3,2,1,0:T(8,128)(2,1)S(1)}, u32[]{:S(2)}, u32[]{:S(2)}) collective-permute-start(bf16[2,2,256,128]{3,2,1,0:T(8,128)(2,1)S(1)} %collective-permute-done.4.refs_8_), channel_id=1, source_target_pairs={{8,16},{16,24},{24,28},{28,20},{20,12},{12,4},{4,0},{0,8},{9,17},{... | collective-permute-start | bytes 786440 | tf_op jit(solution)/shard_map/ppermute | solution.py:252
  60.9 12.9 %collective-permute-start.7 = (bf16[2,2,256,128]{3,2,1,0:T(8,128)(2,1)S(1)}, bf16[2,2,256,128]{3,2,1,0:T(8,128)(2,1)S(1)}, u32[]{:S(2)}, u32[]{:S(2)}) collective-permute-start(bf16[2,2,256,128]{3,2,1,0:T(8,128)(2,1)S(1)} %collective-permute-done.6.refs_14_), channel_id=1, source_target_pairs={{8,0},{16,8},{24,16},{28,24},{20,28},{12,20},{4,12},{0,4},{9,1},{1... | collective-permute-start | bytes 786440 | tf_op jit(solution)/shard_map/ppermute | solution.py:252
  67.4 11.2 %collective-permute-start.15 = (bf16[2,2,256,128]{3,2,1,0:T(8,128)(2,1)S(1)}, bf16[2,2,256,128]{3,2,1,0:T(8,128)(2,1)S(1)}, u32[]{:S(2)}, u32[]{:S(2)}) collective-permute-start(bf16[2,2,256,128]{3,2,1,0:T(8,128)(2,1)S(1)} %collective-permute-done.11.refs_15_), channel_id=1, source_target_pairs={{8,0},{16,8},{24,16},{28,24},{20,28},{12,20},{4,12},{0,4},{9,1},{1... | collective-permute-start | bytes 786440 | tf_op jit(solution)/shard_map/ppermute | solution.py:252
  68.5 11.2 %collective-permute-start.14 = (bf16[2,2,256,128]{3,2,1,0:T(8,128)(2,1)S(1)}, bf16[2,2,256,128]{3,2,1,0:T(8,128)(2,1)S(1)}, u32[]{:S(2)}, u32[]{:S(2)}) collective-permute-start(bf16[2,2,256,128]{3,2,1,0:T(8,128)(2,1)S(1)} %collective-permute-done.10.refs_9_), channel_id=1, source_target_pairs={{8,16},{16,24},{24,28},{28,20},{20,12},{12,4},{4,0},{0,8},{9,17},{... | collective-permute-start | bytes 786440 | tf_op jit(solution)/shard_map/ppermute | solution.py:252
  73.8 11.2 %collective-permute-start.12 = (bf16[2,2,256,128]{3,2,1,0:T(8,128)(2,1)S(1)}, bf16[2,2,256,128]{3,2,1,0:T(8,128)(2,1)S(1)}, u32[]{:S(2)}, u32[]{:S(2)}) collective-permute-start(bf16[2,2,256,128]{3,2,1,0:T(8,128)(2,1)S(1)} %collective-permute-done.5.refs_3_), channel_id=1, source_target_pairs={{8,16},{16,24},{24,28},{28,20},{20,12},{12,4},{4,0},{0,8},{9,17},{... | collective-permute-start | bytes 786440 | tf_op jit(solution)/shard_map/ppermute | solution.py:252
  74.2 10.9 %collective-permute-start.13 = (bf16[2,2,256,128]{3,2,1,0:T(8,128)(2,1)S(1)}, bf16[2,2,256,128]{3,2,1,0:T(8,128)(2,1)S(1)}, u32[]{:S(2)}, u32[]{:S(2)}) collective-permute-start(bf16[2,2,256,128]{3,2,1,0:T(8,128)(2,1)S(1)} %collective-permute-done.7.refs_9_), channel_id=1, source_target_pairs={{8,0},{16,8},{24,16},{28,24},{20,28},{12,20},{4,12},{0,4},{9,1},{1... | collective-permute-start | bytes 786440 | tf_op jit(solution)/shard_map/ppermute | solution.py:252
  78.6 11.1 %collective-permute-start.17 = (bf16[2,2,256,128]{3,2,1,0:T(8,128)(2,1)S(1)}, bf16[2,2,256,128]{3,2,1,0:T(8,128)(2,1)S(1)}, u32[]{:S(2)}, u32[]{:S(2)}) collective-permute-start(bf16[2,2,256,128]{3,2,1,0:T(8,128)(2,1)S(1)} %collective-permute-done.15.refs_10_), channel_id=1, source_target_pairs={{8,0},{16,8},{24,16},{28,24},{20,28},{12,20},{4,12},{0,4},{9,1},{1... | collective-permute-start | bytes 786440 | tf_op jit(solution)/shard_map/ppermute | solution.py:252
  79.8 11.1 %collective-permute-start.16 = (bf16[2,2,256,128]{3,2,1,0:T(8,128)(2,1)S(1)}, bf16[2,2,256,128]{3,2,1,0:T(8,128)(2,1)S(1)}, u32[]{:S(2)}, u32[]{:S(2)}) collective-permute-start(bf16[2,2,256,128]{3,2,1,0:T(8,128)(2,1)S(1)} %collective-permute-done.14.refs_4_), channel_id=1, source_target_pairs={{8,16},{16,24},{24,28},{28,20},{20,12},{12,4},{4,0},{0,8},{9,17},{... | collective-permute-start | bytes 786440 | tf_op jit(solution)/shard_map/ppermute | solution.py:252
  85.1 11.2 %collective-permute-start.18 = (bf16[2,2,256,128]{3,2,1,0:T(8,128)(2,1)S(1)}, bf16[2,2,256,128]{3,2,1,0:T(8,128)(2,1)S(1)}, u32[]{:S(2)}, u32[]{:S(2)}) collective-permute-start(bf16[2,2,256,128]{3,2,1,0:T(8,128)(2,1)S(1)} %collective-permute-done.12.refs_3_), channel_id=1, source_target_pairs={{8,16},{16,24},{24,28},{28,20},{20,12},{12,4},{4,0},{0,8},{9,17},{... | collective-permute-start | bytes 786440 | tf_op jit(solution)/shard_map/ppermute | solution.py:252
  89.7 7.0 %collective-permute-start.19 = (bf16[2,2,256,128]{3,2,1,0:T(8,128)(2,1)S(1)}, bf16[2,2,256,128]{3,2,1,0:T(8,128)(2,1)S(1)}, u32[]{:S(2)}, u32[]{:S(2)}) collective-permute-start(bf16[2,2,256,128]{3,2,1,0:T(8,128)(2,1)S(1)} %collective-permute-done.17.refs_10_), channel_id=1, source_target_pairs={{8,0},{16,8},{24,16},{28,24},{20,28},{12,20},{4,12},{0,4},{9,1},{1... | collective-permute-start | bytes 786440 | tf_op jit(solution)/shard_map/ppermute | solution.py:252
  98.9 8.0 %collective-permute-start.20 = (bf16[256,512]{1,0:T(8,128)(2,1)S(1)}, bf16[256,512]{1,0:T(8,128)(2,1)S(1)}, u32[]{:S(2)}, u32[]{:S(2)}) collective-permute-start(bf16[256,512]{1,0:T(8,128)(2,1)S(1)} %get-tuple-element.35), channel_id=1, source_target_pairs={{0,0},{1,16},{2,8},{3,24},{4,4},{5,20},{6,12},{7,28},{8,1},{9,17},... | collective-permute-start | bytes 786440 | tf_op jit(solution)/shard_map/ppermute | solution.py:266
  103.2 18.4 %collective-permute-start.21 = (bf16[256,512]{1,0:T(8,128)(2,1)S(1)}, bf16[256,512]{1,0:T(8,128)(2,1)S(1)}, u32[]{:S(2)}, u32[]{:S(2)}) collective-permute-start(bf16[256,512]{1,0:T(8,128)(2,1)S(1)} %get-tuple-element.36), channel_id=1, source_target_pairs={{0,4},{1,20},{2,12},{3,28},{4,0},{5,16},{6,8},{7,24},{8,5},{9,21},... | collective-permute-start | bytes 786440 | tf_op jit(solution)/shard_map/ppermute | solution.py:266
  (17 other events, 203.2 us)

commit v7 on v5

--- a/solution.py
+++ b/solution.py
@@ -36,7 +36,7 @@
 
 def pack(outer_gate, inner_gate, values_in, filters, n):
     block, wide = outer_gate.shape
-    tile = block // 2
+    tile = block
     return pl.pallas_call(
         pack_kernel,
         grid=(block // tile,),
@@ -65,7 +65,7 @@
 
     step = 8
 
-    @pl.loop(0, block // step)
+    @pl.loop(0, block // step, unroll=2)
     def _(c):
         re = pl.ds(pl.multiple_of(c * step, step), step)
         im = pl.ds(pl.multiple_of(block + c * step, step), step)

time: 118 us -> 118 us (level)
  no operation moved by 1% of the time
where the time goes in v7:
time: 118 us
  waiting for transfers between devices  69.7 us (59%)
  starting transfers between devices  26.2 us (22%)
  Pallas kernels  20.3 us (17%)
    ppermute x1, waiting for transfers between devices, per_device(): far = lax.ppermute(even, 'ch', pairs)  24.2 us
    ppermute x14, waiting for transfers between devices, per_device(): tips[h][way] = lax.ppermute(tips[h][way], 'ctx', routes[way])  15.2 us
    ppermute x14, starting transfers between devices, per_device(): tips[h][way] = lax.ppermute(tips[h][way], 'ctx', routes[way])  14.3 us
    ppermute x2, waiting for transfers between devices, per_device(): found.append(lax.ppermute(sent[e], ('ctx', 'ch'), route))  14 us
    pallas_call x4, Pallas kernels, project(): pl.pallas_call(lambda *refs: project_kernel(count, m, last, *refs), grid_...  13.6 us
    all_to_all x1, waiting for transfers between devices, per_device(): packed = lax.all_to_all(packed, 'ctx', 0, 0)  9.2 us
    all_to_all x1, starting transfers between devices, per_device(): packed = lax.all_to_all(packed, 'ctx', 0, 0)  5.97 us
    ppermute x3, waiting for transfers between devices, per_device(): lax.ppermute(part, 'ch', [(d, d ^ b) for d in range(m)])  4.28 us
  transfers between devices with their start and end apart: 23, of which 16 were waited for; matrix products, arithmetic and copies ran while one was open for 0% of the time, Pallas kernels for 10%

profile of v7, /device:TPU:2, one launch (start us, length us, event | category | flops | bytes accessed | tf_op | source)
XLA Modules:
  0.0 117.7 jit_solution(8363219538829929980)
XLA Ops:
  0.0 3.2 %pack.1 = bf16[8,3,256,128]{3,2,1,0:T(8,128)(2,1)} custom-call(bf16[256,1024]{1,0:T(8,128)(2,1)} %outer_ref.1, bf16[256,1024]{1,0:T(8,128)(2,1)} %inner_ref.1, bf16[256,1024]{1,0:T(8,128)(2,1)} %values_ref.1, f32[256,1024]{1,0:T(8,128)} %filters_ref.1), custom_call_target="tpu_custom_call" | custom-call | flops 262144 | bytes 4194304 | tf_op jit(solution)/shard_map/pack/pallas_call | solution.py:40
  3.2 6.0 %all-to-all-start = ((bf16[8,3,256,128]{3,2,1,0:T(8,128)(2,1)}), bf16[8,3,256,128]{3,2,1,0:T(8,128)(2,1)S(1)}, u32[]{:S(2)}, u32[]{:S(2)}) async-start(bf16[8,3,256,128]{3,2,1,0:T(8,128)(2,1)} %pack.1), calls=%async_computation | async-start | bytes 3145728 | tf_op jit(solution)/shard_map/all_to_all | solution.py:226
  9.8 24.2 %collective-permute-done.1.refs_6_.refs_12_.refs_18_.refs_7_.refs_13_ = bf16[8,128,512]{2,1,0:T(8,128)(2,1)} collective-permute-done((bf16[8,128,512]{2,1,0:T(8,128)(2,1)S(1)}, bf16[8,128,512]{2,1,0:T(8,128)(2,1)}, u32[]{:S(2)}, u32[]{:S(2)}) %collective-permute-start.1) | collective-permute-done | bytes 1048608 | tf_op jit(solution)/shard_map/ppermute | solution.py:222
  34.1 2.8 %collective-permute-done.2.refs_7_.refs_13_.refs_19_.refs_8_.refs_14_ = bf16[8,128,512]{2,1,0:T(8,128)(2,1)} collective-permute-done((bf16[8,128,512]{2,1,0:T(8,128)(2,1)}, bf16[8,128,512]{2,1,0:T(8,128)(2,1)}, u32[]{:S(2)}, u32[]{:S(2)}) %collective-permute-start.2) | collective-permute-done | bytes 1048608 | tf_op jit(solution)/shard_map/ppermute | solution.py:223
  37.0 9.2 %all-to-all-done.refs_1_ = bf16[8,3,256,128]{3,2,1,0:T(8,128)(2,1)S(1)} async-done(((bf16[8,3,256,128]{3,2,1,0:T(8,128)(2,1)}), bf16[8,3,256,128]{3,2,1,0:T(8,128)(2,1)S(1)}, u32[]{:S(2)}, u32[]{:S(2)}) %all-to-all-start) | async-done | bytes 1572896 | tf_op jit(solution)/shard_map/all_to_all | solution.py:226
  46.2 3.4 %convolve.1 = (bf16[2,256,128]{2,1,0:T(8,128)(2,1)S(1)}, bf16[2,256,128]{2,1,0:T(8,128)(2,1)S(1)}, bf16[2,256,128]{2,1,0:T(8,128)(2,1)S(1)}, bf16[2,256,128]{2,1,0:T(8,128)(2,1)S(1)}) custom-call(s32[2]{0:T(128)S(1)} %pad_add_fusion.refs_0_, bf16[8,3,256,128]{3,2,1,0:T(8,128)(2,1)S(1)} %all-to-all-done.refs_1_, ...), custom_call_target="tpu_custom_call" | custom-call | flops 2147483648 | bytes 4194304 | tf_op jit(solution)/shard_map/convolve/pallas_call | solution.py:106
  51.7 2.0 %collective-permute-start.6 = (bf16[2,2,256,128]{3,2,1,0:T(8,128)(2,1)S(1)}, bf16[2,2,256,128]{3,2,1,0:T(8,128)(2,1)S(1)}, u32[]{:S(2)}, u32[]{:S(2)}) collective-permute-start(bf16[2,2,256,128]{3,2,1,0:T(8,128)(2,1)S(1)} %pad_maximum_fusion.refs_2_), channel_id=1, source_target_pairs={{8,0},{16,8},{24,16},{28,24},{20,28},{12,20},{4,12},{0,4},{9,1},{1... | collective-permute-start | bytes 786440 | tf_op jit(solution)/shard_map/ppermute | solution.py:252
  53.7 2.4 %collective-permute-done.8 = bf16[2,256,128]{2,1,0:T(8,128)(2,1)S(1)} collective-permute-done((bf16[2,256,128]{2,1,0:T(8,128)(2,1)S(1)}, bf16[2,256,128]{2,1,0:T(8,128)(2,1)S(1)}, u32[]{:S(2)}, u32[]{:S(2)}) %collective-permute-start.8) | collective-permute-done | bytes 131104 | tf_op jit(solution)/shard_map/ppermute | solution.py:231
  56.1 1.9 %collective-permute-done.9 = bf16[2,256,128]{2,1,0:T(8,128)(2,1)S(1)} collective-permute-done((bf16[2,256,128]{2,1,0:T(8,128)(2,1)S(1)}, bf16[2,256,128]{2,1,0:T(8,128)(2,1)S(1)}, u32[]{:S(2)}, u32[]{:S(2)}) %collective-permute-start.9) | collective-permute-done | bytes 131104 | tf_op jit(solution)/shard_map/ppermute | solution.py:231
  58.0 1.5 %collective-permute-start.11 = (bf16[2,2,256,128]{3,2,1,0:T(8,128)(2,1)S(1)}, bf16[2,2,256,128]{3,2,1,0:T(8,128)(2,1)S(1)}, u32[]{:S(2)}, u32[]{:S(2)}) collective-permute-start(bf16[2,2,256,128]{3,2,1,0:T(8,128)(2,1)S(1)} %pad_maximum_fusion.1.refs_3_), channel_id=1, source_target_pairs={{8,0},{16,8},{24,16},{28,24},{20,28},{12,20},{4,12},{0,4},{9,1},{1... | collective-permute-start | bytes 786440 | tf_op jit(solution)/shard_map/ppermute | solution.py:252
  60.5 1.7 %collective-permute-start.7 = (bf16[2,2,256,128]{3,2,1,0:T(8,128)(2,1)S(1)}, bf16[2,2,256,128]{3,2,1,0:T(8,128)(2,1)S(1)}, u32[]{:S(2)}, u32[]{:S(2)}) collective-permute-start(bf16[2,2,256,128]{3,2,1,0:T(8,128)(2,1)S(1)} %collective-permute-done.6.refs_14_), channel_id=1, source_target_pairs={{8,0},{16,8},{24,16},{28,24},{20,28},{12,20},{4,12},{0,4},{9,1},{1... | collective-permute-start | bytes 786440 | tf_op jit(solution)/shard_map/ppermute | solution.py:252
  62.3 4.9 %collective-permute-done.11.refs_15_ = bf16[2,2,256,128]{3,2,1,0:T(8,128)(2,1)S(1)} collective-permute-done((bf16[2,2,256,128]{3,2,1,0:T(8,128)(2,1)S(1)}, bf16[2,2,256,128]{3,2,1,0:T(8,128)(2,1)S(1)}, u32[]{:S(2)}, u32[]{:S(2)}) %collective-permute-start.11) | collective-permute-done | bytes 262176 | tf_op jit(solution)/shard_map/ppermute | solution.py:252
  69.3 4.5 %project.4.refs_2_ = f32[512,512]{1,0:T(8,128)} custom-call(s32[2]{0:T(128)} %copy-done.1, s32[24]{0:T(128)} %constant.52.clone.refs_1_, bf16[2,2,256,128]{3,2,1,0:T(8,128)(2,1)} %copy-done.8, bf16[2,2,256,128]{3,2,1,0:T(8,128)(2,1)} %copy-done.9, bf16[8,128,512]{2,1,0:T(8,128)(2,1)} %bitcast.10, ...), custom_call_target="tpu_custom_call" | custom-call | tf_op jit(solution)/shard_map/project/pallas_call | solution.py:176
  74.9 1.4 %collective-permute-start.13 = (bf16[2,2,256,128]{3,2,1,0:T(8,128)(2,1)S(1)}, bf16[2,2,256,128]{3,2,1,0:T(8,128)(2,1)S(1)}, u32[]{:S(2)}, u32[]{:S(2)}) collective-permute-start(bf16[2,2,256,128]{3,2,1,0:T(8,128)(2,1)S(1)} %collective-permute-done.7.refs_9_), channel_id=1, source_target_pairs={{8,0},{16,8},{24,16},{28,24},{20,28},{12,20},{4,12},{0,4},{9,1},{1... | collective-permute-start | bytes 786440 | tf_op jit(solution)/shard_map/ppermute | solution.py:252
  76.3 2.1 %collective-permute-done.15.refs_10_ = bf16[2,2,256,128]{3,2,1,0:T(8,128)(2,1)S(1)} collective-permute-done((bf16[2,2,256,128]{3,2,1,0:T(8,128)(2,1)S(1)}, bf16[2,2,256,128]{3,2,1,0:T(8,128)(2,1)S(1)}, u32[]{:S(2)}, u32[]{:S(2)}) %collective-permute-start.15) | collective-permute-done | bytes 262176 | tf_op jit(solution)/shard_map/ppermute | solution.py:252
  78.4 1.4 %collective-permute-start.17 = (bf16[2,2,256,128]{3,2,1,0:T(8,128)(2,1)S(1)}, bf16[2,2,256,128]{3,2,1,0:T(8,128)(2,1)S(1)}, u32[]{:S(2)}, u32[]{:S(2)}) collective-permute-start(bf16[2,2,256,128]{3,2,1,0:T(8,128)(2,1)S(1)} %collective-permute-done.15.refs_10_), channel_id=1, source_target_pairs={{8,0},{16,8},{24,16},{28,24},{20,28},{12,20},{4,12},{0,4},{9,1},{1... | collective-permute-start | bytes 786440 | tf_op jit(solution)/shard_map/ppermute | solution.py:252
  80.6 4.2 %project.5.refs_2_ = f32[512,512]{1,0:T(8,128)} custom-call(s32[2]{0:T(128)} %copy-done.1, s32[16]{0:T(128)} %constant.53.clone.refs_1_, f32[512,512]{1,0:T(8,128)} %project.4.refs_2_, bf16[2,2,256,128]{3,2,1,0:T(8,128)(2,1)} %copy-done.14, bf16[2,2,256,128]{3,2,1,0:T(8,128)(2,1)} %copy-done.15, bf16[8,128,512]{2,1,0:T(8,128)(2,1)} %bitcast.13, ...), custom_call_target="tpu_custom_call" | custom-call | tf_op jit(solution)/shard_map/project/pallas_call | solution.py:176
  86.1 3.2 %collective-permute-done.17.refs_10_ = bf16[2,2,256,128]{3,2,1,0:T(8,128)(2,1)S(1)} collective-permute-done((bf16[2,2,256,128]{3,2,1,0:T(8,128)(2,1)S(1)}, bf16[2,2,256,128]{3,2,1,0:T(8,128)(2,1)S(1)}, u32[]{:S(2)}, u32[]{:S(2)}) %collective-permute-start.17) | collective-permute-done | bytes 262176 | tf_op jit(solution)/shard_map/ppermute | solution.py:252
  91.1 2.9 %project.6.refs_2_ = f32[512,512]{1,0:T(8,128)S(1)} custom-call(s32[2]{0:T(128)S(1)} %copy-done.2, s32[16]{0:T(128)S(1)} %copy-done.4, f32[512,512]{1,0:T(8,128)} %project.5.refs_2_, bf16[2,2,256,128]{3,2,1,0:T(8,128)(2,1)S(1)} %collective-permute-done.12.refs_3_, bf16[2,2,256,128]{3,2,1,0:T(8,128)(2,1)S(1)} %collective-permute-done.16.refs_4_, ...), custom_call_target="tpu_custom_call" | custom-call | tf_op jit(solution)/shard_map/project/pallas_call | solution.py:176
  94.0 2.1 %collective-permute-done.18.refs_3_ = bf16[2,2,256,128]{3,2,1,0:T(8,128)(2,1)S(1)} collective-permute-done((bf16[2,2,256,128]{3,2,1,0:T(8,128)(2,1)S(1)}, bf16[2,2,256,128]{3,2,1,0:T(8,128)(2,1)S(1)}, u32[]{:S(2)}, u32[]{:S(2)}) %collective-permute-start.18) | collective-permute-done | bytes 262176 | tf_op jit(solution)/shard_map/ppermute | solution.py:252
  97.2 2.1 %project.7 = (bf16[256,512]{1,0:T(8,128)(2,1)S(1)}, bf16[256,512]{1,0:T(8,128)(2,1)S(1)}) custom-call(s32[2]{0:T(128)S(1)} %copy-done.2, s32[8]{0:T(128)S(1)} %copy-done.3, f32[512,512]{1,0:T(8,128)S(1)} %project.6.refs_2_, bf16[2,2,256,128]{3,2,1,0:T(8,128)(2,1)S(1)} %collective-permute-done.18.refs_3_, ...), custom_call_target="tpu_custom_call" | custom-call | tf_op jit(solution)/shard_map/project/pallas_call | solution.py:176
  99.4 3.3 %collective-permute-start.20 = (bf16[256,512]{1,0:T(8,128)(2,1)S(1)}, bf16[256,512]{1,0:T(8,128)(2,1)S(1)}, u32[]{:S(2)}, u32[]{:S(2)}) collective-permute-start(bf16[256,512]{1,0:T(8,128)(2,1)S(1)} %get-tuple-element.35), channel_id=1, source_target_pairs={{0,0},{1,16},{2,4},{3,20},{4,8},{5,24},{6,12},{7,28},{8,1},{9,17},... | collective-permute-start | bytes 786440 | tf_op jit(solution)/shard_map/ppermute | solution.py:266
  102.8 12.0 %collective-permute-done.20 = bf16[256,512]{1,0:T(8,128)(2,1)S(1)} collective-permute-done((bf16[256,512]{1,0:T(8,128)(2,1)S(1)}, bf16[256,512]{1,0:T(8,128)(2,1)S(1)}, u32[]{:S(2)}, u32[]{:S(2)}) %collective-permute-start.20) | collective-permute-done | bytes 262176 | tf_op jit(solution)/shard_map/ppermute | solution.py:266
  114.7 2.0 %collective-permute-done.21 = bf16[256,512]{1,0:T(8,128)(2,1)S(1)} collective-permute-done((bf16[256,512]{1,0:T(8,128)(2,1)S(1)}, bf16[256,512]{1,0:T(8,128)(2,1)S(1)}, u32[]{:S(2)}, u32[]{:S(2)}) %collective-permute-start.21) | collective-permute-done | bytes 262176 | tf_op jit(solution)/shard_map/ppermute | solution.py:266
  (69 shorter events, 13.1 us)
Async XLA Ops:
  3.2 43.0 %copy-start.6 = (bf16[256,512]{1,0:T(8,128)(2,1)S(1)}, bf16[256,512]{1,0:T(8,128)(2,1)}, u32[]{:S(2)}) copy-start(bf16[256,512]{1,0:T(8,128)(2,1)} %constant.51.clone.refs_4_) | copy-start | bytes 786436
  3.2 43.0 %all-to-all-start = ((bf16[8,3,256,128]{3,2,1,0:T(8,128)(2,1)}), bf16[8,3,256,128]{3,2,1,0:T(8,128)(2,1)S(1)}, u32[]{:S(2)}, u32[]{:S(2)}) async-start(bf16[8,3,256,128]{3,2,1,0:T(8,128)(2,1)} %pack.1), calls=%async_computation | async-start | bytes 3145728 | tf_op jit(solution)/shard_map/all_to_all | solution.py:226
  9.2 24.8 %collective-permute-start.1 = (bf16[8,128,512]{2,1,0:T(8,128)(2,1)S(1)}, bf16[8,128,512]{2,1,0:T(8,128)(2,1)}, u32[]{:S(2)}, u32[]{:S(2)}) collective-permute-start(bf16[8,128,512]{2,1,0:T(8,128)(2,1)S(1)} %bitcast.18), channel_id=1, source_target_pairs={{0,2},{1,3},{2,0},{3,1},{4,6},{5,7},{6,4},{7,5},{8,10},{9,11},{10,... | collective-permute-start | bytes 3145736 | tf_op jit(solution)/shard_map/ppermute | solution.py:222
  9.8 24.3 %collective-permute-start = (bf16[8,128,512]{2,1,0:T(8,128)(2,1)S(1)}, bf16[8,128,512]{2,1,0:T(8,128)(2,1)}, u32[]{:S(2)}, u32[]{:S(2)}) collective-permute-start(bf16[8,128,512]{2,1,0:T(8,128)(2,1)S(1)} %bitcast.19), channel_id=1, source_target_pairs={{0,1},{1,0},{2,3},{3,2},{4,5},{5,4},{6,7},{7,6},{8,9},{9,8},{10,11... | collective-permute-start | bytes 3145736 | tf_op jit(solution)/shard_map/ppermute | solution.py:219
  34.0 3.0 %collective-permute-start.2 = (bf16[8,128,512]{2,1,0:T(8,128)(2,1)}, bf16[8,128,512]{2,1,0:T(8,128)(2,1)}, u32[]{:S(2)}, u32[]{:S(2)}) collective-permute-start(bf16[8,128,512]{2,1,0:T(8,128)(2,1)} %collective-permute-done.1.refs_6_.refs_12_.refs_18_.refs_7_.refs_13_), channel_id=1, source_target_pairs={{0,1},{1,0},{2,3},{3,2},{4,5},{5,4},{6,7},{7,6},{8,9},{9,8},{10,11... | collective-permute-start | bytes 3145736 | tf_op jit(solution)/shard_map/ppermute | solution.py:223
  49.7 1.9 %collective-permute-start.3 = (bf16[2,256,128]{2,1,0:T(8,128)(2,1)S(1)}, bf16[2,256,128]{2,1,0:T(8,128)(2,1)S(1)}, u32[]{:S(2)}, u32[]{:S(2)}) collective-permute-start(bf16[2,256,128]{2,1,0:T(8,128)(2,1)S(1)} %get-tuple-element.23), channel_id=1, source_target_pairs={{0,1},{1,0},{2,3},{3,2},{4,5},{5,4},{6,7},{7,6},{8,9},{9,8},{10,11... | collective-permute-start | bytes 393224 | tf_op jit(solution)/shard_map/ppermute | solution.py:231
  49.7 6.4 %collective-permute-start.8 = (bf16[2,256,128]{2,1,0:T(8,128)(2,1)S(1)}, bf16[2,256,128]{2,1,0:T(8,128)(2,1)S(1)}, u32[]{:S(2)}, u32[]{:S(2)}) collective-permute-start(bf16[2,256,128]{2,1,0:T(8,128)(2,1)S(1)} %get-tuple-element.24), channel_id=1, source_target_pairs={{0,2},{1,3},{2,0},{3,1},{4,6},{5,7},{6,4},{7,5},{8,10},{9,11},{10,... | collective-permute-start | bytes 393224 | tf_op jit(solution)/shard_map/ppermute | solution.py:231
  50.3 7.7 %collective-permute-start.9 = (bf16[2,256,128]{2,1,0:T(8,128)(2,1)S(1)}, bf16[2,256,128]{2,1,0:T(8,128)(2,1)S(1)}, u32[]{:S(2)}, u32[]{:S(2)}) collective-permute-start(bf16[2,256,128]{2,1,0:T(8,128)(2,1)S(1)} %get-tuple-element.25), channel_id=1, source_target_pairs={{0,3},{1,2},{2,1},{3,0},{4,7},{5,6},{6,5},{7,4},{8,11},{9,10},{10,... | collective-permute-start | bytes 393224 | tf_op jit(solution)/shard_map/ppermute | solution.py:231
  51.6 8.6 %collective-permute-start.4 = (bf16[2,2,256,128]{3,2,1,0:T(8,128)(2,1)S(1)}, bf16[2,2,256,128]{3,2,1,0:T(8,128)(2,1)S(1)}, u32[]{:S(2)}, u32[]{:S(2)}) collective-permute-start(bf16[2,2,256,128]{3,2,1,0:T(8,128)(2,1)S(1)} %pad_maximum_fusion.refs_2_), channel_id=1, source_target_pairs={{8,16},{16,24},{24,28},{28,20},{20,12},{12,4},{4,0},{0,8},{9,17},{... | collective-permute-start | bytes 786440 | tf_op jit(solution)/shard_map/ppermute | solution.py:252
  51.7 8.8 %collective-permute-start.6 = (bf16[2,2,256,128]{3,2,1,0:T(8,128)(2,1)S(1)}, bf16[2,2,256,128]{3,2,1,0:T(8,128)(2,1)S(1)}, u32[]{:S(2)}, u32[]{:S(2)}) collective-permute-start(bf16[2,2,256,128]{3,2,1,0:T(8,128)(2,1)S(1)} %pad_maximum_fusion.refs_2_), channel_id=1, source_target_pairs={{8,0},{16,8},{24,16},{28,24},{20,28},{12,20},{4,12},{0,4},{9,1},{1... | collective-permute-start | bytes 786440 | tf_op jit(solution)/shard_map/ppermute | solution.py:252
  58.0 9.1 %collective-permute-start.11 = (bf16[2,2,256,128]{3,2,1,0:T(8,128)(2,1)S(1)}, bf16[2,2,256,128]{3,2,1,0:T(8,128)(2,1)S(1)}, u32[]{:S(2)}, u32[]{:S(2)}) collective-permute-start(bf16[2,2,256,128]{3,2,1,0:T(8,128)(2,1)S(1)} %pad_maximum_fusion.1.refs_3_), channel_id=1, source_target_pairs={{8,0},{16,8},{24,16},{28,24},{20,28},{12,20},{4,12},{0,4},{9,1},{1... | collective-permute-start | bytes 786440 | tf_op jit(solution)/shard_map/ppermute | solution.py:252
  59.5 9.1 %collective-permute-start.10 = (bf16[2,2,256,128]{3,2,1,0:T(8,128)(2,1)S(1)}, bf16[2,2,256,128]{3,2,1,0:T(8,128)(2,1)S(1)}, u32[]{:S(2)}, u32[]{:S(2)}) collective-permute-start(bf16[2,2,256,128]{3,2,1,0:T(8,128)(2,1)S(1)} %pad_maximum_fusion.1.refs_3_), channel_id=1, source_target_pairs={{8,16},{16,24},{24,28},{28,20},{20,12},{12,4},{4,0},{0,8},{9,17},{... | collective-permute-start | bytes 786440 | tf_op jit(solution)/shard_map/ppermute | solution.py:252
  60.2 14.0 %collective-permute-start.5 = (bf16[2,2,256,128]{3,2,1,0:T(8,128)(2,1)S(1)}, bf16[2,2,256,128]{3,2,1,0:T(8,128)(2,1)S(1)}, u32[]{:S(2)}, u32[]{:S(2)}) collective-permute-start(bf16[2,2,256,128]{3,2,1,0:T(8,128)(2,1)S(1)} %collective-permute-done.4.refs_8_), channel_id=1, source_target_pairs={{8,16},{16,24},{24,28},{28,20},{20,12},{12,4},{4,0},{0,8},{9,17},{... | collective-permute-start | bytes 786440 | tf_op jit(solution)/shard_map/ppermute | solution.py:252
  60.5 13.7 %collective-permute-start.7 = (bf16[2,2,256,128]{3,2,1,0:T(8,128)(2,1)S(1)}, bf16[2,2,256,128]{3,2,1,0:T(8,128)(2,1)S(1)}, u32[]{:S(2)}, u32[]{:S(2)}) collective-permute-start(bf16[2,2,256,128]{3,2,1,0:T(8,128)(2,1)S(1)} %collective-permute-done.6.refs_14_), channel_id=1, source_target_pairs={{8,0},{16,8},{24,16},{28,24},{20,28},{12,20},{4,12},{0,4},{9,1},{1... | collective-permute-start | bytes 786440 | tf_op jit(solution)/shard_map/ppermute | solution.py:252
  67.2 11.2 %collective-permute-start.15 = (bf16[2,2,256,128]{3,2,1,0:T(8,128)(2,1)S(1)}, bf16[2,2,256,128]{3,2,1,0:T(8,128)(2,1)S(1)}, u32[]{:S(2)}, u32[]{:S(2)}) collective-permute-start(bf16[2,2,256,128]{3,2,1,0:T(8,128)(2,1)S(1)} %collective-permute-done.11.refs_15_), channel_id=1, source_target_pairs={{8,0},{16,8},{24,16},{28,24},{20,28},{12,20},{4,12},{0,4},{9,1},{1... | collective-permute-start | bytes 786440 | tf_op jit(solution)/shard_map/ppermute | solution.py:252
  68.6 11.2 %collective-permute-start.14 = (bf16[2,2,256,128]{3,2,1,0:T(8,128)(2,1)S(1)}, bf16[2,2,256,128]{3,2,1,0:T(8,128)(2,1)S(1)}, u32[]{:S(2)}, u32[]{:S(2)}) collective-permute-start(bf16[2,2,256,128]{3,2,1,0:T(8,128)(2,1)S(1)} %collective-permute-done.10.refs_9_), channel_id=1, source_target_pairs={{8,16},{16,24},{24,28},{28,20},{20,12},{12,4},{4,0},{0,8},{9,17},{... | collective-permute-start | bytes 786440 | tf_op jit(solution)/shard_map/ppermute | solution.py:252
  74.3 11.2 %collective-permute-start.12 = (bf16[2,2,256,128]{3,2,1,0:T(8,128)(2,1)S(1)}, bf16[2,2,256,128]{3,2,1,0:T(8,128)(2,1)S(1)}, u32[]{:S(2)}, u32[]{:S(2)}) collective-permute-start(bf16[2,2,256,128]{3,2,1,0:T(8,128)(2,1)S(1)} %collective-permute-done.5.refs_3_), channel_id=1, source_target_pairs={{8,16},{16,24},{24,28},{28,20},{20,12},{12,4},{4,0},{0,8},{9,17},{... | collective-permute-start | bytes 786440 | tf_op jit(solution)/shard_map/ppermute | solution.py:252
  74.9 10.6 %collective-permute-start.13 = (bf16[2,2,256,128]{3,2,1,0:T(8,128)(2,1)S(1)}, bf16[2,2,256,128]{3,2,1,0:T(8,128)(2,1)S(1)}, u32[]{:S(2)}, u32[]{:S(2)}) collective-permute-start(bf16[2,2,256,128]{3,2,1,0:T(8,128)(2,1)S(1)} %collective-permute-done.7.refs_9_), channel_id=1, source_target_pairs={{8,0},{16,8},{24,16},{28,24},{20,28},{12,20},{4,12},{0,4},{9,1},{1... | collective-permute-start | bytes 786440 | tf_op jit(solution)/shard_map/ppermute | solution.py:252
  78.4 10.9 %collective-permute-start.17 = (bf16[2,2,256,128]{3,2,1,0:T(8,128)(2,1)S(1)}, bf16[2,2,256,128]{3,2,1,0:T(8,128)(2,1)S(1)}, u32[]{:S(2)}, u32[]{:S(2)}) collective-permute-start(bf16[2,2,256,128]{3,2,1,0:T(8,128)(2,1)S(1)} %collective-permute-done.15.refs_10_), channel_id=1, source_target_pairs={{8,0},{16,8},{24,16},{28,24},{20,28},{12,20},{4,12},{0,4},{9,1},{1... | collective-permute-start | bytes 786440 | tf_op jit(solution)/shard_map/ppermute | solution.py:252
  79.9 11.2 %collective-permute-start.16 = (bf16[2,2,256,128]{3,2,1,0:T(8,128)(2,1)S(1)}, bf16[2,2,256,128]{3,2,1,0:T(8,128)(2,1)S(1)}, u32[]{:S(2)}, u32[]{:S(2)}) collective-permute-start(bf16[2,2,256,128]{3,2,1,0:T(8,128)(2,1)S(1)} %collective-permute-done.14.refs_4_), channel_id=1, source_target_pairs={{8,16},{16,24},{24,28},{28,20},{20,12},{12,4},{4,0},{0,8},{9,17},{... | collective-permute-start | bytes 786440 | tf_op jit(solution)/shard_map/ppermute | solution.py:252
  85.5 10.6 %collective-permute-start.18 = (bf16[2,2,256,128]{3,2,1,0:T(8,128)(2,1)S(1)}, bf16[2,2,256,128]{3,2,1,0:T(8,128)(2,1)S(1)}, u32[]{:S(2)}, u32[]{:S(2)}) collective-permute-start(bf16[2,2,256,128]{3,2,1,0:T(8,128)(2,1)S(1)} %collective-permute-done.12.refs_3_), channel_id=1, source_target_pairs={{8,16},{16,24},{24,28},{28,20},{20,12},{12,4},{4,0},{0,8},{9,17},{... | collective-permute-start | bytes 786440 | tf_op jit(solution)/shard_map/ppermute | solution.py:252
  89.3 7.9 %collective-permute-start.19 = (bf16[2,2,256,128]{3,2,1,0:T(8,128)(2,1)S(1)}, bf16[2,2,256,128]{3,2,1,0:T(8,128)(2,1)S(1)}, u32[]{:S(2)}, u32[]{:S(2)}) collective-permute-start(bf16[2,2,256,128]{3,2,1,0:T(8,128)(2,1)S(1)} %collective-permute-done.17.refs_10_), channel_id=1, source_target_pairs={{8,0},{16,8},{24,16},{28,24},{20,28},{12,20},{4,12},{0,4},{9,1},{1... | collective-permute-start | bytes 786440 | tf_op jit(solution)/shard_map/ppermute | solution.py:252
  99.4 15.4 %collective-permute-start.20 = (bf16[256,512]{1,0:T(8,128)(2,1)S(1)}, bf16[256,512]{1,0:T(8,128)(2,1)S(1)}, u32[]{:S(2)}, u32[]{:S(2)}) collective-permute-start(bf16[256,512]{1,0:T(8,128)(2,1)S(1)} %get-tuple-element.35), channel_id=1, source_target_pairs={{0,0},{1,16},{2,4},{3,20},{4,8},{5,24},{6,12},{7,28},{8,1},{9,17},... | collective-permute-start | bytes 786440 | tf_op jit(solution)/shard_map/ppermute | solution.py:266
  102.7 14.1 %collective-permute-start.21 = (bf16[256,512]{1,0:T(8,128)(2,1)S(1)}, bf16[256,512]{1,0:T(8,128)(2,1)S(1)}, u32[]{:S(2)}, u32[]{:S(2)}) collective-permute-start(bf16[256,512]{1,0:T(8,128)(2,1)S(1)} %get-tuple-element.36), channel_id=1, source_target_pairs={{0,8},{1,24},{2,12},{3,28},{4,0},{5,16},{6,4},{7,20},{8,9},{9,25},... | collective-permute-start | bytes 786440 | tf_op jit(solution)/shard_map/ppermute | solution.py:266
  (17 other events, 210.1 us)

commit v8 on v5

--- a/solution.py
+++ b/solution.py
@@ -65,7 +65,7 @@
 
     step = 8
 
-    @pl.loop(0, block // step)
+    @pl.loop(0, block // step, unroll=4)
     def _(c):
         re = pl.ds(pl.multiple_of(c * step, step), step)
         im = pl.ds(pl.multiple_of(block + c * step, step), step)

time: 118 us -> 118 us (level)
  no operation moved by 1% of the time
where the time goes in v8:
time: 118 us; the launch traced here: 117 us
  waiting for transfers between devices  69.7 us (59%)
  starting transfers between devices  26.2 us (22%)
  Pallas kernels  19.8 us (17%)
    ppermute x1, waiting for transfers between devices, per_device(): far = lax.ppermute(even, 'ch', pairs)  24.2 us
    ppermute x14, waiting for transfers between devices, per_device(): tips[h][way] = lax.ppermute(tips[h][way], 'ctx', routes[way])  15.2 us
    ppermute x14, starting transfers between devices, per_device(): tips[h][way] = lax.ppermute(tips[h][way], 'ctx', routes[way])  14.3 us
    ppermute x2, waiting for transfers between devices, per_device(): found.append(lax.ppermute(sent[e], ('ctx', 'ch'), route))  14 us
    pallas_call x4, Pallas kernels, project(): pl.pallas_call(lambda *refs: project_kernel(count, m, last, *refs), grid_...  13.6 us
    all_to_all x1, waiting for transfers between devices, per_device(): packed = lax.all_to_all(packed, 'ctx', 0, 0)  9.2 us
    all_to_all x1, starting transfers between devices, per_device(): packed = lax.all_to_all(packed, 'ctx', 0, 0)  5.98 us
    ppermute x3, waiting for transfers between devices, per_device(): lax.ppermute(part, 'ch', [(d, d ^ b) for d in range(m)])  4.28 us
  transfers between devices with their start and end apart: 23, of which 16 were waited for; matrix products, arithmetic and copies ran while one was open for 0% of the time, Pallas kernels for 10%

profile of v8, /device:TPU:2, one launch (start us, length us, event | category | flops | bytes accessed | tf_op | source)
XLA Modules:
  0.0 117.2 jit_solution(14790956195024368974)
XLA Ops:
  0.0 2.8 %pack.1 = bf16[8,3,256,128]{3,2,1,0:T(8,128)(2,1)} custom-call(bf16[256,1024]{1,0:T(8,128)(2,1)} %outer_ref.1, bf16[256,1024]{1,0:T(8,128)(2,1)} %inner_ref.1, bf16[256,1024]{1,0:T(8,128)(2,1)} %values_ref.1, f32[256,1024]{1,0:T(8,128)} %filters_ref.1), custom_call_target="tpu_custom_call" | custom-call | flops 262144 | bytes 4194304 | tf_op jit(solution)/shard_map/pack/pallas_call | solution.py:40
  2.8 6.0 %all-to-all-start = ((bf16[8,3,256,128]{3,2,1,0:T(8,128)(2,1)}), bf16[8,3,256,128]{3,2,1,0:T(8,128)(2,1)S(1)}, u32[]{:S(2)}, u32[]{:S(2)}) async-start(bf16[8,3,256,128]{3,2,1,0:T(8,128)(2,1)} %pack.1), calls=%async_computation | async-start | bytes 3145728 | tf_op jit(solution)/shard_map/all_to_all | solution.py:226
  9.4 24.2 %collective-permute-done.1.refs_6_.refs_12_.refs_18_.refs_7_.refs_13_ = bf16[8,128,512]{2,1,0:T(8,128)(2,1)} collective-permute-done((bf16[8,128,512]{2,1,0:T(8,128)(2,1)S(1)}, bf16[8,128,512]{2,1,0:T(8,128)(2,1)}, u32[]{:S(2)}, u32[]{:S(2)}) %collective-permute-start.1) | collective-permute-done | bytes 1048608 | tf_op jit(solution)/shard_map/ppermute | solution.py:222
  33.7 2.8 %collective-permute-done.2.refs_7_.refs_13_.refs_19_.refs_8_.refs_14_ = bf16[8,128,512]{2,1,0:T(8,128)(2,1)} collective-permute-done((bf16[8,128,512]{2,1,0:T(8,128)(2,1)}, bf16[8,128,512]{2,1,0:T(8,128)(2,1)}, u32[]{:S(2)}, u32[]{:S(2)}) %collective-permute-start.2) | collective-permute-done | bytes 1048608 | tf_op jit(solution)/shard_map/ppermute | solution.py:223
  36.5 9.2 %all-to-all-done.refs_1_ = bf16[8,3,256,128]{3,2,1,0:T(8,128)(2,1)S(1)} async-done(((bf16[8,3,256,128]{3,2,1,0:T(8,128)(2,1)}), bf16[8,3,256,128]{3,2,1,0:T(8,128)(2,1)S(1)}, u32[]{:S(2)}, u32[]{:S(2)}) %all-to-all-start) | async-done | bytes 1572896 | tf_op jit(solution)/shard_map/all_to_all | solution.py:226
  45.8 3.4 %convolve.1 = (bf16[2,256,128]{2,1,0:T(8,128)(2,1)S(1)}, bf16[2,256,128]{2,1,0:T(8,128)(2,1)S(1)}, bf16[2,256,128]{2,1,0:T(8,128)(2,1)S(1)}, bf16[2,256,128]{2,1,0:T(8,128)(2,1)S(1)}) custom-call(s32[2]{0:T(128)S(1)} %pad_add_fusion.refs_0_, bf16[8,3,256,128]{3,2,1,0:T(8,128)(2,1)S(1)} %all-to-all-done.refs_1_, ...), custom_call_target="tpu_custom_call" | custom-call | flops 2147483648 | bytes 4194304 | tf_op jit(solution)/shard_map/convolve/pallas_call | solution.py:106
  51.2 2.0 %collective-permute-start.6 = (bf16[2,2,256,128]{3,2,1,0:T(8,128)(2,1)S(1)}, bf16[2,2,256,128]{3,2,1,0:T(8,128)(2,1)S(1)}, u32[]{:S(2)}, u32[]{:S(2)}) collective-permute-start(bf16[2,2,256,128]{3,2,1,0:T(8,128)(2,1)S(1)} %pad_maximum_fusion.refs_2_), channel_id=1, source_target_pairs={{8,0},{16,8},{24,16},{28,24},{20,28},{12,20},{4,12},{0,4},{9,1},{1... | collective-permute-start | bytes 786440 | tf_op jit(solution)/shard_map/ppermute | solution.py:252
  53.2 2.4 %collective-permute-done.8 = bf16[2,256,128]{2,1,0:T(8,128)(2,1)S(1)} collective-permute-done((bf16[2,256,128]{2,1,0:T(8,128)(2,1)S(1)}, bf16[2,256,128]{2,1,0:T(8,128)(2,1)S(1)}, u32[]{:S(2)}, u32[]{:S(2)}) %collective-permute-start.8) | collective-permute-done | bytes 131104 | tf_op jit(solution)/shard_map/ppermute | solution.py:231
  55.6 1.9 %collective-permute-done.9 = bf16[2,256,128]{2,1,0:T(8,128)(2,1)S(1)} collective-permute-done((bf16[2,256,128]{2,1,0:T(8,128)(2,1)S(1)}, bf16[2,256,128]{2,1,0:T(8,128)(2,1)S(1)}, u32[]{:S(2)}, u32[]{:S(2)}) %collective-permute-start.9) | collective-permute-done | bytes 131104 | tf_op jit(solution)/shard_map/ppermute | solution.py:231
  57.5 1.5 %collective-permute-start.11 = (bf16[2,2,256,128]{3,2,1,0:T(8,128)(2,1)S(1)}, bf16[2,2,256,128]{3,2,1,0:T(8,128)(2,1)S(1)}, u32[]{:S(2)}, u32[]{:S(2)}) collective-permute-start(bf16[2,2,256,128]{3,2,1,0:T(8,128)(2,1)S(1)} %pad_maximum_fusion.1.refs_3_), channel_id=1, source_target_pairs={{8,0},{16,8},{24,16},{28,24},{20,28},{12,20},{4,12},{0,4},{9,1},{1... | collective-permute-start | bytes 786440 | tf_op jit(solution)/shard_map/ppermute | solution.py:252
  60.0 1.7 %collective-permute-start.7 = (bf16[2,2,256,128]{3,2,1,0:T(8,128)(2,1)S(1)}, bf16[2,2,256,128]{3,2,1,0:T(8,128)(2,1)S(1)}, u32[]{:S(2)}, u32[]{:S(2)}) collective-permute-start(bf16[2,2,256,128]{3,2,1,0:T(8,128)(2,1)S(1)} %collective-permute-done.6.refs_14_), channel_id=1, source_target_pairs={{8,0},{16,8},{24,16},{28,24},{20,28},{12,20},{4,12},{0,4},{9,1},{1... | collective-permute-start | bytes 786440 | tf_op jit(solution)/shard_map/ppermute | solution.py:252
  61.8 4.9 %collective-permute-done.11.refs_15_ = bf16[2,2,256,128]{3,2,1,0:T(8,128)(2,1)S(1)} collective-permute-done((bf16[2,2,256,128]{3,2,1,0:T(8,128)(2,1)S(1)}, bf16[2,2,256,128]{3,2,1,0:T(8,128)(2,1)S(1)}, u32[]{:S(2)}, u32[]{:S(2)}) %collective-permute-start.11) | collective-permute-done | bytes 262176 | tf_op jit(solution)/shard_map/ppermute | solution.py:252
  66.7 1.4 %collective-permute-start.15 = (bf16[2,2,256,128]{3,2,1,0:T(8,128)(2,1)S(1)}, bf16[2,2,256,128]{3,2,1,0:T(8,128)(2,1)S(1)}, u32[]{:S(2)}, u32[]{:S(2)}) collective-permute-start(bf16[2,2,256,128]{3,2,1,0:T(8,128)(2,1)S(1)} %collective-permute-done.11.refs_15_), channel_id=1, source_target_pairs={{8,0},{16,8},{24,16},{28,24},{20,28},{12,20},{4,12},{0,4},{9,1},{1... | collective-permute-start | bytes 786440 | tf_op jit(solution)/shard_map/ppermute | solution.py:252
  68.8 4.5 %project.4.refs_2_ = f32[512,512]{1,0:T(8,128)} custom-call(s32[2]{0:T(128)} %copy-done.1, s32[24]{0:T(128)} %constant.52.clone.refs_1_, bf16[2,2,256,128]{3,2,1,0:T(8,128)(2,1)} %copy-done.8, bf16[2,2,256,128]{3,2,1,0:T(8,128)(2,1)} %copy-done.9, bf16[8,128,512]{2,1,0:T(8,128)(2,1)} %bitcast.10, ...), custom_call_target="tpu_custom_call" | custom-call | tf_op jit(solution)/shard_map/project/pallas_call | solution.py:176
  74.4 1.4 %collective-permute-start.13 = (bf16[2,2,256,128]{3,2,1,0:T(8,128)(2,1)S(1)}, bf16[2,2,256,128]{3,2,1,0:T(8,128)(2,1)S(1)}, u32[]{:S(2)}, u32[]{:S(2)}) collective-permute-start(bf16[2,2,256,128]{3,2,1,0:T(8,128)(2,1)S(1)} %collective-permute-done.7.refs_9_), channel_id=1, source_target_pairs={{8,0},{16,8},{24,16},{28,24},{20,28},{12,20},{4,12},{0,4},{9,1},{1... | collective-permute-start | bytes 786440 | tf_op jit(solution)/shard_map/ppermute | solution.py:252
  75.8 2.1 %collective-permute-done.15.refs_10_ = bf16[2,2,256,128]{3,2,1,0:T(8,128)(2,1)S(1)} collective-permute-done((bf16[2,2,256,128]{3,2,1,0:T(8,128)(2,1)S(1)}, bf16[2,2,256,128]{3,2,1,0:T(8,128)(2,1)S(1)}, u32[]{:S(2)}, u32[]{:S(2)}) %collective-permute-start.15) | collective-permute-done | bytes 262176 | tf_op jit(solution)/shard_map/ppermute | solution.py:252
  80.1 4.2 %project.5.refs_2_ = f32[512,512]{1,0:T(8,128)} custom-call(s32[2]{0:T(128)} %copy-done.1, s32[16]{0:T(128)} %constant.53.clone.refs_1_, f32[512,512]{1,0:T(8,128)} %project.4.refs_2_, bf16[2,2,256,128]{3,2,1,0:T(8,128)(2,1)} %copy-done.14, bf16[2,2,256,128]{3,2,1,0:T(8,128)(2,1)} %copy-done.15, bf16[8,128,512]{2,1,0:T(8,128)(2,1)} %bitcast.13, ...), custom_call_target="tpu_custom_call" | custom-call | tf_op jit(solution)/shard_map/project/pallas_call | solution.py:176
  85.6 3.2 %collective-permute-done.17.refs_10_ = bf16[2,2,256,128]{3,2,1,0:T(8,128)(2,1)S(1)} collective-permute-done((bf16[2,2,256,128]{3,2,1,0:T(8,128)(2,1)S(1)}, bf16[2,2,256,128]{3,2,1,0:T(8,128)(2,1)S(1)}, u32[]{:S(2)}, u32[]{:S(2)}) %collective-permute-start.17) | collective-permute-done | bytes 262176 | tf_op jit(solution)/shard_map/ppermute | solution.py:252
  90.6 2.9 %project.6.refs_2_ = f32[512,512]{1,0:T(8,128)S(1)} custom-call(s32[2]{0:T(128)S(1)} %copy-done.2, s32[16]{0:T(128)S(1)} %copy-done.4, f32[512,512]{1,0:T(8,128)} %project.5.refs_2_, bf16[2,2,256,128]{3,2,1,0:T(8,128)(2,1)S(1)} %collective-permute-done.12.refs_3_, bf16[2,2,256,128]{3,2,1,0:T(8,128)(2,1)S(1)} %collective-permute-done.16.refs_4_, ...), custom_call_target="tpu_custom_call" | custom-call | tf_op jit(solution)/shard_map/project/pallas_call | solution.py:176
  93.5 2.1 %collective-permute-done.18.refs_3_ = bf16[2,2,256,128]{3,2,1,0:T(8,128)(2,1)S(1)} collective-permute-done((bf16[2,2,256,128]{3,2,1,0:T(8,128)(2,1)S(1)}, bf16[2,2,256,128]{3,2,1,0:T(8,128)(2,1)S(1)}, u32[]{:S(2)}, u32[]{:S(2)}) %collective-permute-start.18) | collective-permute-done | bytes 262176 | tf_op jit(solution)/shard_map/ppermute | solution.py:252
  96.7 2.1 %project.7 = (bf16[256,512]{1,0:T(8,128)(2,1)S(1)}, bf16[256,512]{1,0:T(8,128)(2,1)S(1)}) custom-call(s32[2]{0:T(128)S(1)} %copy-done.2, s32[8]{0:T(128)S(1)} %copy-done.3, f32[512,512]{1,0:T(8,128)S(1)} %project.6.refs_2_, bf16[2,2,256,128]{3,2,1,0:T(8,128)(2,1)S(1)} %collective-permute-done.18.refs_3_, ...), custom_call_target="tpu_custom_call" | custom-call | tf_op jit(solution)/shard_map/project/pallas_call | solution.py:176
  98.9 3.3 %collective-permute-start.20 = (bf16[256,512]{1,0:T(8,128)(2,1)S(1)}, bf16[256,512]{1,0:T(8,128)(2,1)S(1)}, u32[]{:S(2)}, u32[]{:S(2)}) collective-permute-start(bf16[256,512]{1,0:T(8,128)(2,1)S(1)} %get-tuple-element.35), channel_id=1, source_target_pairs={{0,0},{1,16},{2,4},{3,20},{4,8},{5,24},{6,12},{7,28},{8,1},{9,17},... | collective-permute-start | bytes 786440 | tf_op jit(solution)/shard_map/ppermute | solution.py:266
  102.3 12.0 %collective-permute-done.20 = bf16[256,512]{1,0:T(8,128)(2,1)S(1)} collective-permute-done((bf16[256,512]{1,0:T(8,128)(2,1)S(1)}, bf16[256,512]{1,0:T(8,128)(2,1)S(1)}, u32[]{:S(2)}, u32[]{:S(2)}) %collective-permute-start.20) | collective-permute-done | bytes 262176 | tf_op jit(solution)/shard_map/ppermute | solution.py:266
  114.2 2.0 %collective-permute-done.21 = bf16[256,512]{1,0:T(8,128)(2,1)S(1)} collective-permute-done((bf16[256,512]{1,0:T(8,128)(2,1)S(1)}, bf16[256,512]{1,0:T(8,128)(2,1)S(1)}, u32[]{:S(2)}, u32[]{:S(2)}) %collective-permute-start.21) | collective-permute-done | bytes 262176 | tf_op jit(solution)/shard_map/ppermute | solution.py:266
  (69 shorter events, 13.1 us)
Async XLA Ops:
  2.8 43.0 %copy-start.6 = (bf16[256,512]{1,0:T(8,128)(2,1)S(1)}, bf16[256,512]{1,0:T(8,128)(2,1)}, u32[]{:S(2)}) copy-start(bf16[256,512]{1,0:T(8,128)(2,1)} %constant.51.clone.refs_4_) | copy-start | bytes 786436
  2.8 43.0 %all-to-all-start = ((bf16[8,3,256,128]{3,2,1,0:T(8,128)(2,1)}), bf16[8,3,256,128]{3,2,1,0:T(8,128)(2,1)S(1)}, u32[]{:S(2)}, u32[]{:S(2)}) async-start(bf16[8,3,256,128]{3,2,1,0:T(8,128)(2,1)} %pack.1), calls=%async_computation | async-start | bytes 3145728 | tf_op jit(solution)/shard_map/all_to_all | solution.py:226
  8.8 24.8 %collective-permute-start.1 = (bf16[8,128,512]{2,1,0:T(8,128)(2,1)S(1)}, bf16[8,128,512]{2,1,0:T(8,128)(2,1)}, u32[]{:S(2)}, u32[]{:S(2)}) collective-permute-start(bf16[8,128,512]{2,1,0:T(8,128)(2,1)S(1)} %bitcast.18), channel_id=1, source_target_pairs={{0,2},{1,3},{2,0},{3,1},{4,6},{5,7},{6,4},{7,5},{8,10},{9,11},{10,... | collective-permute-start | bytes 3145736 | tf_op jit(solution)/shard_map/ppermute | solution.py:222
  9.4 24.3 %collective-permute-start = (bf16[8,128,512]{2,1,0:T(8,128)(2,1)S(1)}, bf16[8,128,512]{2,1,0:T(8,128)(2,1)}, u32[]{:S(2)}, u32[]{:S(2)}) collective-permute-start(bf16[8,128,512]{2,1,0:T(8,128)(2,1)S(1)} %bitcast.19), channel_id=1, source_target_pairs={{0,1},{1,0},{2,3},{3,2},{4,5},{5,4},{6,7},{7,6},{8,9},{9,8},{10,11... | collective-permute-start | bytes 3145736 | tf_op jit(solution)/shard_map/ppermute | solution.py:219
  33.5 3.0 %collective-permute-start.2 = (bf16[8,128,512]{2,1,0:T(8,128)(2,1)}, bf16[8,128,512]{2,1,0:T(8,128)(2,1)}, u32[]{:S(2)}, u32[]{:S(2)}) collective-permute-start(bf16[8,128,512]{2,1,0:T(8,128)(2,1)} %collective-permute-done.1.refs_6_.refs_12_.refs_18_.refs_7_.refs_13_), channel_id=1, source_target_pairs={{0,1},{1,0},{2,3},{3,2},{4,5},{5,4},{6,7},{7,6},{8,9},{9,8},{10,11... | collective-permute-start | bytes 3145736 | tf_op jit(solution)/shard_map/ppermute | solution.py:223
  49.1 1.9 %collective-permute-start.3 = (bf16[2,256,128]{2,1,0:T(8,128)(2,1)S(1)}, bf16[2,256,128]{2,1,0:T(8,128)(2,1)S(1)}, u32[]{:S(2)}, u32[]{:S(2)}) collective-permute-start(bf16[2,256,128]{2,1,0:T(8,128)(2,1)S(1)} %get-tuple-element.23), channel_id=1, source_target_pairs={{0,1},{1,0},{2,3},{3,2},{4,5},{5,4},{6,7},{7,6},{8,9},{9,8},{10,11... | collective-permute-start | bytes 393224 | tf_op jit(solution)/shard_map/ppermute | solution.py:231
  49.2 6.4 %collective-permute-start.8 = (bf16[2,256,128]{2,1,0:T(8,128)(2,1)S(1)}, bf16[2,256,128]{2,1,0:T(8,128)(2,1)S(1)}, u32[]{:S(2)}, u32[]{:S(2)}) collective-permute-start(bf16[2,256,128]{2,1,0:T(8,128)(2,1)S(1)} %get-tuple-element.24), channel_id=1, source_target_pairs={{0,2},{1,3},{2,0},{3,1},{4,6},{5,7},{6,4},{7,5},{8,10},{9,11},{10,... | collective-permute-start | bytes 393224 | tf_op jit(solution)/shard_map/ppermute | solution.py:231
  49.8 7.7 %collective-permute-start.9 = (bf16[2,256,128]{2,1,0:T(8,128)(2,1)S(1)}, bf16[2,256,128]{2,1,0:T(8,128)(2,1)S(1)}, u32[]{:S(2)}, u32[]{:S(2)}) collective-permute-start(bf16[2,256,128]{2,1,0:T(8,128)(2,1)S(1)} %get-tuple-element.25), channel_id=1, source_target_pairs={{0,3},{1,2},{2,1},{3,0},{4,7},{5,6},{6,5},{7,4},{8,11},{9,10},{10,... | collective-permute-start | bytes 393224 | tf_op jit(solution)/shard_map/ppermute | solution.py:231
  51.1 8.6 %collective-permute-start.4 = (bf16[2,2,256,128]{3,2,1,0:T(8,128)(2,1)S(1)}, bf16[2,2,256,128]{3,2,1,0:T(8,128)(2,1)S(1)}, u32[]{:S(2)}, u32[]{:S(2)}) collective-permute-start(bf16[2,2,256,128]{3,2,1,0:T(8,128)(2,1)S(1)} %pad_maximum_fusion.refs_2_), channel_id=1, source_target_pairs={{8,16},{16,24},{24,28},{28,20},{20,12},{12,4},{4,0},{0,8},{9,17},{... | collective-permute-start | bytes 786440 | tf_op jit(solution)/shard_map/ppermute | solution.py:252
  51.2 8.8 %collective-permute-start.6 = (bf16[2,2,256,128]{3,2,1,0:T(8,128)(2,1)S(1)}, bf16[2,2,256,128]{3,2,1,0:T(8,128)(2,1)S(1)}, u32[]{:S(2)}, u32[]{:S(2)}) collective-permute-start(bf16[2,2,256,128]{3,2,1,0:T(8,128)(2,1)S(1)} %pad_maximum_fusion.refs_2_), channel_id=1, source_target_pairs={{8,0},{16,8},{24,16},{28,24},{20,28},{12,20},{4,12},{0,4},{9,1},{1... | collective-permute-start | bytes 786440 | tf_op jit(solution)/shard_map/ppermute | solution.py:252
  57.5 9.1 %collective-permute-start.11 = (bf16[2,2,256,128]{3,2,1,0:T(8,128)(2,1)S(1)}, bf16[2,2,256,128]{3,2,1,0:T(8,128)(2,1)S(1)}, u32[]{:S(2)}, u32[]{:S(2)}) collective-permute-start(bf16[2,2,256,128]{3,2,1,0:T(8,128)(2,1)S(1)} %pad_maximum_fusion.1.refs_3_), channel_id=1, source_target_pairs={{8,0},{16,8},{24,16},{28,24},{20,28},{12,20},{4,12},{0,4},{9,1},{1... | collective-permute-start | bytes 786440 | tf_op jit(solution)/shard_map/ppermute | solution.py:252
  59.0 9.1 %collective-permute-start.10 = (bf16[2,2,256,128]{3,2,1,0:T(8,128)(2,1)S(1)}, bf16[2,2,256,128]{3,2,1,0:T(8,128)(2,1)S(1)}, u32[]{:S(2)}, u32[]{:S(2)}) collective-permute-start(bf16[2,2,256,128]{3,2,1,0:T(8,128)(2,1)S(1)} %pad_maximum_fusion.1.refs_3_), channel_id=1, source_target_pairs={{8,16},{16,24},{24,28},{28,20},{20,12},{12,4},{4,0},{0,8},{9,17},{... | collective-permute-start | bytes 786440 | tf_op jit(solution)/shard_map/ppermute | solution.py:252
  59.7 14.0 %collective-permute-start.5 = (bf16[2,2,256,128]{3,2,1,0:T(8,128)(2,1)S(1)}, bf16[2,2,256,128]{3,2,1,0:T(8,128)(2,1)S(1)}, u32[]{:S(2)}, u32[]{:S(2)}) collective-permute-start(bf16[2,2,256,128]{3,2,1,0:T(8,128)(2,1)S(1)} %collective-permute-done.4.refs_8_), channel_id=1, source_target_pairs={{8,16},{16,24},{24,28},{28,20},{20,12},{12,4},{4,0},{0,8},{9,17},{... | collective-permute-start | bytes 786440 | tf_op jit(solution)/shard_map/ppermute | solution.py:252
  60.0 13.7 %collective-permute-start.7 = (bf16[2,2,256,128]{3,2,1,0:T(8,128)(2,1)S(1)}, bf16[2,2,256,128]{3,2,1,0:T(8,128)(2,1)S(1)}, u32[]{:S(2)}, u32[]{:S(2)}) collective-permute-start(bf16[2,2,256,128]{3,2,1,0:T(8,128)(2,1)S(1)} %collective-permute-done.6.refs_14_), channel_id=1, source_target_pairs={{8,0},{16,8},{24,16},{28,24},{20,28},{12,20},{4,12},{0,4},{9,1},{1... | collective-permute-start | bytes 786440 | tf_op jit(solution)/shard_map/ppermute | solution.py:252
  66.7 11.2 %collective-permute-start.15 = (bf16[2,2,256,128]{3,2,1,0:T(8,128)(2,1)S(1)}, bf16[2,2,256,128]{3,2,1,0:T(8,128)(2,1)S(1)}, u32[]{:S(2)}, u32[]{:S(2)}) collective-permute-start(bf16[2,2,256,128]{3,2,1,0:T(8,128)(2,1)S(1)} %collective-permute-done.11.refs_15_), channel_id=1, source_target_pairs={{8,0},{16,8},{24,16},{28,24},{20,28},{12,20},{4,12},{0,4},{9,1},{1... | collective-permute-start | bytes 786440 | tf_op jit(solution)/shard_map/ppermute | solution.py:252
  68.1 11.2 %collective-permute-start.14 = (bf16[2,2,256,128]{3,2,1,0:T(8,128)(2,1)S(1)}, bf16[2,2,256,128]{3,2,1,0:T(8,128)(2,1)S(1)}, u32[]{:S(2)}, u32[]{:S(2)}) collective-permute-start(bf16[2,2,256,128]{3,2,1,0:T(8,128)(2,1)S(1)} %collective-permute-done.10.refs_9_), channel_id=1, source_target_pairs={{8,16},{16,24},{24,28},{28,20},{20,12},{12,4},{4,0},{0,8},{9,17},{... | collective-permute-start | bytes 786440 | tf_op jit(solution)/shard_map/ppermute | solution.py:252
  73.7 11.2 %collective-permute-start.12 = (bf16[2,2,256,128]{3,2,1,0:T(8,128)(2,1)S(1)}, bf16[2,2,256,128]{3,2,1,0:T(8,128)(2,1)S(1)}, u32[]{:S(2)}, u32[]{:S(2)}) collective-permute-start(bf16[2,2,256,128]{3,2,1,0:T(8,128)(2,1)S(1)} %collective-permute-done.5.refs_3_), channel_id=1, source_target_pairs={{8,16},{16,24},{24,28},{28,20},{20,12},{12,4},{4,0},{0,8},{9,17},{... | collective-permute-start | bytes 786440 | tf_op jit(solution)/shard_map/ppermute | solution.py:252
  74.4 10.6 %collective-permute-start.13 = (bf16[2,2,256,128]{3,2,1,0:T(8,128)(2,1)S(1)}, bf16[2,2,256,128]{3,2,1,0:T(8,128)(2,1)S(1)}, u32[]{:S(2)}, u32[]{:S(2)}) collective-permute-start(bf16[2,2,256,128]{3,2,1,0:T(8,128)(2,1)S(1)} %collective-permute-done.7.refs_9_), channel_id=1, source_target_pairs={{8,0},{16,8},{24,16},{28,24},{20,28},{12,20},{4,12},{0,4},{9,1},{1... | collective-permute-start | bytes 786440 | tf_op jit(solution)/shard_map/ppermute | solution.py:252
  77.9 10.9 %collective-permute-start.17 = (bf16[2,2,256,128]{3,2,1,0:T(8,128)(2,1)S(1)}, bf16[2,2,256,128]{3,2,1,0:T(8,128)(2,1)S(1)}, u32[]{:S(2)}, u32[]{:S(2)}) collective-permute-start(bf16[2,2,256,128]{3,2,1,0:T(8,128)(2,1)S(1)} %collective-permute-done.15.refs_10_), channel_id=1, source_target_pairs={{8,0},{16,8},{24,16},{28,24},{20,28},{12,20},{4,12},{0,4},{9,1},{1... | collective-permute-start | bytes 786440 | tf_op jit(solution)/shard_map/ppermute | solution.py:252
  79.4 11.2 %collective-permute-start.16 = (bf16[2,2,256,128]{3,2,1,0:T(8,128)(2,1)S(1)}, bf16[2,2,256,128]{3,2,1,0:T(8,128)(2,1)S(1)}, u32[]{:S(2)}, u32[]{:S(2)}) collective-permute-start(bf16[2,2,256,128]{3,2,1,0:T(8,128)(2,1)S(1)} %collective-permute-done.14.refs_4_), channel_id=1, source_target_pairs={{8,16},{16,24},{24,28},{28,20},{20,12},{12,4},{4,0},{0,8},{9,17},{... | collective-permute-start | bytes 786440 | tf_op jit(solution)/shard_map/ppermute | solution.py:252
  85.0 10.6 %collective-permute-start.18 = (bf16[2,2,256,128]{3,2,1,0:T(8,128)(2,1)S(1)}, bf16[2,2,256,128]{3,2,1,0:T(8,128)(2,1)S(1)}, u32[]{:S(2)}, u32[]{:S(2)}) collective-permute-start(bf16[2,2,256,128]{3,2,1,0:T(8,128)(2,1)S(1)} %collective-permute-done.12.refs_3_), channel_id=1, source_target_pairs={{8,16},{16,24},{24,28},{28,20},{20,12},{12,4},{4,0},{0,8},{9,17},{... | collective-permute-start | bytes 786440 | tf_op jit(solution)/shard_map/ppermute | solution.py:252
  88.8 7.9 %collective-permute-start.19 = (bf16[2,2,256,128]{3,2,1,0:T(8,128)(2,1)S(1)}, bf16[2,2,256,128]{3,2,1,0:T(8,128)(2,1)S(1)}, u32[]{:S(2)}, u32[]{:S(2)}) collective-permute-start(bf16[2,2,256,128]{3,2,1,0:T(8,128)(2,1)S(1)} %collective-permute-done.17.refs_10_), channel_id=1, source_target_pairs={{8,0},{16,8},{24,16},{28,24},{20,28},{12,20},{4,12},{0,4},{9,1},{1... | collective-permute-start | bytes 786440 | tf_op jit(solution)/shard_map/ppermute | solution.py:252
  98.9 15.4 %collective-permute-start.20 = (bf16[256,512]{1,0:T(8,128)(2,1)S(1)}, bf16[256,512]{1,0:T(8,128)(2,1)S(1)}, u32[]{:S(2)}, u32[]{:S(2)}) collective-permute-start(bf16[256,512]{1,0:T(8,128)(2,1)S(1)} %get-tuple-element.35), channel_id=1, source_target_pairs={{0,0},{1,16},{2,4},{3,20},{4,8},{5,24},{6,12},{7,28},{8,1},{9,17},... | collective-permute-start | bytes 786440 | tf_op jit(solution)/shard_map/ppermute | solution.py:266
  102.2 14.1 %collective-permute-start.21 = (bf16[256,512]{1,0:T(8,128)(2,1)S(1)}, bf16[256,512]{1,0:T(8,128)(2,1)S(1)}, u32[]{:S(2)}, u32[]{:S(2)}) collective-permute-start(bf16[256,512]{1,0:T(8,128)(2,1)S(1)} %get-tuple-element.36), channel_id=1, source_target_pairs={{0,8},{1,24},{2,12},{3,28},{4,0},{5,16},{6,4},{7,20},{8,9},{9,25},... | collective-permute-start | bytes 786440 | tf_op jit(solution)/shard_map/ppermute | solution.py:266
  (17 other events, 209.6 us)

commit v9 on v5

--- a/solution.py
+++ b/solution.py
@@ -150,7 +150,7 @@
         refs[0][...] = total
 
 
-def project(pieces, owners, total, here, weights, last=False, grant=60):
+def project(pieces, owners, total, here, weights, last=False, grant=51):
     m, count = len(weights), len(pieces)
     _, chans, columns = weights[0].shape
     block = pieces[0][0].shape[-2]

time: 118 us -> 118 us (level)
  Pallas kernels: 20 us -> 17.2 us
  local copies, waits for them, and re-layouts: 0.3 us -> 2.06 us
    pallas_call x4, Pallas kernels: 13.6 us -> 10.8 us  [project(): pl.pallas_call(lambda *refs: project_kernel(count, m, last, *refs), grid_...]
    unnamed x36 -> x20, local copies, waits for them, and re-layouts: 0.22 us -> 1.98 us
  transfers between devices with their start and end apart: 23 -> 23, of which waited for: 16 -> 16; matrix products, arithmetic and copies ran while one was open for 0% -> 0% of each run, Pallas kernels for 10% -> 7%
where the time goes in v9:
time: 118 us; the launch traced here: 117 us
  waiting for transfers between devices  70.7 us (60%)
  starting transfers between devices  26.3 us (22%)
  Pallas kernels  17.2 us (15%)
  local copies, waits for them, and re-layouts  2.06 us (2%)
    ppermute x1, waiting for transfers between devices, per_device(): far = lax.ppermute(even, 'ch', pairs)  24.2 us
    ppermute x14, waiting for transfers between devices, per_device(): tips[h][way] = lax.ppermute(tips[h][way], 'ctx', routes[way])  16.4 us
    ppermute x14, starting transfers between devices, per_device(): tips[h][way] = lax.ppermute(tips[h][way], 'ctx', routes[way])  14.3 us
    ppermute x2, waiting for transfers between devices, per_device(): found.append(lax.ppermute(sent[e], ('ctx', 'ch'), route))  13.9 us
    pallas_call x4, Pallas kernels, project(): pl.pallas_call(lambda *refs: project_kernel(count, m, last, *refs), grid_...  10.8 us
    all_to_all x1, waiting for transfers between devices, per_device(): packed = lax.all_to_all(packed, 'ctx', 0, 0)  9.2 us
    all_to_all x1, starting transfers between devices, per_device(): packed = lax.all_to_all(packed, 'ctx', 0, 0)  5.98 us
    ppermute x3, waiting for transfers between devices, per_device(): lax.ppermute(part, 'ch', [(d, d ^ b) for d in range(m)])  4.29 us
  transfers between devices with their start and end apart: 23, of which 16 were waited for; matrix products, arithmetic and copies ran while one was open for 0% of the time, Pallas kernels for 7%

profile of v9, /device:TPU:2, one launch (start us, length us, event | category | flops | bytes accessed | tf_op | source)
XLA Modules:
  0.0 117.5 jit_solution(4535493200249019991)
XLA Ops:
  0.0 2.7 %pack.1 = bf16[8,3,256,128]{3,2,1,0:T(8,128)(2,1)} custom-call(bf16[256,1024]{1,0:T(8,128)(2,1)} %outer_ref.1, bf16[256,1024]{1,0:T(8,128)(2,1)} %inner_ref.1, bf16[256,1024]{1,0:T(8,128)(2,1)} %values_ref.1, f32[256,1024]{1,0:T(8,128)} %filters_ref.1), custom_call_target="tpu_custom_call" | custom-call | flops 262144 | bytes 4194304 | tf_op jit(solution)/shard_map/pack/pallas_call | solution.py:40
  2.8 6.0 %all-to-all-start = ((bf16[8,3,256,128]{3,2,1,0:T(8,128)(2,1)}), bf16[8,3,256,128]{3,2,1,0:T(8,128)(2,1)S(1)}, u32[]{:S(2)}, u32[]{:S(2)}) async-start(bf16[8,3,256,128]{3,2,1,0:T(8,128)(2,1)} %pack.1), calls=%async_computation | async-start | bytes 3145728 | tf_op jit(solution)/shard_map/all_to_all | solution.py:226
  9.3 24.2 %collective-permute-done.1.refs_6_.refs_12_.refs_18_.refs_7_.refs_13_ = bf16[8,128,512]{2,1,0:T(8,128)(2,1)} collective-permute-done((bf16[8,128,512]{2,1,0:T(8,128)(2,1)S(1)}, bf16[8,128,512]{2,1,0:T(8,128)(2,1)}, u32[]{:S(2)}, u32[]{:S(2)}) %collective-permute-start.1) | collective-permute-done | bytes 1048608 | tf_op jit(solution)/shard_map/ppermute | solution.py:222
  33.7 2.8 %collective-permute-done.2.refs_7_.refs_13_.refs_19_.refs_8_.refs_14_ = bf16[8,128,512]{2,1,0:T(8,128)(2,1)} collective-permute-done((bf16[8,128,512]{2,1,0:T(8,128)(2,1)}, bf16[8,128,512]{2,1,0:T(8,128)(2,1)}, u32[]{:S(2)}, u32[]{:S(2)}) %collective-permute-start.2) | collective-permute-done | bytes 1048608 | tf_op jit(solution)/shard_map/ppermute | solution.py:223
  36.5 9.2 %all-to-all-done.refs_1_ = bf16[8,3,256,128]{3,2,1,0:T(8,128)(2,1)S(1)} async-done(((bf16[8,3,256,128]{3,2,1,0:T(8,128)(2,1)}), bf16[8,3,256,128]{3,2,1,0:T(8,128)(2,1)S(1)}, u32[]{:S(2)}, u32[]{:S(2)}) %all-to-all-start) | async-done | bytes 1572896 | tf_op jit(solution)/shard_map/all_to_all | solution.py:226
  45.7 3.6 %convolve.1 = (bf16[2,256,128]{2,1,0:T(8,128)(2,1)S(1)}, bf16[2,256,128]{2,1,0:T(8,128)(2,1)S(1)}, bf16[2,256,128]{2,1,0:T(8,128)(2,1)S(1)}, bf16[2,256,128]{2,1,0:T(8,128)(2,1)S(1)}) custom-call(s32[2]{0:T(128)S(1)} %pad_add_fusion.refs_0_, bf16[8,3,256,128]{3,2,1,0:T(8,128)(2,1)S(1)} %all-to-all-done.refs_1_, ...), custom_call_target="tpu_custom_call" | custom-call | flops 2147483648 | bytes 4194304 | tf_op jit(solution)/shard_map/convolve/pallas_call | solution.py:106
  51.4 2.0 %collective-permute-start.6 = (bf16[2,2,256,128]{3,2,1,0:T(8,128)(2,1)S(1)}, bf16[2,2,256,128]{3,2,1,0:T(8,128)(2,1)S(1)}, u32[]{:S(2)}, u32[]{:S(2)}) collective-permute-start(bf16[2,2,256,128]{3,2,1,0:T(8,128)(2,1)S(1)} %pad_maximum_fusion.refs_2_), channel_id=1, source_target_pairs={{8,0},{16,8},{24,16},{28,24},{20,28},{12,20},{4,12},{0,4},{9,1},{1... | collective-permute-start | bytes 786440 | tf_op jit(solution)/shard_map/ppermute | solution.py:252
  53.4 2.4 %collective-permute-done.8 = bf16[2,256,128]{2,1,0:T(8,128)(2,1)S(1)} collective-permute-done((bf16[2,256,128]{2,1,0:T(8,128)(2,1)S(1)}, bf16[2,256,128]{2,1,0:T(8,128)(2,1)S(1)}, u32[]{:S(2)}, u32[]{:S(2)}) %collective-permute-start.8) | collective-permute-done | bytes 131104 | tf_op jit(solution)/shard_map/ppermute | solution.py:231
  55.8 1.9 %collective-permute-done.9 = bf16[2,256,128]{2,1,0:T(8,128)(2,1)S(1)} collective-permute-done((bf16[2,256,128]{2,1,0:T(8,128)(2,1)S(1)}, bf16[2,256,128]{2,1,0:T(8,128)(2,1)S(1)}, u32[]{:S(2)}, u32[]{:S(2)}) %collective-permute-start.9) | collective-permute-done | bytes 131104 | tf_op jit(solution)/shard_map/ppermute | solution.py:231
  57.8 1.5 %collective-permute-start.11 = (bf16[2,2,256,128]{3,2,1,0:T(8,128)(2,1)S(1)}, bf16[2,2,256,128]{3,2,1,0:T(8,128)(2,1)S(1)}, u32[]{:S(2)}, u32[]{:S(2)}) collective-permute-start(bf16[2,2,256,128]{3,2,1,0:T(8,128)(2,1)S(1)} %pad_maximum_fusion.1.refs_3_), channel_id=1, source_target_pairs={{8,0},{16,8},{24,16},{28,24},{20,28},{12,20},{4,12},{0,4},{9,1},{1... | collective-permute-start | bytes 786440 | tf_op jit(solution)/shard_map/ppermute | solution.py:252
  60.2 1.7 %collective-permute-start.7 = (bf16[2,2,256,128]{3,2,1,0:T(8,128)(2,1)S(1)}, bf16[2,2,256,128]{3,2,1,0:T(8,128)(2,1)S(1)}, u32[]{:S(2)}, u32[]{:S(2)}) collective-permute-start(bf16[2,2,256,128]{3,2,1,0:T(8,128)(2,1)S(1)} %collective-permute-done.6.refs_14_), channel_id=1, source_target_pairs={{8,0},{16,8},{24,16},{28,24},{20,28},{12,20},{4,12},{0,4},{9,1},{1... | collective-permute-start | bytes 786440 | tf_op jit(solution)/shard_map/ppermute | solution.py:252
  62.0 4.9 %collective-permute-done.11.refs_15_ = bf16[2,2,256,128]{3,2,1,0:T(8,128)(2,1)S(1)} collective-permute-done((bf16[2,2,256,128]{3,2,1,0:T(8,128)(2,1)S(1)}, bf16[2,2,256,128]{3,2,1,0:T(8,128)(2,1)S(1)}, u32[]{:S(2)}, u32[]{:S(2)}) %collective-permute-start.11) | collective-permute-done | bytes 262176 | tf_op jit(solution)/shard_map/ppermute | solution.py:252
  66.9 1.4 %collective-permute-start.15 = (bf16[2,2,256,128]{3,2,1,0:T(8,128)(2,1)S(1)}, bf16[2,2,256,128]{3,2,1,0:T(8,128)(2,1)S(1)}, u32[]{:S(2)}, u32[]{:S(2)}) collective-permute-start(bf16[2,2,256,128]{3,2,1,0:T(8,128)(2,1)S(1)} %collective-permute-done.11.refs_15_), channel_id=1, source_target_pairs={{8,0},{16,8},{24,16},{28,24},{20,28},{12,20},{4,12},{0,4},{9,1},{1... | collective-permute-start | bytes 786440 | tf_op jit(solution)/shard_map/ppermute | solution.py:252
  69.0 3.0 %project.4.refs_2_ = f32[512,512]{1,0:T(8,128)S(1)} custom-call(s32[2]{0:T(128)S(1)} %pad_add_fusion.refs_0_, s32[24]{0:T(128)S(1)} %copy-done.6, bf16[2,2,256,128]{3,2,1,0:T(8,128)(2,1)S(1)} %pad_maximum_fusion.refs_2_, bf16[2,2,256,128]{3,2,1,0:T(8,128)(2,1)S(1)} %pad_maximum_fusion.1.refs_3_, bf16[8,128,512]{2,1,0:T(8,128)(2,1)} %bitcast.10, ...), custom_call_target="tpu_custom_call" | custom-call | tf_op jit(solution)/shard_map/project/pallas_call | solution.py:176
  74.6 1.4 %collective-permute-start.13 = (bf16[2,2,256,128]{3,2,1,0:T(8,128)(2,1)S(1)}, bf16[2,2,256,128]{3,2,1,0:T(8,128)(2,1)S(1)}, u32[]{:S(2)}, u32[]{:S(2)}) collective-permute-start(bf16[2,2,256,128]{3,2,1,0:T(8,128)(2,1)S(1)} %collective-permute-done.7.refs_9_), channel_id=1, source_target_pairs={{8,0},{16,8},{24,16},{28,24},{20,28},{12,20},{4,12},{0,4},{9,1},{1... | collective-permute-start | bytes 786440 | tf_op jit(solution)/shard_map/ppermute | solution.py:252
  76.0 2.1 %collective-permute-done.15.refs_10_ = bf16[2,2,256,128]{3,2,1,0:T(8,128)(2,1)S(1)} collective-permute-done((bf16[2,2,256,128]{3,2,1,0:T(8,128)(2,1)S(1)}, bf16[2,2,256,128]{3,2,1,0:T(8,128)(2,1)S(1)}, u32[]{:S(2)}, u32[]{:S(2)}) %collective-permute-start.15) | collective-permute-done | bytes 262176 | tf_op jit(solution)/shard_map/ppermute | solution.py:252
  80.2 2.9 %project.5.refs_2_ = f32[512,512]{1,0:T(8,128)S(1)} custom-call(s32[2]{0:T(128)S(1)} %pad_add_fusion.refs_0_, s32[16]{0:T(128)S(1)} %copy-done.5, f32[512,512]{1,0:T(8,128)} %copy-done.2, bf16[2,2,256,128]{3,2,1,0:T(8,128)(2,1)S(1)} %collective-permute-done.5.refs_3_, bf16[2,2,256,128]{3,2,1,0:T(8,128)(2,1)S(1)} %collective-permute-done.14.refs_4_, ...), custom_call_target="tpu_custom_call" | custom-call | tf_op jit(solution)/shard_map/project/pallas_call | solution.py:176
  85.8 3.2 %collective-permute-done.17.refs_10_ = bf16[2,2,256,128]{3,2,1,0:T(8,128)(2,1)S(1)} collective-permute-done((bf16[2,2,256,128]{3,2,1,0:T(8,128)(2,1)S(1)}, bf16[2,2,256,128]{3,2,1,0:T(8,128)(2,1)S(1)}, u32[]{:S(2)}, u32[]{:S(2)}) %collective-permute-start.17) | collective-permute-done | bytes 262176 | tf_op jit(solution)/shard_map/ppermute | solution.py:252
  90.8 2.9 %project.6.refs_2_ = f32[512,512]{1,0:T(8,128)S(1)} custom-call(s32[2]{0:T(128)S(1)} %pad_add_fusion.refs_0_, s32[16]{0:T(128)S(1)} %copy-done.4, f32[512,512]{1,0:T(8,128)} %copy-done.1, bf16[2,2,256,128]{3,2,1,0:T(8,128)(2,1)S(1)} %collective-permute-done.12.refs_3_, bf16[2,2,256,128]{3,2,1,0:T(8,128)(2,1)S(1)} %collective-permute-done.16.refs_4_, ...), custom_call_target="tpu_custom_call" | custom-call | tf_op jit(solution)/shard_map/project/pallas_call | solution.py:176
  93.7 2.1 %collective-permute-done.18.refs_3_ = bf16[2,2,256,128]{3,2,1,0:T(8,128)(2,1)S(1)} collective-permute-done((bf16[2,2,256,128]{3,2,1,0:T(8,128)(2,1)S(1)}, bf16[2,2,256,128]{3,2,1,0:T(8,128)(2,1)S(1)}, u32[]{:S(2)}, u32[]{:S(2)}) %collective-permute-start.18) | collective-permute-done | bytes 262176 | tf_op jit(solution)/shard_map/ppermute | solution.py:252
  97.0 2.1 %project.7 = (bf16[256,512]{1,0:T(8,128)(2,1)S(1)}, bf16[256,512]{1,0:T(8,128)(2,1)S(1)}) custom-call(s32[2]{0:T(128)S(1)} %pad_add_fusion.refs_0_, s32[8]{0:T(128)S(1)} %copy-done.3, f32[512,512]{1,0:T(8,128)S(1)} %project.6.refs_2_, bf16[2,2,256,128]{3,2,1,0:T(8,128)(2,1)S(1)} %collective-permute-done.18.refs_3_, ...), custom_call_target="tpu_custom_call" | custom-call | tf_op jit(solution)/shard_map/project/pallas_call | solution.py:176
  99.1 3.3 %collective-permute-start.20 = (bf16[256,512]{1,0:T(8,128)(2,1)S(1)}, bf16[256,512]{1,0:T(8,128)(2,1)S(1)}, u32[]{:S(2)}, u32[]{:S(2)}) collective-permute-start(bf16[256,512]{1,0:T(8,128)(2,1)S(1)} %get-tuple-element.35), channel_id=1, source_target_pairs={{0,0},{1,16},{2,4},{3,20},{4,8},{5,24},{6,12},{7,28},{8,1},{9,17},... | collective-permute-start | bytes 786440 | tf_op jit(solution)/shard_map/ppermute | solution.py:266
  102.7 11.8 %collective-permute-done.20 = bf16[256,512]{1,0:T(8,128)(2,1)S(1)} collective-permute-done((bf16[256,512]{1,0:T(8,128)(2,1)S(1)}, bf16[256,512]{1,0:T(8,128)(2,1)S(1)}, u32[]{:S(2)}, u32[]{:S(2)}) %collective-permute-start.20) | collective-permute-done | bytes 262176 | tf_op jit(solution)/shard_map/ppermute | solution.py:266
  114.5 2.0 %collective-permute-done.21 = bf16[256,512]{1,0:T(8,128)(2,1)S(1)} collective-permute-done((bf16[256,512]{1,0:T(8,128)(2,1)S(1)}, bf16[256,512]{1,0:T(8,128)(2,1)S(1)}, u32[]{:S(2)}, u32[]{:S(2)}) %collective-permute-start.21) | collective-permute-done | bytes 262176 | tf_op jit(solution)/shard_map/ppermute | solution.py:266
  (53 shorter events, 16.1 us)
Async XLA Ops:
  2.8 43.0 %copy-start.8 = (bf16[256,512]{1,0:T(8,128)(2,1)S(1)}, bf16[256,512]{1,0:T(8,128)(2,1)}, u32[]{:S(2)}) copy-start(bf16[256,512]{1,0:T(8,128)(2,1)} %constant.51.clone.refs_4_) | copy-start | bytes 786436
  2.8 43.0 %all-to-all-start = ((bf16[8,3,256,128]{3,2,1,0:T(8,128)(2,1)}), bf16[8,3,256,128]{3,2,1,0:T(8,128)(2,1)S(1)}, u32[]{:S(2)}, u32[]{:S(2)}) async-start(bf16[8,3,256,128]{3,2,1,0:T(8,128)(2,1)} %pack.1), calls=%async_computation | async-start | bytes 3145728 | tf_op jit(solution)/shard_map/all_to_all | solution.py:226
  8.7 24.8 %collective-permute-start.1 = (bf16[8,128,512]{2,1,0:T(8,128)(2,1)S(1)}, bf16[8,128,512]{2,1,0:T(8,128)(2,1)}, u32[]{:S(2)}, u32[]{:S(2)}) collective-permute-start(bf16[8,128,512]{2,1,0:T(8,128)(2,1)S(1)} %bitcast.18), channel_id=1, source_target_pairs={{0,2},{1,3},{2,0},{3,1},{4,6},{5,7},{6,4},{7,5},{8,10},{9,11},{10,... | collective-permute-start | bytes 3145736 | tf_op jit(solution)/shard_map/ppermute | solution.py:222
  9.3 24.3 %collective-permute-start = (bf16[8,128,512]{2,1,0:T(8,128)(2,1)S(1)}, bf16[8,128,512]{2,1,0:T(8,128)(2,1)}, u32[]{:S(2)}, u32[]{:S(2)}) collective-permute-start(bf16[8,128,512]{2,1,0:T(8,128)(2,1)S(1)} %bitcast.19), channel_id=1, source_target_pairs={{0,1},{1,0},{2,3},{3,2},{4,5},{5,4},{6,7},{7,6},{8,9},{9,8},{10,11... | collective-permute-start | bytes 3145736 | tf_op jit(solution)/shard_map/ppermute | solution.py:219
  33.5 3.0 %collective-permute-start.2 = (bf16[8,128,512]{2,1,0:T(8,128)(2,1)}, bf16[8,128,512]{2,1,0:T(8,128)(2,1)}, u32[]{:S(2)}, u32[]{:S(2)}) collective-permute-start(bf16[8,128,512]{2,1,0:T(8,128)(2,1)} %collective-permute-done.1.refs_6_.refs_12_.refs_18_.refs_7_.refs_13_), channel_id=1, source_target_pairs={{0,1},{1,0},{2,3},{3,2},{4,5},{5,4},{6,7},{7,6},{8,9},{9,8},{10,11... | collective-permute-start | bytes 3145736 | tf_op jit(solution)/shard_map/ppermute | solution.py:223
  49.4 1.9 %collective-permute-start.3 = (bf16[2,256,128]{2,1,0:T(8,128)(2,1)S(1)}, bf16[2,256,128]{2,1,0:T(8,128)(2,1)S(1)}, u32[]{:S(2)}, u32[]{:S(2)}) collective-permute-start(bf16[2,256,128]{2,1,0:T(8,128)(2,1)S(1)} %get-tuple-element.23), channel_id=1, source_target_pairs={{0,1},{1,0},{2,3},{3,2},{4,5},{5,4},{6,7},{7,6},{8,9},{9,8},{10,11... | collective-permute-start | bytes 393224 | tf_op jit(solution)/shard_map/ppermute | solution.py:231
  49.4 6.4 %collective-permute-start.8 = (bf16[2,256,128]{2,1,0:T(8,128)(2,1)S(1)}, bf16[2,256,128]{2,1,0:T(8,128)(2,1)S(1)}, u32[]{:S(2)}, u32[]{:S(2)}) collective-permute-start(bf16[2,256,128]{2,1,0:T(8,128)(2,1)S(1)} %get-tuple-element.24), channel_id=1, source_target_pairs={{0,2},{1,3},{2,0},{3,1},{4,6},{5,7},{6,4},{7,5},{8,10},{9,11},{10,... | collective-permute-start | bytes 393224 | tf_op jit(solution)/shard_map/ppermute | solution.py:231
  50.0 7.7 %collective-permute-start.9 = (bf16[2,256,128]{2,1,0:T(8,128)(2,1)S(1)}, bf16[2,256,128]{2,1,0:T(8,128)(2,1)S(1)}, u32[]{:S(2)}, u32[]{:S(2)}) collective-permute-start(bf16[2,256,128]{2,1,0:T(8,128)(2,1)S(1)} %get-tuple-element.25), channel_id=1, source_target_pairs={{0,3},{1,2},{2,1},{3,0},{4,7},{5,6},{6,5},{7,4},{8,11},{9,10},{10,... | collective-permute-start | bytes 393224 | tf_op jit(solution)/shard_map/ppermute | solution.py:231
  51.3 8.6 %collective-permute-start.4 = (bf16[2,2,256,128]{3,2,1,0:T(8,128)(2,1)S(1)}, bf16[2,2,256,128]{3,2,1,0:T(8,128)(2,1)S(1)}, u32[]{:S(2)}, u32[]{:S(2)}) collective-permute-start(bf16[2,2,256,128]{3,2,1,0:T(8,128)(2,1)S(1)} %pad_maximum_fusion.refs_2_), channel_id=1, source_target_pairs={{8,16},{16,24},{24,28},{28,20},{20,12},{12,4},{4,0},{0,8},{9,17},{... | collective-permute-start | bytes 786440 | tf_op jit(solution)/shard_map/ppermute | solution.py:252
  51.4 8.8 %collective-permute-start.6 = (bf16[2,2,256,128]{3,2,1,0:T(8,128)(2,1)S(1)}, bf16[2,2,256,128]{3,2,1,0:T(8,128)(2,1)S(1)}, u32[]{:S(2)}, u32[]{:S(2)}) collective-permute-start(bf16[2,2,256,128]{3,2,1,0:T(8,128)(2,1)S(1)} %pad_maximum_fusion.refs_2_), channel_id=1, source_target_pairs={{8,0},{16,8},{24,16},{28,24},{20,28},{12,20},{4,12},{0,4},{9,1},{1... | collective-permute-start | bytes 786440 | tf_op jit(solution)/shard_map/ppermute | solution.py:252
  57.8 9.1 %collective-permute-start.11 = (bf16[2,2,256,128]{3,2,1,0:T(8,128)(2,1)S(1)}, bf16[2,2,256,128]{3,2,1,0:T(8,128)(2,1)S(1)}, u32[]{:S(2)}, u32[]{:S(2)}) collective-permute-start(bf16[2,2,256,128]{3,2,1,0:T(8,128)(2,1)S(1)} %pad_maximum_fusion.1.refs_3_), channel_id=1, source_target_pairs={{8,0},{16,8},{24,16},{28,24},{20,28},{12,20},{4,12},{0,4},{9,1},{1... | collective-permute-start | bytes 786440 | tf_op jit(solution)/shard_map/ppermute | solution.py:252
  59.2 9.1 %collective-permute-start.10 = (bf16[2,2,256,128]{3,2,1,0:T(8,128)(2,1)S(1)}, bf16[2,2,256,128]{3,2,1,0:T(8,128)(2,1)S(1)}, u32[]{:S(2)}, u32[]{:S(2)}) collective-permute-start(bf16[2,2,256,128]{3,2,1,0:T(8,128)(2,1)S(1)} %pad_maximum_fusion.1.refs_3_), channel_id=1, source_target_pairs={{8,16},{16,24},{24,28},{28,20},{20,12},{12,4},{4,0},{0,8},{9,17},{... | collective-permute-start | bytes 786440 | tf_op jit(solution)/shard_map/ppermute | solution.py:252
  60.0 14.0 %collective-permute-start.5 = (bf16[2,2,256,128]{3,2,1,0:T(8,128)(2,1)S(1)}, bf16[2,2,256,128]{3,2,1,0:T(8,128)(2,1)S(1)}, u32[]{:S(2)}, u32[]{:S(2)}) collective-permute-start(bf16[2,2,256,128]{3,2,1,0:T(8,128)(2,1)S(1)} %collective-permute-done.4.refs_8_), channel_id=1, source_target_pairs={{8,16},{16,24},{24,28},{28,20},{20,12},{12,4},{4,0},{0,8},{9,17},{... | collective-permute-start | bytes 786440 | tf_op jit(solution)/shard_map/ppermute | solution.py:252
  60.2 13.7 %collective-permute-start.7 = (bf16[2,2,256,128]{3,2,1,0:T(8,128)(2,1)S(1)}, bf16[2,2,256,128]{3,2,1,0:T(8,128)(2,1)S(1)}, u32[]{:S(2)}, u32[]{:S(2)}) collective-permute-start(bf16[2,2,256,128]{3,2,1,0:T(8,128)(2,1)S(1)} %collective-permute-done.6.refs_14_), channel_id=1, source_target_pairs={{8,0},{16,8},{24,16},{28,24},{20,28},{12,20},{4,12},{0,4},{9,1},{1... | collective-permute-start | bytes 786440 | tf_op jit(solution)/shard_map/ppermute | solution.py:252
  66.9 11.2 %collective-permute-start.15 = (bf16[2,2,256,128]{3,2,1,0:T(8,128)(2,1)S(1)}, bf16[2,2,256,128]{3,2,1,0:T(8,128)(2,1)S(1)}, u32[]{:S(2)}, u32[]{:S(2)}) collective-permute-start(bf16[2,2,256,128]{3,2,1,0:T(8,128)(2,1)S(1)} %collective-permute-done.11.refs_15_), channel_id=1, source_target_pairs={{8,0},{16,8},{24,16},{28,24},{20,28},{12,20},{4,12},{0,4},{9,1},{1... | collective-permute-start | bytes 786440 | tf_op jit(solution)/shard_map/ppermute | solution.py:252
  68.4 11.2 %collective-permute-start.14 = (bf16[2,2,256,128]{3,2,1,0:T(8,128)(2,1)S(1)}, bf16[2,2,256,128]{3,2,1,0:T(8,128)(2,1)S(1)}, u32[]{:S(2)}, u32[]{:S(2)}) collective-permute-start(bf16[2,2,256,128]{3,2,1,0:T(8,128)(2,1)S(1)} %collective-permute-done.10.refs_9_), channel_id=1, source_target_pairs={{8,16},{16,24},{24,28},{28,20},{20,12},{12,4},{4,0},{0,8},{9,17},{... | collective-permute-start | bytes 786440 | tf_op jit(solution)/shard_map/ppermute | solution.py:252
  74.0 11.2 %collective-permute-start.12 = (bf16[2,2,256,128]{3,2,1,0:T(8,128)(2,1)S(1)}, bf16[2,2,256,128]{3,2,1,0:T(8,128)(2,1)S(1)}, u32[]{:S(2)}, u32[]{:S(2)}) collective-permute-start(bf16[2,2,256,128]{3,2,1,0:T(8,128)(2,1)S(1)} %collective-permute-done.5.refs_3_), channel_id=1, source_target_pairs={{8,16},{16,24},{24,28},{28,20},{20,12},{12,4},{4,0},{0,8},{9,17},{... | collective-permute-start | bytes 786440 | tf_op jit(solution)/shard_map/ppermute | solution.py:252
  74.6 10.6 %collective-permute-start.13 = (bf16[2,2,256,128]{3,2,1,0:T(8,128)(2,1)S(1)}, bf16[2,2,256,128]{3,2,1,0:T(8,128)(2,1)S(1)}, u32[]{:S(2)}, u32[]{:S(2)}) collective-permute-start(bf16[2,2,256,128]{3,2,1,0:T(8,128)(2,1)S(1)} %collective-permute-done.7.refs_9_), channel_id=1, source_target_pairs={{8,0},{16,8},{24,16},{28,24},{20,28},{12,20},{4,12},{0,4},{9,1},{1... | collective-permute-start | bytes 786440 | tf_op jit(solution)/shard_map/ppermute | solution.py:252
  78.1 10.9 %collective-permute-start.17 = (bf16[2,2,256,128]{3,2,1,0:T(8,128)(2,1)S(1)}, bf16[2,2,256,128]{3,2,1,0:T(8,128)(2,1)S(1)}, u32[]{:S(2)}, u32[]{:S(2)}) collective-permute-start(bf16[2,2,256,128]{3,2,1,0:T(8,128)(2,1)S(1)} %collective-permute-done.15.refs_10_), channel_id=1, source_target_pairs={{8,0},{16,8},{24,16},{28,24},{20,28},{12,20},{4,12},{0,4},{9,1},{1... | collective-permute-start | bytes 786440 | tf_op jit(solution)/shard_map/ppermute | solution.py:252
  79.6 11.2 %collective-permute-start.16 = (bf16[2,2,256,128]{3,2,1,0:T(8,128)(2,1)S(1)}, bf16[2,2,256,128]{3,2,1,0:T(8,128)(2,1)S(1)}, u32[]{:S(2)}, u32[]{:S(2)}) collective-permute-start(bf16[2,2,256,128]{3,2,1,0:T(8,128)(2,1)S(1)} %collective-permute-done.14.refs_4_), channel_id=1, source_target_pairs={{8,16},{16,24},{24,28},{28,20},{20,12},{12,4},{4,0},{0,8},{9,17},{... | collective-permute-start | bytes 786440 | tf_op jit(solution)/shard_map/ppermute | solution.py:252
  85.2 10.6 %collective-permute-start.18 = (bf16[2,2,256,128]{3,2,1,0:T(8,128)(2,1)S(1)}, bf16[2,2,256,128]{3,2,1,0:T(8,128)(2,1)S(1)}, u32[]{:S(2)}, u32[]{:S(2)}) collective-permute-start(bf16[2,2,256,128]{3,2,1,0:T(8,128)(2,1)S(1)} %collective-permute-done.12.refs_3_), channel_id=1, source_target_pairs={{8,16},{16,24},{24,28},{28,20},{20,12},{12,4},{4,0},{0,8},{9,17},{... | collective-permute-start | bytes 786440 | tf_op jit(solution)/shard_map/ppermute | solution.py:252
  89.1 7.9 %collective-permute-start.19 = (bf16[2,2,256,128]{3,2,1,0:T(8,128)(2,1)S(1)}, bf16[2,2,256,128]{3,2,1,0:T(8,128)(2,1)S(1)}, u32[]{:S(2)}, u32[]{:S(2)}) collective-permute-start(bf16[2,2,256,128]{3,2,1,0:T(8,128)(2,1)S(1)} %collective-permute-done.17.refs_10_), channel_id=1, source_target_pairs={{8,0},{16,8},{24,16},{28,24},{20,28},{12,20},{4,12},{0,4},{9,1},{1... | collective-permute-start | bytes 786440 | tf_op jit(solution)/shard_map/ppermute | solution.py:252
  99.1 15.4 %collective-permute-start.20 = (bf16[256,512]{1,0:T(8,128)(2,1)S(1)}, bf16[256,512]{1,0:T(8,128)(2,1)S(1)}, u32[]{:S(2)}, u32[]{:S(2)}) collective-permute-start(bf16[256,512]{1,0:T(8,128)(2,1)S(1)} %get-tuple-element.35), channel_id=1, source_target_pairs={{0,0},{1,16},{2,4},{3,20},{4,8},{5,24},{6,12},{7,28},{8,1},{9,17},... | collective-permute-start | bytes 786440 | tf_op jit(solution)/shard_map/ppermute | solution.py:266
  102.4 14.1 %collective-permute-start.21 = (bf16[256,512]{1,0:T(8,128)(2,1)S(1)}, bf16[256,512]{1,0:T(8,128)(2,1)S(1)}, u32[]{:S(2)}, u32[]{:S(2)}) collective-permute-start(bf16[256,512]{1,0:T(8,128)(2,1)S(1)} %get-tuple-element.36), channel_id=1, source_target_pairs={{0,8},{1,24},{2,12},{3,28},{4,0},{5,16},{6,4},{7,20},{8,9},{9,25},... | collective-permute-start | bytes 786440 | tf_op jit(solution)/shard_map/ppermute | solution.py:266
  (9 other events, 173.1 us)
